TPU v7x, 1024 devices: a whole 8x8x8 slice. The times are simulated.
1024 devices in a mesh: dp: 16 (over y, x_hi), exp: 2 (over core), etp: 32 (over z, x_lo).
Axes of the slice: x: 8 (x_hi: 2, x_lo: 4; x = x_hi * 4 + x_lo), y: 8, z: 8, core: 2. Of those that a mesh axis runs over, the one named last changes fastest.
Arguments:
- tokens: bfloat16 [4096, 4096], P('etp', 'dp'), may hold values from -6 to 6
- routes: int32 [4096, 2], P('etp'), may hold values from 0 to 63, all different within a row; in each aligned block of 128 rows (0 to 127, 128 to 255, ...) at most 8 rows name the same one
- route_weights: float32 [4096, 2], P('etp'), may hold values from 0.2 to 1
- gate_weight: bfloat16 [64, 4096, 1536], P('etp', 'dp', 'exp'), may hold values from -0.09375 to 0.09375
- up_weight: bfloat16 [64, 4096, 1536], P('etp', 'dp', 'exp'), may hold values from -0.09375 to 0.09375
- down_weight: bfloat16 [64, 1536, 4096], P('etp', 'exp', 'dp'), may hold values from -0.15625 to 0.15625
- cotangent: bfloat16 [4096, 4096], P('etp', 'dp'), may hold values from -6 to 6
Outputs:
- mixed: bfloat16 [4096, 4096], P('etp', ('dp', 'exp'))
- d_tokens: bfloat16 [4096, 4096], P('etp', ('dp', 'exp'))
- d_down: bfloat16 [64, 1536, 4096], P('etp', 'exp', 'dp')
Inputs may be any that keep to these rules, and one draw needn't show every extreme that they name: `routes`: each row names 2 different experts. Within the rows of one group of 128 consecutive tokens no expert is named by more than 8 rows; in every draw some group names some expert exactly 8 times.
All inputs are finite; a program needn't handle non-finite values.
Results may differ from a plain program's by a relative error of at most 0.012.
Values may be sent and summed in bfloat16 or wider, within the bound.
No kernel may reach another device: no remote copies, remote signals or barrier semaphores. Data moves between devices by JAX's collectives and lax.ppermute only.
A program may use at most 32 MiB of HBM per device.

v0:
```python
import jax
import jax.numpy as jnp
from jax import lax
from jax.sharding import PartitionSpec as P


def by_expert(rows, groups, local_experts, capacity):
    width = rows.shape[-1]
    shaped = rows.reshape(groups, local_experts, capacity, width)
    return jnp.swapaxes(shaped, 0, 1).reshape(local_experts, groups * capacity, width)


def by_owner(rows, groups, local_experts, capacity):
    width = rows.shape[-1]
    shaped = rows.reshape(local_experts, groups, capacity, width)
    return jnp.swapaxes(shaped, 0, 1).reshape(groups * local_experts * capacity, width)


def shards(tokens, routes, route_weights, gate_weight, up_weight, down_weight, cotangent):
    local_experts = gate_weight.shape[0]
    groups = lax.axis_size("etp")
    num_experts = groups * local_experts
    tok_rows = tokens.shape[0]
    top_count = routes.shape[1]
    pairs = tok_rows * top_count
    capacity = 2 * pairs // num_experts
    slots_all = num_experts * capacity
    routes_flat = routes.reshape(pairs)
    expert_hot = (routes_flat[:, None] == jnp.arange(num_experts, dtype=jnp.int32)[None, :]).astype(
        jnp.int32
    )
    position = jnp.sum((jnp.cumsum(expert_hot, axis=0) - 1) * expert_hot, axis=1)
    slot_index = routes_flat * capacity + position
    slot_range = jnp.arange(slots_all, dtype=jnp.int32)
    placing = (slot_range[:, None] == slot_index[None, :]).astype(jnp.bfloat16)
    token_rows = jnp.repeat(tokens, top_count, axis=0)
    grad_rows = (
        route_weights.reshape(pairs, 1)
        * jnp.repeat(cotangent, top_count, axis=0).astype(jnp.float32)
    ).astype(jnp.bfloat16)
    send_tokens = jnp.dot(placing, token_rows, preferred_element_type=jnp.float32).astype(
        jnp.bfloat16
    )
    send_grads = jnp.dot(placing, grad_rows, preferred_element_type=jnp.float32).astype(
        jnp.bfloat16
    )
    recv_tokens, recv_grads = (
        lax.all_to_all(send_tokens, "etp", split_axis=0, concat_axis=0, tiled=True),
        lax.all_to_all(send_grads, "etp", split_axis=0, concat_axis=0, tiled=True),
    )
    expert_in = by_expert(recv_tokens, groups, local_experts, capacity)
    expert_grad = by_expert(recv_grads, groups, local_experts, capacity)
    gate_term = jnp.einsum(
        "erd,edf->erf", expert_in, gate_weight, preferred_element_type=jnp.float32
    )
    up_term = jnp.einsum("erd,edf->erf", expert_in, up_weight, preferred_element_type=jnp.float32)
    back_term = jnp.einsum(
        "erd,efd->erf", expert_grad, down_weight, preferred_element_type=jnp.float32
    )
    gate, up_proj, d_hidden = (
        lax.psum_scatter(gate_term, "dp", scatter_dimension=1, tiled=True),
        lax.psum_scatter(up_term, "dp", scatter_dimension=1, tiled=True),
        lax.psum_scatter(back_term, "dp", scatter_dimension=1, tiled=True),
    )
    sigmoid_gate = jax.nn.sigmoid(gate)
    silu_gate = gate * sigmoid_gate
    hidden = (silu_gate * up_proj).astype(jnp.bfloat16)
    d_up = (d_hidden * silu_gate).astype(jnp.bfloat16)
    d_gate = (d_hidden * up_proj * sigmoid_gate * (1.0 + gate * (1.0 - sigmoid_gate))).astype(
        jnp.bfloat16
    )
    hidden, d_gate, d_up = (hidden, d_gate, d_up)
    all_hidden, all_dgate, all_dup = (
        lax.all_gather(hidden, "dp", axis=1, tiled=True),
        lax.all_gather(d_gate, "dp", axis=1, tiled=True),
        lax.all_gather(d_up, "dp", axis=1, tiled=True),
    )
    part_out = jnp.einsum(
        "erf,efd->erd", all_hidden, down_weight, preferred_element_type=jnp.float32
    ).astype(jnp.bfloat16)
    grad_terms = jnp.einsum(
        "erf,edf->erd", all_dgate, gate_weight, preferred_element_type=jnp.float32
    )
    grad_terms = grad_terms + jnp.einsum(
        "erf,edf->erd", all_dup, up_weight, preferred_element_type=jnp.float32
    )
    part_grad = grad_terms.astype(jnp.bfloat16)
    d_down = jnp.einsum(
        "erf,erd->efd", all_hidden, expert_grad, preferred_element_type=jnp.float32
    ).astype(jnp.bfloat16)
    summed_out, summed_grad = (
        lax.psum_scatter(
            part_out.astype(jnp.float32).astype(jnp.bfloat16),
            "exp",
            scatter_dimension=2,
            tiled=True,
        ).astype(jnp.float32),
        lax.psum_scatter(
            part_grad.astype(jnp.float32).astype(jnp.bfloat16),
            "exp",
            scatter_dimension=2,
            tiled=True,
        ).astype(jnp.float32),
    )
    back_out, back_grad = (
        lax.all_to_all(
            by_owner(summed_out, groups, local_experts, capacity),
            "etp",
            split_axis=0,
            concat_axis=0,
            tiled=True,
        ),
        lax.all_to_all(
            by_owner(summed_grad, groups, local_experts, capacity),
            "etp",
            split_axis=0,
            concat_axis=0,
            tiled=True,
        ),
    )
    width = back_out.shape[1]
    picked_out = jnp.take(back_out, slot_index, axis=0).reshape(tok_rows, top_count, width)
    picked_grad = jnp.take(back_grad, slot_index, axis=0).reshape(tok_rows, top_count, width)
    out_total = jnp.sum(picked_out * route_weights[:, :, None], axis=1)
    grad_total = jnp.sum(picked_grad, axis=1)
    mixed = out_total.astype(jnp.bfloat16)
    d_tokens = grad_total.astype(jnp.bfloat16)
    return (mixed, d_tokens, d_down)


def solution(mesh):
    in_specs = (
        P("etp", "dp"),
        P("etp", None),
        P("etp", None),
        P("etp", "dp", "exp"),
        P("etp", "dp", "exp"),
        P("etp", "exp", "dp"),
        P("etp", "dp"),
    )
    out_specs = (P("etp", ("dp", "exp")), P("etp", ("dp", "exp")), P("etp", "exp", "dp"))
    return jax.shard_map(shards, mesh=mesh, in_specs=in_specs, out_specs=out_specs, check_vma=False)
```

profile of v0, /device:TPU:1, one launch (start us, length us, event | category | flops | bytes accessed | tf_op | source)
XLA Modules:
  0.0 989.3 jit_solution(9003044819352194938)
XLA Ops:
  7.2 0.9 copy.29
  8.4 0.6 reduce-window.6
  9.4 0.8 copy.34
  10.3 0.9 broadcast_in_dim.20
  11.7 31.4 %all_to_all.54 = bf16[32,16,256]{2,1,0:T(8,128)(2,1)S(1)} all-to-all(bf16[32,16,256]{2,1,0:T(8,128)(2,1)S(1)} %bitcast.90), channel_id=1, replica_groups=mesh['dp'=16,'exp'=2,'etp'=32] {'etp'}, dimensions={0} | all-to-all | bytes 524288 | tf_op jit(solution)/shard_map/all_to_all | solution.py:49
  43.1 1.6 fusion.2
  45.1 16.2 %all_to_all.55 = bf16[32,16,256]{2,1,0:T(8,128)(2,1)S(1)} all-to-all(bf16[32,16,256]{2,1,0:T(8,128)(2,1)S(1)} %bitcast.91), channel_id=1, replica_groups=mesh['dp'=16,'exp'=2,'etp'=32] {'etp'}, dimensions={0} | all-to-all | bytes 524288 | tf_op jit(solution)/shard_map/all_to_all | solution.py:48
  61.4 1.5 fusion.6
  63.0 1.5 fusion.4
  64.6 200.2 %reduce-scatter.14.cloned.1.call-done = f32[2,16,768]{2,1,0:T(8,128)} async-done(((f32[2,256,768]{2,1,0:T(8,128)}), f32[2,16,768]{2,1,0:T(8,128)}) %reduce-scatter.14.cloned.1.call-update) | async-done | bytes 98320 | tf_op jit(solution)/shard_map/reduce_scatter | solution.py:63
  264.7 232.1 %reduce-scatter.10.cloned.1.call-done = f32[2,16,768]{2,1,0:T(8,128)} async-done(((f32[2,256,768]{2,1,0:T(8,128)}), f32[2,16,768]{2,1,0:T(8,128)}) %reduce-scatter.10.cloned.1.call-update) | async-done | bytes 98320 | tf_op jit(solution)/shard_map/reduce_scatter | solution.py:61
  496.8 231.7 %reduce-scatter.12.cloned.1.call-done = f32[2,16,768]{2,1,0:T(8,128)} async-done(((f32[2,256,768]{2,1,0:T(8,128)}), f32[2,16,768]{2,1,0:T(8,128)}) %reduce-scatter.12.cloned.1.call-update) | async-done | bytes 98320 | tf_op jit(solution)/shard_map/reduce_scatter | solution.py:62
  728.5 1.0 multiply_convert_fusion.2
  729.6 51.6 %all_gather.10 = bf16[2,256,768]{2,1,0:T(8,128)(2,1)S(1)} all-gather(bf16[2,16,768]{2,1,0:T(8,128)(2,1)S(1)} %get-tuple-element.7), channel_id=1, replica_groups=mesh['dp'=16,'exp'=2,'etp'=32] {'dp'}, dimensions={1}, use_global_device_ids=true | all-gather | bytes 835584 | tf_op jit(solution)/shard_map/all_gather | solution.py:75
  781.5 55.1 %all_gather.11 = bf16[2,256,768]{2,1,0:T(8,128)(2,1)S(1)} all-gather(bf16[2,16,768]{2,1,0:T(8,128)(2,1)S(1)} %get-tuple-element.6), channel_id=1, replica_groups=mesh['dp'=16,'exp'=2,'etp'=32] {'dp'}, dimensions={1}, use_global_device_ids=true | all-gather | bytes 835584 | tf_op jit(solution)/shard_map/all_gather | solution.py:76
  836.6 0.4 fusion
  837.2 0.7 copy.44
  838.0 60.0 %all_gather.9 = bf16[2,256,768]{2,1,0:T(8,128)(2,1)S(1)} all-gather(bf16[2,16,768]{2,1,0:T(8,128)(2,1)S(1)} %get-tuple-element.8), channel_id=1, replica_groups=mesh['dp'=16,'exp'=2,'etp'=32] {'dp'}, dimensions={1}, use_global_device_ids=true | all-gather | bytes 835584 | tf_op jit(solution)/shard_map/all_gather | solution.py:74
  898.6 0.7 copy.43
  899.4 0.9 reshape.131
  900.5 0.7 copy_bitcast_fusion
  901.2 27.2 %all-to-all-start.3 = ((f32[32,16,128]{2,1,0:T(8,128)}), f32[32,16,128]{2,1,0:T(8,128)S(1)}, u32[]{:S(2)}, u32[]{:S(2)}) async-start(f32[32,16,128]{2,1,0:T(8,128)} %copy_bitcast_fusion), calls=%async_computation.6 | async-start | bytes 524288 | tf_op jit(solution)/shard_map/all_to_all | solution.py:113
  928.4 30.6 %reduce-scatter.16.cloned.1.call-done = bf16[128,512]{1,0:T(8,128)(2,1)} async-done(((bf16[256,512]{1,0:T(8,128)(2,1)}), bf16[128,512]{1,0:T(8,128)(2,1)}) %reduce-scatter.16.cloned.1.call-update) | async-done | bytes 131088
  959.0 0.9 reshape.129
  960.1 0.7 copy_bitcast_fusion.1
  960.8 8.5 all-to-all-start.1
  969.3 1.3 convolution_convert_fusion
  970.7 0.7 gather_fusion.1
  971.4 8.9 all-to-all-done.1
  980.3 0.7 gather_fusion
  981.2 0.9 multiply_reduce_fusion
  982.0 0.8 reduce_sum.29
  (43 shorter events, 3.5 us)
Async XLA Ops:
  7.2 54.2 %copy-start = (bf16[2,256,768]{2,1,0:T(8,128)(2,1)S(1)}, bf16[2,256,768]{2,1,0:T(8,128)(2,1)}, u32[]{:S(2)}) copy-start(bf16[2,256,768]{2,1,0:T(8,128)(2,1)} %param.12) | copy-start | bytes 2359300
  7.2 35.9 %copy-start.1 = (bf16[2,768,256]{2,1,0:T(8,128)(2,1)S(1)}, bf16[2,768,256]{2,1,0:T(8,128)(2,1)}, u32[]{:S(2)}) copy-start(bf16[2,768,256]{2,1,0:T(8,128)(2,1)} %param.14) | copy-start | bytes 2359300
  7.2 257.5 %reduce-scatter.14.cloned.1.call-start = ((), (), s32[]{:S(2)}) async-start(), calls=%async_computation.11 | async-start | bytes 1671168 | tf_op jit(solution)/shard_map/reduce_scatter | solution.py:63
  43.1 1.6 copy-start.3
  44.7 452.1 %reduce-scatter.10.cloned.1.call-start = ((), (), s32[]{:S(2)}) async-start(), calls=%async_computation.9 | async-start | bytes 1671168 | tf_op jit(solution)/shard_map/reduce_scatter | solution.py:61
  61.4 1.6 copy-start.2
  62.9 665.6 %reduce-scatter.12.cloned.1.call-start = ((), (), s32[]{:S(2)}) async-start(), calls=%async_computation.10 | async-start | bytes 1671168 | tf_op jit(solution)/shard_map/reduce_scatter | solution.py:62
  64.5 834.8 %reduce-scatter.18.cloned.1.call-start = ((), (), s32[]{:S(2)}) async-start(), calls=%async_computation.13 | async-start | bytes 393216
  838.0 121.1 %reduce-scatter.16.cloned.1.call-start = ((), (), s32[]{:S(2)}) async-start(), calls=%async_computation.12 | async-start | bytes 393216
  901.2 59.6 %all-to-all-start.3 = ((f32[32,16,128]{2,1,0:T(8,128)}), f32[32,16,128]{2,1,0:T(8,128)S(1)}, u32[]{:S(2)}, u32[]{:S(2)}) async-start(f32[32,16,128]{2,1,0:T(8,128)} %copy_bitcast_fusion), calls=%async_computation.6 | async-start | bytes 524288 | tf_op jit(solution)/shard_map/all_to_all | solution.py:113
  960.8 19.5 %all-to-all-start.1 = ((f32[32,16,128]{2,1,0:T(8,128)}), f32[32,16,128]{2,1,0:T(8,128)S(1)}, u32[]{:S(2)}, u32[]{:S(2)}) async-start(f32[32,16,128]{2,1,0:T(8,128)} %copy_bitcast_fusion.1), calls=%async_computation.3 | async-start | bytes 524288 | tf_op jit(solution)/shard_map/all_to_all | solution.py:106
Sparse Core Ops, SparseCore 0:
  44.8 219.8 reduce-scatter.13
  271.3 225.5 reduce-scatter.9
  502.5 225.9 reduce-scatter.11
  838.1 56.2 reduce-scatter.17
  899.5 59.4 reduce-scatter.15
where the time goes:
time: 991 us; the launch traced here: 989 us
  waiting for transfers between devices  704 us (71%)
  blocking collectives  214 us (22%)
  starting transfers between devices  35.9 us (4%)
  between operations  14 us (1%)
    reduce_scatter x1, waiting for transfers between devices, shards(): lax.psum_scatter(gate_term, 'dp', scatter_dimension=1, tiled=True)  232 us
    reduce_scatter x1, waiting for transfers between devices, shards(): lax.psum_scatter(up_term, 'dp', scatter_dimension=1, tiled=True)  232 us
    reduce_scatter x1, waiting for transfers between devices, shards(): lax.psum_scatter(back_term, 'dp', scatter_dimension=1, tiled=True)  200 us
    all_gather x1, blocking collectives, shards(): lax.all_gather(hidden, 'dp', axis=1, tiled=True)  60 us
    all_gather x1, blocking collectives, shards(): lax.all_gather(d_up, 'dp', axis=1, tiled=True)  55.1 us
    all_gather x1, blocking collectives, shards(): lax.all_gather(d_gate, 'dp', axis=1, tiled=True)  51.6 us
    all_to_all x1, blocking collectives, shards(): lax.all_to_all(send_grads, 'etp', split_axis=0, concat_axis=0, tiled=True)  31.4 us
    unnamed x7, waiting for transfers between devices  30.7 us
  transfers between devices with their start and end apart: 7, of which 5 were waited for; matrix products, arithmetic and copies ran while one was open for 1% of the time, Pallas kernels for 0%

commit v1 on v0

v1 whole, which is shorter than its diff:
```python
import jax
import jax.numpy as jnp
from jax import lax
from jax.sharding import Mesh, PartitionSpec as P

BF = jnp.bfloat16
F32 = jnp.float32
ETP = ("z", "xl")
CAPACITY = 8


def exchange(rows, axis):
    return lax.all_to_all(rows, axis, split_axis=0, concat_axis=0, tiled=True)


def shards(tokens, routes, route_weights, gate_weight, up_weight, down_weight, cotangent):
    local_experts, depth, hidden_width = gate_weight.shape
    groups = lax.axis_size("z") * lax.axis_size("xl")
    dp_size = lax.axis_size("y") * lax.axis_size("xh")
    num_experts = groups * local_experts
    tok_rows, top_count = routes.shape
    pairs = tok_rows * top_count
    slots_all = num_experts * CAPACITY
    half = depth // 2

    routes_flat = routes.reshape(pairs)
    expert_hot = (
        routes_flat[:, None] == jnp.arange(num_experts, dtype=jnp.int32)[None, :]
    ).astype(jnp.int32)
    position = jnp.sum((jnp.cumsum(expert_hot, axis=0) - 1) * expert_hot, axis=1)
    slot_index = (routes_flat * CAPACITY + position).reshape(tok_rows, top_count)

    slot_range = jnp.arange(slots_all, dtype=jnp.int32)
    hits = [slot_range[:, None] == slot_index[None, :, k] for k in range(top_count)]
    placing = sum(hit.astype(BF) for hit in hits)
    slot_weight = sum(
        jnp.sum(jnp.where(hit, route_weights[None, :, k], 0.0), axis=1)
        for k, hit in enumerate(hits)
    )
    sources = jnp.concatenate([tokens, cotangent], axis=1)
    placed = jnp.dot(placing, sources, preferred_element_type=F32)
    send = jnp.concatenate(
        [placed[:, :depth], placed[:, depth:] * slot_weight[:, None]], axis=1
    ).astype(BF)
    arrived = exchange(send, ETP)
    arrived = arrived.reshape(groups, local_experts, CAPACITY, 2 * depth)
    arrived = jnp.swapaxes(arrived, 0, 1).reshape(local_experts, groups * CAPACITY, 2 * depth)
    expert_in, expert_grad = arrived[..., :depth], arrived[..., depth:]

    terms = jnp.concatenate(
        [
            jnp.einsum("erd,edf->erf", expert_in, gate_weight, preferred_element_type=F32).astype(BF),
            jnp.einsum("erd,edf->erf", expert_in, up_weight, preferred_element_type=F32).astype(BF),
            jnp.einsum("erd,efd->erf", expert_grad, down_weight, preferred_element_type=F32).astype(BF),
        ],
        axis=2,
    )
    rows_all = local_experts * groups * CAPACITY
    terms = exchange(terms.reshape(rows_all, 3 * hidden_width), ("y", "xh"))
    sums = jnp.sum(
        terms.reshape(dp_size, rows_all // dp_size, 3 * hidden_width).astype(F32), axis=0
    )
    gate, up_proj, d_hidden = jnp.split(sums, 3, axis=1)
    sigmoid_gate = jax.nn.sigmoid(gate)
    silu_gate = gate * sigmoid_gate
    hidden = (silu_gate * up_proj).astype(BF)
    d_up = (d_hidden * silu_gate).astype(BF)
    d_gate = (d_hidden * up_proj * sigmoid_gate * (1.0 + gate * (1.0 - sigmoid_gate))).astype(BF)
    acts = jnp.concatenate([hidden, d_gate, d_up], axis=1)
    acts = lax.all_gather(acts, "xh", axis=0, tiled=True)
    acts = lax.all_gather(acts, "y", axis=0, tiled=True)
    acts = acts.reshape(local_experts, groups * CAPACITY, 3 * hidden_width)
    all_hidden, all_dgate, all_dup = jnp.split(acts, 3, axis=2)

    part_out = jnp.einsum(
        "erf,efd->erd", all_hidden, down_weight, preferred_element_type=F32
    ).astype(BF)
    part_grad = (
        jnp.einsum("erf,edf->erd", all_dgate, gate_weight, preferred_element_type=F32)
        + jnp.einsum("erf,edf->erd", all_dup, up_weight, preferred_element_type=F32)
    ).astype(BF)
    d_down = jnp.einsum(
        "erf,erd->efd", all_hidden, expert_grad, preferred_element_type=F32
    ).astype(BF)

    parts = jnp.stack(
        [
            jnp.concatenate([part_out[..., :half], part_grad[..., :half]], axis=2),
            jnp.concatenate([part_out[..., half:], part_grad[..., half:]], axis=2),
        ]
    )
    parts = lax.all_to_all(parts, "exp", split_axis=0, concat_axis=0, tiled=True)
    slot_sums = (parts[0].astype(F32) + parts[1].astype(F32)).astype(BF)
    slot_sums = slot_sums.reshape(local_experts, groups, CAPACITY, depth)
    slot_sums = jnp.swapaxes(slot_sums, 0, 1).reshape(slots_all, depth)
    back = exchange(slot_sums, ETP)

    picked = [
        jnp.dot(
            (slot_index[:, k, None] == slot_range[None, :]).astype(BF),
            back,
            preferred_element_type=F32,
        )
        for k in range(top_count)
    ]
    mixed = sum(p[:, :half] * route_weights[:, k, None] for k, p in enumerate(picked)).astype(BF)
    d_tokens = sum(p[:, half:] for p in picked).astype(BF)
    return mixed, d_tokens, d_down


def solution(mesh):
    fine = Mesh(mesh.devices.reshape(8, 2, 2, 8, 4), ("y", "xh", "exp", "z", "xl"))
    dp = ("y", "xh")
    in_specs = (
        P(ETP, dp),
        P(ETP, None),
        P(ETP, None),
        P(ETP, dp, "exp"),
        P(ETP, dp, "exp"),
        P(ETP, "exp", dp),
        P(ETP, dp),
    )
    out_specs = (P(ETP, dp + ("exp",)), P(ETP, dp + ("exp",)), P(ETP, "exp", dp))
    return jax.shard_map(shards, mesh=fine, in_specs=in_specs, out_specs=out_specs, check_vma=False)
```

time: 991 us -> 220 us (0.22)
  waiting for transfers between devices: 704 us -> 59.7 us
  blocking collectives: 214 us -> 118 us
  starting transfers between devices: 35.9 us -> 11 us
    reduce_scatter x3 -> x0, waiting for transfers between devices: 664 us -> none  [the longest x1 232 us: shards(): lax.psum_scatter(gate_term, 'dp', scatter_dimension=1, tiled=True)]
    all_gather x3 -> x1, blocking collectives: 167 us -> 13.8 us  [shards(): acts = lax.all_gather(acts, 'xh', axis=0, tiled=True)]
    all_to_all x2 -> x3, blocking collectives: 47.6 us -> 104 us  [the longest x2 96.7 us: exchange(): return lax.all_to_all(rows, axis, split_axis=0, concat_axis=0, tiled=True)]
    all_gather x0 -> x1, waiting for transfers between devices: none -> 50.6 us  [shards(): acts = lax.all_gather(acts, 'y', axis=0, tiled=True)]
    unnamed x7 -> x1, waiting for transfers between devices: 30.7 us -> 0.02 us
    all_to_all x2 -> x1, starting transfers between devices: 35.7 us -> 10.9 us  [exchange(): return lax.all_to_all(rows, axis, split_axis=0, concat_axis=0, tiled=True)]
  transfers between devices with their start and end apart: 7 -> 2, of which waited for: 5 -> 2; matrix products, arithmetic and copies ran while one was open for 1% -> 1% of each run, Pallas kernels for 0% -> 0%
where the time goes in v1:
time: 220 us
  blocking collectives  118 us (54%)
  waiting for transfers between devices  59.7 us (27%)
  between operations  14.3 us (6%)
  starting transfers between devices  11 us (5%)
  matrix products  9.85 us (4%)
  local copies, waits for them, and re-layouts  3.55 us (2%)
  other arithmetic  3.32 us (2%)
    all_to_all x2, blocking collectives, exchange(): return lax.all_to_all(rows, axis, split_axis=0, concat_axis=0, tiled=True)  96.7 us
    all_gather x1, waiting for transfers between devices, shards(): acts = lax.all_gather(acts, 'y', axis=0, tiled=True)  50.6 us
    all_gather x1, blocking collectives, shards(): acts = lax.all_gather(acts, 'xh', axis=0, tiled=True)  13.8 us
    all_to_all x1, starting transfers between devices, exchange(): return lax.all_to_all(rows, axis, split_axis=0, concat_axis=0, tiled=True)  10.9 us
    all_to_all x1, waiting for transfers between devices, exchange(): return lax.all_to_all(rows, axis, split_axis=0, concat_axis=0, tiled=True)  9.15 us
    all_to_all x1, blocking collectives, shards(): lax.all_to_all(parts, 'exp', split_axis=0, concat_axis=0, tiled=True)  7.59 us
  transfers between devices with their start and end apart: 2, of which 2 were waited for; matrix products, arithmetic and copies ran while one was open for 1% of the time, Pallas kernels for 0%

profile of v1, /device:TPU:1, one launch (start us, length us, event | category | flops | bytes accessed | tf_op | source)
XLA Modules:
  0.0 219.7 jit_solution(7147181292319965104)
XLA Ops:
  7.2 0.9 copy.43
  8.1 0.1 eq.85
  8.2 0.1 eq.81
  8.4 0.8 slice_bitcast_fusion
  9.1 0.6 reduce-window.6
  9.7 0.2 slice_reduce_fusion
  10.1 0.1 reduce_sum.39
  10.3 0.7 multiply_add_fusion
  11.0 1.2 fusion.16
  12.2 0.2 select_reduce_fusion
  12.5 0.1 fusion.6
  12.7 35.1 %all_to_all.32 = bf16[32,16,512]{2,1,0:T(8,128)(2,1)S(1)} all-to-all(bf16[32,16,512]{2,1,0:T(8,128)(2,1)S(1)} %pad_maximum_fusion.1), channel_id=1, replica_groups=mesh['y'=8,'xh'=2,'exp'=2,'z'=8,'xl'=4] {'z','xl'}, dimensions={0} | all-to-all | bytes 1048576 | tf_op jit(solution)/shard_map/all_to_all | solution.py:13
  47.8 0.4 convolution_convert_fusion.2
  48.2 0.4 convolution_convert_fusion.1
  48.6 0.3 copy-done.2
  48.9 0.4 convolution_convert_fusion.3
  49.3 0.2 pad_maximum_fusion
  49.4 61.6 %all_to_all.33 = bf16[16,32,2304]{2,1,0:T(8,128)(2,1)S(1)} all-to-all(bf16[16,32,2304]{2,1,0:T(8,128)(2,1)S(1)} %bitcast.54), channel_id=1, replica_groups=mesh['y'=8,'xh'=2,'exp'=2,'z'=8,'xl'=4] {'y','xh'}, dimensions={0} | all-to-all | bytes 4718592 | tf_op jit(solution)/shard_map/all_to_all | solution.py:13
  111.0 0.3 convert_reduce_fusion
  111.4 13.8 %all_gather.6 = bf16[64,2304]{1,0:T(8,128)(2,1)} all-gather(bf16[32,2304]{1,0:T(8,128)(2,1)S(1)} %pad_maximum_fusion.3), channel_id=1, replica_groups=mesh['y'=8,'xh'=2,'exp'=2,'z'=8,'xl'=4] {'xh'}, dimensions={0}, use_global_device_ids=true | all-gather | bytes 442368 | tf_op jit(solution)/shard_map/all_gather | solution.py:70
  125.2 50.6 %all-gather.2.cloned.1.call-done = bf16[512,2304]{1,0:T(8,128)(2,1)} async-done(((bf16[64,2304]{1,0:T(8,128)(2,1)}), bf16[512,2304]{1,0:T(8,128)(2,1)}) %all-gather.2.cloned.1.call-update) | async-done | bytes 2359312 | tf_op jit(solution)/shard_map/all_gather | solution.py:71
  175.8 1.6 convolution_convert_fusion.4
  177.3 1.5 fusion.2
  178.9 1.5 fusion
  180.6 7.6 %all_to_all.34 = bf16[2,2,256,256]{2,3,1,0:T(8,128)(2,1)S(1)} all-to-all(bf16[2,2,256,256]{2,3,1,0:T(8,128)(2,1)S(1)} %pad_maximum_fusion.2), channel_id=1, replica_groups=mesh['y'=8,'xh'=2,'exp'=2,'z'=8,'xl'=4] {'exp'}, dimensions={0} | all-to-all | bytes 1048576 | tf_op jit(solution)/shard_map/all_to_all | solution.py:92
  188.4 0.7 copy_bitcast_fusion.1
  189.1 10.9 %all-to-all-start.3 = ((bf16[32,16,256]{2,1,0:T(8,128)(2,1)}), bf16[32,16,256]{2,1,0:T(8,128)(2,1)S(1)}, u32[]{:S(2)}, u32[]{:S(2)}) async-start(bf16[32,16,256]{2,1,0:T(8,128)(2,1)} %copy_bitcast_fusion.1), calls=%async_computation.3 | async-start | bytes 524288 | tf_op jit(solution)/shard_map/all_to_all | solution.py:13
  200.1 2.5 %convolution_convert_fusion = bf16[2,768,256]{2,1,0:T(8,128)(2,1)} fusion(bf16[2,256,2304]{2,1,0:T(8,128)(2,1)} %bitcast.60, bf16[2,256,512]{2,1,0:T(8,128)(2,1)S(1)} %copy_bitcast_fusion), kind=kOutput, calls=%fused_computation.2 | convolution fusion | flops 201719808 | bytes 1835008 | tf_op jit(solution)/shard_map/erf,erd->efd/dot_general | solution.py:82
  202.5 9.2 %all-to-all-done.3 = bf16[32,16,256]{2,1,0:T(8,128)(2,1)S(1)} async-done(((bf16[32,16,256]{2,1,0:T(8,128)(2,1)}), bf16[32,16,256]{2,1,0:T(8,128)(2,1)S(1)}, u32[]{:S(2)}, u32[]{:S(2)}) %all-to-all-start.3) | async-done | bytes 262176 | tf_op jit(solution)/shard_map/all_to_all | solution.py:13
  211.7 0.2 fusion.10
  211.9 0.2 fusion.9
  212.1 0.7 fusion.29
  (26 shorter events, 0.8 us)
Async XLA Ops:
  7.2 41.0 %copy-start = (bf16[2,768,256]{2,1,0:T(8,128)(2,1)S(1)}, bf16[2,768,256]{2,1,0:T(8,128)(2,1)}, u32[]{:S(2)}) copy-start(bf16[2,768,256]{2,1,0:T(8,128)(2,1)} %param.12) | copy-start | bytes 2359300
  7.2 168.6 %all-gather.2.cloned.1.call-start = ((), (), s32[]{:S(2)}) async-start(), calls=%async_computation.4 | async-start | bytes 2654208 | tf_op jit(solution)/shard_map/all_gather | solution.py:71
  12.2 35.6 %copy-start.1 = (bf16[2,256,768]{2,1,0:T(8,128)(2,1)S(1)}, bf16[2,256,768]{2,1,0:T(8,128)(2,1)}, u32[]{:S(2)}) copy-start(bf16[2,256,768]{2,1,0:T(8,128)(2,1)} %param.11) | copy-start | bytes 2359300
  47.8 1.1 copy-start.2
  189.1 22.6 %all-to-all-start.3 = ((bf16[32,16,256]{2,1,0:T(8,128)(2,1)}), bf16[32,16,256]{2,1,0:T(8,128)(2,1)S(1)}, u32[]{:S(2)}, u32[]{:S(2)}) async-start(bf16[32,16,256]{2,1,0:T(8,128)(2,1)} %copy_bitcast_fusion.1), calls=%async_computation.3 | async-start | bytes 524288 | tf_op jit(solution)/shard_map/all_to_all | solution.py:13
Sparse Core Ops, SparseCore 0:
  125.3 50.3 all-gather.1

commit v2 on v1

--- a/solution.py
+++ b/solution.py
@@ -13,15 +13,65 @@
     return lax.all_to_all(rows, axis, split_axis=0, concat_axis=0, tiled=True)
 
 
+def step(block, axis, shift):
+    size = lax.axis_size(axis)
+    return lax.ppermute(block, axis, [(i, (i + shift) % size) for i in range(size)])
+
+
+def ring_sum(terms, rows):
+    size = lax.axis_size("y")
+    mine = lax.axis_index("y")
+    far, half = size // 2, rows // 2
+
+    def own(offset, start, count):
+        chunk = lax.rem(mine + offset + size, size)
+        return lax.dynamic_slice_in_dim(terms, chunk * rows + start, count, 0)
+
+    up = step(own(far, 0, half).astype(BF), "y", 1)
+    down = step(own(-far, half, half).astype(BF), "y", -1)
+    up = jnp.concatenate(
+        [own(far - 1, 0, half) + up.astype(F32), own(far - 1, half, half)], axis=0
+    ).astype(BF)
+    down = jnp.concatenate(
+        [own(1 - far, 0, half), own(1 - far, half, half) + down.astype(F32)], axis=0
+    ).astype(BF)
+    for distance in range(far - 2, -1, -1):
+        up, down = step(up, "y", 1), step(down, "y", -1)
+        if distance > 0:
+            up = (own(distance, 0, rows) + up.astype(F32)).astype(BF)
+            down = (own(-distance, 0, rows) + down.astype(F32)).astype(BF)
+    return own(0, 0, rows) + (up.astype(F32) + down.astype(F32))
+
+
+def ring_gather(block):
+    size = lax.axis_size("y")
+    mine = lax.axis_index("y")
+    rows = block.shape[0]
+    far, half = size // 2, rows // 2
+    whole = jnp.zeros((size * rows, block.shape[1]), block.dtype)
+
+    def put(whole, piece, offset, start):
+        chunk = lax.rem(mine + offset + size, size)
+        return lax.dynamic_update_slice_in_dim(whole, piece, chunk * rows + start, 0)
+
+    whole = put(whole, block, 0, 0)
+    up = down = block
+    for distance in range(1, far):
+        up, down = step(up, "y", 1), step(down, "y", -1)
+        whole = put(put(whole, up, -distance, 0), down, distance, 0)
+    up, down = step(up[:half], "y", 1), step(down[half:], "y", -1)
+    return put(put(whole, up, far, 0), down, far, half)
+
+
 def shards(tokens, routes, route_weights, gate_weight, up_weight, down_weight, cotangent):
     local_experts, depth, hidden_width = gate_weight.shape
     groups = lax.axis_size("z") * lax.axis_size("xl")
-    dp_size = lax.axis_size("y") * lax.axis_size("xh")
     num_experts = groups * local_experts
     tok_rows, top_count = routes.shape
     pairs = tok_rows * top_count
     slots_all = num_experts * CAPACITY
     half = depth // 2
+    core = lax.axis_index("exp")
 
     routes_flat = routes.reshape(pairs)
     expert_hot = (
@@ -37,38 +87,32 @@
         jnp.sum(jnp.where(hit, route_weights[None, :, k], 0.0), axis=1)
         for k, hit in enumerate(hits)
     )
-    sources = jnp.concatenate([tokens, cotangent], axis=1)
-    placed = jnp.dot(placing, sources, preferred_element_type=F32)
-    send = jnp.concatenate(
-        [placed[:, :depth], placed[:, depth:] * slot_weight[:, None]], axis=1
-    ).astype(BF)
-    arrived = exchange(send, ETP)
-    arrived = arrived.reshape(groups, local_experts, CAPACITY, 2 * depth)
-    arrived = jnp.swapaxes(arrived, 0, 1).reshape(local_experts, groups * CAPACITY, 2 * depth)
-    expert_in, expert_grad = arrived[..., :depth], arrived[..., depth:]
+    source = jnp.where(core == 0, tokens, cotangent)
+    scale = jnp.where(core == 0, 1.0, slot_weight)
+    send = (jnp.dot(placing, source, preferred_element_type=F32) * scale[:, None]).astype(BF)
+    arrived = exchange(send, ETP).reshape(groups, local_experts, CAPACITY, depth)
+    arrived = jnp.swapaxes(arrived, 0, 1).reshape(slots_all, depth)
+    arrived = lax.all_gather(arrived, "exp", axis=0, tiled=True)
+    arrived = arrived.reshape(2, local_experts, groups * CAPACITY, depth)
+    expert_in, expert_grad = arrived[0], arrived[1]
 
     terms = jnp.concatenate(
         [
-            jnp.einsum("erd,edf->erf", expert_in, gate_weight, preferred_element_type=F32).astype(BF),
-            jnp.einsum("erd,edf->erf", expert_in, up_weight, preferred_element_type=F32).astype(BF),
-            jnp.einsum("erd,efd->erf", expert_grad, down_weight, preferred_element_type=F32).astype(BF),
+            jnp.einsum("erd,edf->erf", expert_in, gate_weight, preferred_element_type=F32),
+            jnp.einsum("erd,edf->erf", expert_in, up_weight, preferred_element_type=F32),
+            jnp.einsum("erd,efd->erf", expert_grad, down_weight, preferred_element_type=F32),
         ],
         axis=2,
-    )
-    rows_all = local_experts * groups * CAPACITY
-    terms = exchange(terms.reshape(rows_all, 3 * hidden_width), ("y", "xh"))
-    sums = jnp.sum(
-        terms.reshape(dp_size, rows_all // dp_size, 3 * hidden_width).astype(F32), axis=0
-    )
+    ).reshape(slots_all, 3 * hidden_width)
+    sums = ring_sum(terms, slots_all // lax.axis_size("y"))
+    sums = sums + step(sums.astype(BF), "xh", 1).astype(F32)
     gate, up_proj, d_hidden = jnp.split(sums, 3, axis=1)
     sigmoid_gate = jax.nn.sigmoid(gate)
     silu_gate = gate * sigmoid_gate
     hidden = (silu_gate * up_proj).astype(BF)
     d_up = (d_hidden * silu_gate).astype(BF)
     d_gate = (d_hidden * up_proj * sigmoid_gate * (1.0 + gate * (1.0 - sigmoid_gate))).astype(BF)
-    acts = jnp.concatenate([hidden, d_gate, d_up], axis=1)
-    acts = lax.all_gather(acts, "xh", axis=0, tiled=True)
-    acts = lax.all_gather(acts, "y", axis=0, tiled=True)
+    acts = ring_gather(jnp.concatenate([hidden, d_gate, d_up], axis=1))
     acts = acts.reshape(local_experts, groups * CAPACITY, 3 * hidden_width)
     all_hidden, all_dgate, all_dup = jnp.split(acts, 3, axis=2)
 

time: 220 us -> 199 us (0.905); the launches traced: 220 us -> 196 us
  blocking collectives: 118 us -> 17.5 us
  starting transfers between devices: 11 us -> 82.9 us
  between operations: 14.3 us -> 1.24 us
  other arithmetic: 3.32 us -> 11.5 us
  local copies, waits for them, and re-layouts: 3.55 us -> 9.74 us
  waiting for transfers between devices: 59.7 us -> 65.7 us
    all_to_all x2 -> x0, blocking collectives: 96.7 us -> none  [exchange(): return lax.all_to_all(rows, axis, split_axis=0, concat_axis=0, tiled=True)]
    ppermute x0 -> x17, starting transfers between devices: none -> 56.6 us  [step(): lax.ppermute(block, axis, [(i, (i + shift) % size) for i in range(size)])]
    all_gather x1 -> x0, waiting for transfers between devices: 50.6 us -> none  [shards(): acts = lax.all_gather(acts, 'y', axis=0, tiled=True)]
    ppermute x0 -> x17, waiting for transfers between devices: none -> 44.3 us  [step(): lax.ppermute(block, axis, [(i, (i + shift) % size) for i in range(size)])]
    all_to_all x1 -> x2, starting transfers between devices: 10.9 us -> 26.3 us  [exchange(): return lax.all_to_all(rows, axis, split_axis=0, concat_axis=0, tiled=True)]
    all_to_all x1 -> x2, waiting for transfers between devices: 9.15 us -> 21.4 us  [exchange(): return lax.all_to_all(rows, axis, split_axis=0, concat_axis=0, tiled=True)]
    all_gather x1, blocking collectives: 13.8 us -> 4.37 us  [shards(): arrived = lax.all_gather(arrived, 'exp', axis=0, tiled=True)]
    all_to_all x1, blocking collectives: 7.59 us -> 13.1 us  [shards(): lax.all_to_all(parts, 'exp', split_axis=0, concat_axis=0, tiled=True)]
  transfers between devices with their start and end apart: 2 -> 19, of which waited for: 2 -> 16; matrix products, arithmetic and copies ran while one was open for 1% -> 2% of each run, Pallas kernels for 0% -> 0%
where the time goes in v2:
time: 199 us; the launch traced here: 196 us
  starting transfers between devices  82.9 us (42%)
  waiting for transfers between devices  65.7 us (33%)
  blocking collectives  17.5 us (9%)
  other arithmetic  11.5 us (6%)
  local copies, waits for them, and re-layouts  9.74 us (5%)
  matrix products  7.84 us (4%)
    ppermute x17, starting transfers between devices, step(): lax.ppermute(block, axis, [(i, (i + shift) % size) for i in range(size)])  56.6 us
    ppermute x17, waiting for transfers between devices, step(): lax.ppermute(block, axis, [(i, (i + shift) % size) for i in range(size)])  44.3 us
    all_to_all x2, starting transfers between devices, exchange(): return lax.all_to_all(rows, axis, split_axis=0, concat_axis=0, tiled=True)  26.3 us
    all_to_all x2, waiting for transfers between devices, exchange(): return lax.all_to_all(rows, axis, split_axis=0, concat_axis=0, tiled=True)  21.4 us
    all_to_all x1, blocking collectives, shards(): lax.all_to_all(parts, 'exp', split_axis=0, concat_axis=0, tiled=True)  13.1 us
    all_gather x1, blocking collectives, shards(): arrived = lax.all_gather(arrived, 'exp', axis=0, tiled=True)  4.37 us
  transfers between devices with their start and end apart: 19, of which 16 were waited for; matrix products, arithmetic and copies ran while one was open for 2% of the time, Pallas kernels for 0%

profile of v2, /device:TPU:1, one launch (start us, length us, event | category | flops | bytes accessed | tf_op | source)
XLA Modules:
  0.0 196.3 jit_solution(1860845108131889298)
XLA Ops:
  6.5 20.4 %all-to-all-start = ((bf16[32,16,256]{2,1,0:T(8,128)(2,1)}), bf16[32,16,256]{2,1,0:T(8,128)(2,1)S(1)}, u32[]{:S(2)}, u32[]{:S(2)}) async-start(bf16[32,16,256]{2,1,0:T(8,128)(2,1)} %bitcast.5), calls=%async_computation | async-start | bytes 524288 | tf_op jit(solution)/shard_map/all_to_all | solution.py:13
  26.9 11.1 %all-to-all-done = bf16[32,16,256]{2,1,0:T(8,128)(2,1)S(1)} async-done(((bf16[32,16,256]{2,1,0:T(8,128)(2,1)}), bf16[32,16,256]{2,1,0:T(8,128)(2,1)S(1)}, u32[]{:S(2)}, u32[]{:S(2)}) %all-to-all-start) | async-done | bytes 262176 | tf_op jit(solution)/shard_map/all_to_all | solution.py:13
  38.1 4.4 %all_gather.3 = bf16[1024,256]{1,0:T(8,128)(2,1)S(1)} all-gather(bf16[512,256]{1,0:T(8,128)(2,1)S(1)} %bitcast.71), channel_id=1, replica_groups=mesh['y'=8,'xh'=2,'exp'=2,'z'=8,'xl'=4] {'exp'}, dimensions={0}, use_global_device_ids=true | all-gather | bytes 786432 | tf_op jit(solution)/shard_map/all_gather | solution.py:95
  44.4 2.1 %copy-done.1 = f32[2,256,2304]{2,1,0:T(8,128)} copy-done((f32[2,256,2304]{2,1,0:T(8,128)}, f32[2,256,2304]{2,1,0:T(8,128)S(1)}, u32[]{:S(2)}) %copy-start.1) | copy-done | bytes 4718616
  46.5 3.3 %collective-permute-start = (bf16[32,2304]{1,0:T(8,128)(2,1)S(1)}, bf16[32,2304]{1,0:T(8,128)(2,1)S(1)}, u32[]{:S(2)}, u32[]{:S(2)}) collective-permute-start(bf16[32,2304]{1,0:T(8,128)(2,1)S(1)} %get-tuple-element.7), channel_id=1, source_target_pairs={{0,128},{128,256},{256,384},{384,512},{512,640},{640,768},{768,896... | collective-permute-start | bytes 442376 | tf_op jit(solution)/shard_map/ppermute | solution.py:18
  49.9 4.5 %collective-permute-start.4 = (bf16[32,2304]{1,0:T(8,128)(2,1)S(1)}, bf16[32,2304]{1,0:T(8,128)(2,1)S(1)}, u32[]{:S(2)}, u32[]{:S(2)}) collective-permute-start(bf16[32,2304]{1,0:T(8,128)(2,1)S(1)} %get-tuple-element.8), channel_id=1, source_target_pairs={{0,896},{128,0},{256,128},{384,256},{512,384},{640,512},{768,640},... | collective-permute-start | bytes 442376 | tf_op jit(solution)/shard_map/ppermute | solution.py:18
  54.4 2.0 collective-permute-done
  58.4 2.6 %collective-permute-start.1 = (bf16[64,2304]{1,0:T(8,128)(2,1)S(1)}, bf16[64,2304]{1,0:T(8,128)(2,1)S(1)}, u32[]{:S(2)}, u32[]{:S(2)}) collective-permute-start(bf16[64,2304]{1,0:T(8,128)(2,1)S(1)} %pad_maximum_fusion.2), channel_id=1, source_target_pairs={{0,128},{128,256},{256,384},{384,512},{512,640},{640,768},{768,896... | collective-permute-start | bytes 884744 | tf_op jit(solution)/shard_map/ppermute | solution.py:18
  61.0 4.6 %collective-permute-start.5 = (bf16[64,2304]{1,0:T(8,128)(2,1)S(1)}, bf16[64,2304]{1,0:T(8,128)(2,1)S(1)}, u32[]{:S(2)}, u32[]{:S(2)}) collective-permute-start(bf16[64,2304]{1,0:T(8,128)(2,1)S(1)} %pad_maximum_fusion.3), channel_id=1, source_target_pairs={{0,896},{128,0},{256,128},{384,256},{512,384},{640,512},{768,640},... | collective-permute-start | bytes 884744 | tf_op jit(solution)/shard_map/ppermute | solution.py:18
  65.6 4.2 %collective-permute-done.1 = bf16[64,2304]{1,0:T(8,128)(2,1)S(1)} collective-permute-done((bf16[64,2304]{1,0:T(8,128)(2,1)S(1)}, bf16[64,2304]{1,0:T(8,128)(2,1)S(1)}, u32[]{:S(2)}, u32[]{:S(2)}) %collective-permute-start.1) | collective-permute-done | bytes 294944 | tf_op jit(solution)/shard_map/ppermute | solution.py:18
  70.9 1.9 collective-permute-start.2
  72.9 7.8 %collective-permute-done.2 = bf16[64,2304]{1,0:T(8,128)(2,1)S(1)} collective-permute-done((bf16[64,2304]{1,0:T(8,128)(2,1)S(1)}, bf16[64,2304]{1,0:T(8,128)(2,1)S(1)}, u32[]{:S(2)}, u32[]{:S(2)}) %collective-permute-start.2) | collective-permute-done | bytes 294944 | tf_op jit(solution)/shard_map/ppermute | solution.py:18
  82.1 1.9 collective-permute-start.6
  84.0 3.4 %collective-permute-start.3 = (bf16[64,2304]{1,0:T(8,128)(2,1)S(1)}, bf16[64,2304]{1,0:T(8,128)(2,1)S(1)}, u32[]{:S(2)}, u32[]{:S(2)}) collective-permute-start(bf16[64,2304]{1,0:T(8,128)(2,1)S(1)} %get-tuple-element.3), channel_id=1, source_target_pairs={{0,128},{128,256},{256,384},{384,512},{512,640},{640,768},{768,896... | collective-permute-start | bytes 884744 | tf_op jit(solution)/shard_map/ppermute | solution.py:18
  87.4 2.2 %collective-permute-done.6 = bf16[64,2304]{1,0:T(8,128)(2,1)S(1)} collective-permute-done((bf16[64,2304]{1,0:T(8,128)(2,1)S(1)}, bf16[64,2304]{1,0:T(8,128)(2,1)S(1)}, u32[]{:S(2)}, u32[]{:S(2)}) %collective-permute-start.6) | collective-permute-done | bytes 294944 | tf_op jit(solution)/shard_map/ppermute | solution.py:18
  90.6 3.1 %collective-permute-start.7 = (bf16[64,2304]{1,0:T(8,128)(2,1)S(1)}, bf16[64,2304]{1,0:T(8,128)(2,1)S(1)}, u32[]{:S(2)}, u32[]{:S(2)}) collective-permute-start(bf16[64,2304]{1,0:T(8,128)(2,1)S(1)} %add_convert_fusion), channel_id=1, source_target_pairs={{0,896},{128,0},{256,128},{384,256},{512,384},{640,512},{768,640},... | collective-permute-start | bytes 884744 | tf_op jit(solution)/shard_map/ppermute | solution.py:18
  93.8 4.3 %collective-permute-done.7 = bf16[64,2304]{1,0:T(8,128)(2,1)S(1)} collective-permute-done((bf16[64,2304]{1,0:T(8,128)(2,1)S(1)}, bf16[64,2304]{1,0:T(8,128)(2,1)S(1)}, u32[]{:S(2)}, u32[]{:S(2)}) %collective-permute-start.7) | collective-permute-done | bytes 294944 | tf_op jit(solution)/shard_map/ppermute | solution.py:18
  99.3 4.4 %collective-permute-start.8 = (bf16[64,2304]{1,0:T(8,128)(2,1)S(1)}, bf16[64,2304]{1,0:T(8,128)(2,1)S(1)}, u32[]{:S(2)}, u32[]{:S(2)}) collective-permute-start(bf16[64,2304]{1,0:T(8,128)(2,1)S(1)} %fusion.12), channel_id=1, source_target_pairs={{0,64},{64,0},{1,65},{65,1},{2,66},{66,2},{3,67},{67,3},{4,68},{68... | collective-permute-start | bytes 884744 | tf_op jit(solution)/shard_map/ppermute | solution.py:18
  103.7 12.5 %collective-permute-done.8 = bf16[64,2304]{1,0:T(8,128)(2,1)S(1)} collective-permute-done((bf16[64,2304]{1,0:T(8,128)(2,1)S(1)}, bf16[64,2304]{1,0:T(8,128)(2,1)S(1)}, u32[]{:S(2)}, u32[]{:S(2)}) %collective-permute-start.8) | collective-permute-done | bytes 294944 | tf_op jit(solution)/shard_map/ppermute | solution.py:18
  118.4 2.0 %collective-permute-start.9 = (bf16[64,2304]{1,0:T(8,128)(2,1)}, bf16[64,2304]{1,0:T(8,128)(2,1)}, u32[]{:S(2)}, u32[]{:S(2)}) collective-permute-start(bf16[64,2304]{1,0:T(8,128)(2,1)} %get-tuple-element.16), channel_id=1, source_target_pairs={{0,128},{128,256},{256,384},{384,512},{512,640},{640,768},{768,896... | collective-permute-start | bytes 884744 | tf_op jit(solution)/shard_map/ppermute | solution.py:18
  120.4 4.5 %collective-permute-start.10 = (bf16[64,2304]{1,0:T(8,128)(2,1)}, bf16[64,2304]{1,0:T(8,128)(2,1)S(1)}, u32[]{:S(2)}, u32[]{:S(2)}) collective-permute-start(bf16[64,2304]{1,0:T(8,128)(2,1)} %get-tuple-element.16), channel_id=1, source_target_pairs={{0,896},{128,0},{256,128},{384,256},{512,384},{640,512},{768,640},... | collective-permute-start | bytes 884744 | tf_op jit(solution)/shard_map/ppermute | solution.py:18
  124.9 2.5 %collective-permute-done.9 = bf16[64,2304]{1,0:T(8,128)(2,1)} collective-permute-done((bf16[64,2304]{1,0:T(8,128)(2,1)}, bf16[64,2304]{1,0:T(8,128)(2,1)}, u32[]{:S(2)}, u32[]{:S(2)}) %collective-permute-start.9) | collective-permute-done | bytes 294944 | tf_op jit(solution)/shard_map/ppermute | solution.py:18
  130.3 4.6 %collective-permute-start.12 = (bf16[64,2304]{1,0:T(8,128)(2,1)S(1)}, bf16[64,2304]{1,0:T(8,128)(2,1)S(1)}, u32[]{:S(2)}, u32[]{:S(2)}) collective-permute-start(bf16[64,2304]{1,0:T(8,128)(2,1)S(1)} %collective-permute-done.10), channel_id=1, source_target_pairs={{0,896},{128,0},{256,128},{384,256},{512,384},{640,512},{768,640},... | collective-permute-start | bytes 884744 | tf_op jit(solution)/shard_map/ppermute | solution.py:18
  136.2 1.9 collective-permute-start.13
  138.5 5.0 %collective-permute-start.14 = (bf16[64,2304]{1,0:T(8,128)(2,1)S(1)}, bf16[64,2304]{1,0:T(8,128)(2,1)S(1)}, u32[]{:S(2)}, u32[]{:S(2)}) collective-permute-start(bf16[64,2304]{1,0:T(8,128)(2,1)S(1)} %collective-permute-done.12), channel_id=1, source_target_pairs={{0,896},{128,0},{256,128},{384,256},{512,384},{640,512},{768,640},... | collective-permute-start | bytes 884744 | tf_op jit(solution)/shard_map/ppermute | solution.py:18
  143.6 2.2 %collective-permute-done.13 = bf16[64,2304]{1,0:T(8,128)(2,1)S(1)} collective-permute-done((bf16[64,2304]{1,0:T(8,128)(2,1)S(1)}, bf16[64,2304]{1,0:T(8,128)(2,1)S(1)}, u32[]{:S(2)}, u32[]{:S(2)}) %collective-permute-start.13) | collective-permute-done | bytes 294944 | tf_op jit(solution)/shard_map/ppermute | solution.py:18
  145.8 1.9 collective-permute-start.15
  148.4 5.0 %collective-permute-start.16 = (bf16[32,2304]{1,0:T(8,128)(2,1)S(1)}, bf16[32,2304]{1,0:T(8,128)(2,1)S(1)}, u32[]{:S(2)}, u32[]{:S(2)}) collective-permute-start(bf16[32,2304]{1,0:T(8,128)(2,1)S(1)} %slice.90), channel_id=1, source_target_pairs={{0,896},{128,0},{256,128},{384,256},{512,384},{640,512},{768,640},... | collective-permute-start | bytes 442376 | tf_op jit(solution)/shard_map/ppermute | solution.py:18
  154.8 2.2 %collective-permute-done.16 = bf16[32,2304]{1,0:T(8,128)(2,1)S(1)} collective-permute-done((bf16[32,2304]{1,0:T(8,128)(2,1)S(1)}, bf16[32,2304]{1,0:T(8,128)(2,1)S(1)}, u32[]{:S(2)}, u32[]{:S(2)}) %collective-permute-start.16) | collective-permute-done | bytes 147488 | tf_op jit(solution)/shard_map/ppermute | solution.py:18
  158.5 13.1 %all_to_all.26 = bf16[2,2,256,256]{2,3,1,0:T(8,128)(2,1)S(1)} all-to-all(bf16[2,2,256,256]{2,3,1,0:T(8,128)(2,1)S(1)} %pad_maximum_fusion.1), channel_id=1, replica_groups=mesh['y'=8,'xh'=2,'exp'=2,'z'=8,'xl'=4] {'exp'}, dimensions={0} | all-to-all | bytes 1048576 | tf_op jit(solution)/shard_map/all_to_all | solution.py:136
  175.8 5.9 %all-to-all-start.2 = ((bf16[32,16,256]{2,1,0:T(8,128)(2,1)}), bf16[32,16,256]{2,1,0:T(8,128)(2,1)}, u32[]{:S(2)}, u32[]{:S(2)}) async-start(bf16[32,16,256]{2,1,0:T(8,128)(2,1)} %copy_bitcast_fusion), calls=%async_computation.2 | async-start | bytes 524288 | tf_op jit(solution)/shard_map/all_to_all | solution.py:13
  183.0 10.3 %all-to-all-done.2 = bf16[32,16,256]{2,1,0:T(8,128)(2,1)} async-done(((bf16[32,16,256]{2,1,0:T(8,128)(2,1)}), bf16[32,16,256]{2,1,0:T(8,128)(2,1)}, u32[]{:S(2)}, u32[]{:S(2)}) %all-to-all-start.2) | async-done | bytes 262176 | tf_op jit(solution)/shard_map/all_to_all | solution.py:13
  (80 shorter events, 33.3 us)
Async XLA Ops:
  0.6 41.9 %copy-start = (bf16[2,256,768]{2,1,0:T(8,128)(2,1)S(1)}, bf16[2,256,768]{2,1,0:T(8,128)(2,1)}, u32[]{:S(2)}) copy-start(bf16[2,256,768]{2,1,0:T(8,128)(2,1)} %param.11) | copy-start | bytes 2359300
  6.5 31.6 %all-to-all-start = ((bf16[32,16,256]{2,1,0:T(8,128)(2,1)}), bf16[32,16,256]{2,1,0:T(8,128)(2,1)S(1)}, u32[]{:S(2)}, u32[]{:S(2)}) async-start(bf16[32,16,256]{2,1,0:T(8,128)(2,1)} %bitcast.5), calls=%async_computation | async-start | bytes 524288 | tf_op jit(solution)/shard_map/all_to_all | solution.py:13
  38.1 4.8 %copy-start.2 = (bf16[2,256,768]{2,1,0:T(8,128)(2,1)S(1)}, bf16[2,256,768]{2,1,0:T(8,128)(2,1)}, u32[]{:S(2)}) copy-start(bf16[2,256,768]{2,1,0:T(8,128)(2,1)} %param.10) | copy-start | bytes 2359300
  42.5 1.1 copy-start.4
  44.4 2.1 %copy-start.1 = (f32[2,256,2304]{2,1,0:T(8,128)}, f32[2,256,2304]{2,1,0:T(8,128)S(1)}, u32[]{:S(2)}) copy-start(f32[2,256,2304]{2,1,0:T(8,128)S(1)} %pad_maximum_fusion) | copy-start | bytes 14155780
  46.5 9.8 %collective-permute-start = (bf16[32,2304]{1,0:T(8,128)(2,1)S(1)}, bf16[32,2304]{1,0:T(8,128)(2,1)S(1)}, u32[]{:S(2)}, u32[]{:S(2)}) collective-permute-start(bf16[32,2304]{1,0:T(8,128)(2,1)S(1)} %get-tuple-element.7), channel_id=1, source_target_pairs={{0,128},{128,256},{256,384},{384,512},{512,640},{640,768},{768,896... | collective-permute-start | bytes 442376 | tf_op jit(solution)/shard_map/ppermute | solution.py:18
  49.9 7.3 %collective-permute-start.4 = (bf16[32,2304]{1,0:T(8,128)(2,1)S(1)}, bf16[32,2304]{1,0:T(8,128)(2,1)S(1)}, u32[]{:S(2)}, u32[]{:S(2)}) collective-permute-start(bf16[32,2304]{1,0:T(8,128)(2,1)S(1)} %get-tuple-element.8), channel_id=1, source_target_pairs={{0,896},{128,0},{256,128},{384,256},{512,384},{640,512},{768,640},... | collective-permute-start | bytes 442376 | tf_op jit(solution)/shard_map/ppermute | solution.py:18
  58.4 11.4 %collective-permute-start.1 = (bf16[64,2304]{1,0:T(8,128)(2,1)S(1)}, bf16[64,2304]{1,0:T(8,128)(2,1)S(1)}, u32[]{:S(2)}, u32[]{:S(2)}) collective-permute-start(bf16[64,2304]{1,0:T(8,128)(2,1)S(1)} %pad_maximum_fusion.2), channel_id=1, source_target_pairs={{0,128},{128,256},{256,384},{384,512},{512,640},{640,768},{768,896... | collective-permute-start | bytes 884744 | tf_op jit(solution)/shard_map/ppermute | solution.py:18
  61.0 11.9 %collective-permute-start.5 = (bf16[64,2304]{1,0:T(8,128)(2,1)S(1)}, bf16[64,2304]{1,0:T(8,128)(2,1)S(1)}, u32[]{:S(2)}, u32[]{:S(2)}) collective-permute-start(bf16[64,2304]{1,0:T(8,128)(2,1)S(1)} %pad_maximum_fusion.3), channel_id=1, source_target_pairs={{0,896},{128,0},{256,128},{384,256},{512,384},{640,512},{768,640},... | collective-permute-start | bytes 884744 | tf_op jit(solution)/shard_map/ppermute | solution.py:18
  70.9 9.8 %collective-permute-start.2 = (bf16[64,2304]{1,0:T(8,128)(2,1)S(1)}, bf16[64,2304]{1,0:T(8,128)(2,1)S(1)}, u32[]{:S(2)}, u32[]{:S(2)}) collective-permute-start(bf16[64,2304]{1,0:T(8,128)(2,1)S(1)} %add_convert_fusion.3), channel_id=1, source_target_pairs={{0,128},{128,256},{256,384},{384,512},{512,640},{640,768},{768,896... | collective-permute-start | bytes 884744 | tf_op jit(solution)/shard_map/ppermute | solution.py:18
  82.1 7.5 %collective-permute-start.6 = (bf16[64,2304]{1,0:T(8,128)(2,1)S(1)}, bf16[64,2304]{1,0:T(8,128)(2,1)S(1)}, u32[]{:S(2)}, u32[]{:S(2)}) collective-permute-start(bf16[64,2304]{1,0:T(8,128)(2,1)S(1)} %get-tuple-element.4), channel_id=1, source_target_pairs={{0,896},{128,0},{256,128},{384,256},{512,384},{640,512},{768,640},... | collective-permute-start | bytes 884744 | tf_op jit(solution)/shard_map/ppermute | solution.py:18
  84.0 9.8 %collective-permute-start.3 = (bf16[64,2304]{1,0:T(8,128)(2,1)S(1)}, bf16[64,2304]{1,0:T(8,128)(2,1)S(1)}, u32[]{:S(2)}, u32[]{:S(2)}) collective-permute-start(bf16[64,2304]{1,0:T(8,128)(2,1)S(1)} %get-tuple-element.3), channel_id=1, source_target_pairs={{0,128},{128,256},{256,384},{384,512},{512,640},{640,768},{768,896... | collective-permute-start | bytes 884744 | tf_op jit(solution)/shard_map/ppermute | solution.py:18
  90.6 7.5 %collective-permute-start.7 = (bf16[64,2304]{1,0:T(8,128)(2,1)S(1)}, bf16[64,2304]{1,0:T(8,128)(2,1)S(1)}, u32[]{:S(2)}, u32[]{:S(2)}) collective-permute-start(bf16[64,2304]{1,0:T(8,128)(2,1)S(1)} %add_convert_fusion), channel_id=1, source_target_pairs={{0,896},{128,0},{256,128},{384,256},{512,384},{640,512},{768,640},... | collective-permute-start | bytes 884744 | tf_op jit(solution)/shard_map/ppermute | solution.py:18
  99.3 16.9 %collective-permute-start.8 = (bf16[64,2304]{1,0:T(8,128)(2,1)S(1)}, bf16[64,2304]{1,0:T(8,128)(2,1)S(1)}, u32[]{:S(2)}, u32[]{:S(2)}) collective-permute-start(bf16[64,2304]{1,0:T(8,128)(2,1)S(1)} %fusion.12), channel_id=1, source_target_pairs={{0,64},{64,0},{1,65},{65,1},{2,66},{66,2},{3,67},{67,3},{4,68},{68... | collective-permute-start | bytes 884744 | tf_op jit(solution)/shard_map/ppermute | solution.py:18
  118.4 9.0 %collective-permute-start.9 = (bf16[64,2304]{1,0:T(8,128)(2,1)}, bf16[64,2304]{1,0:T(8,128)(2,1)}, u32[]{:S(2)}, u32[]{:S(2)}) collective-permute-start(bf16[64,2304]{1,0:T(8,128)(2,1)} %get-tuple-element.16), channel_id=1, source_target_pairs={{0,128},{128,256},{256,384},{384,512},{512,640},{640,768},{768,896... | collective-permute-start | bytes 884744 | tf_op jit(solution)/shard_map/ppermute | solution.py:18
  120.4 9.9 %collective-permute-start.10 = (bf16[64,2304]{1,0:T(8,128)(2,1)}, bf16[64,2304]{1,0:T(8,128)(2,1)S(1)}, u32[]{:S(2)}, u32[]{:S(2)}) collective-permute-start(bf16[64,2304]{1,0:T(8,128)(2,1)} %get-tuple-element.16), channel_id=1, source_target_pairs={{0,896},{128,0},{256,128},{384,256},{512,384},{640,512},{768,640},... | collective-permute-start | bytes 884744 | tf_op jit(solution)/shard_map/ppermute | solution.py:18
  127.4 8.9 %collective-permute-start.11 = (bf16[64,2304]{1,0:T(8,128)(2,1)}, bf16[64,2304]{1,0:T(8,128)(2,1)S(1)}, u32[]{:S(2)}, u32[]{:S(2)}) collective-permute-start(bf16[64,2304]{1,0:T(8,128)(2,1)} %collective-permute-done.9), channel_id=1, source_target_pairs={{0,128},{128,256},{256,384},{384,512},{512,640},{640,768},{768,896... | collective-permute-start | bytes 884744 | tf_op jit(solution)/shard_map/ppermute | solution.py:18
  130.3 8.2 %collective-permute-start.12 = (bf16[64,2304]{1,0:T(8,128)(2,1)S(1)}, bf16[64,2304]{1,0:T(8,128)(2,1)S(1)}, u32[]{:S(2)}, u32[]{:S(2)}) collective-permute-start(bf16[64,2304]{1,0:T(8,128)(2,1)S(1)} %collective-permute-done.10), channel_id=1, source_target_pairs={{0,896},{128,0},{256,128},{384,256},{512,384},{640,512},{768,640},... | collective-permute-start | bytes 884744 | tf_op jit(solution)/shard_map/ppermute | solution.py:18
  136.2 9.6 %collective-permute-start.13 = (bf16[64,2304]{1,0:T(8,128)(2,1)S(1)}, bf16[64,2304]{1,0:T(8,128)(2,1)S(1)}, u32[]{:S(2)}, u32[]{:S(2)}) collective-permute-start(bf16[64,2304]{1,0:T(8,128)(2,1)S(1)} %collective-permute-done.11), channel_id=1, source_target_pairs={{0,128},{128,256},{256,384},{384,512},{512,640},{640,768},{768,896... | collective-permute-start | bytes 884744 | tf_op jit(solution)/shard_map/ppermute | solution.py:18
  138.5 9.8 %collective-permute-start.14 = (bf16[64,2304]{1,0:T(8,128)(2,1)S(1)}, bf16[64,2304]{1,0:T(8,128)(2,1)S(1)}, u32[]{:S(2)}, u32[]{:S(2)}) collective-permute-start(bf16[64,2304]{1,0:T(8,128)(2,1)S(1)} %collective-permute-done.12), channel_id=1, source_target_pairs={{0,896},{128,0},{256,128},{384,256},{512,384},{640,512},{768,640},... | collective-permute-start | bytes 884744 | tf_op jit(solution)/shard_map/ppermute | solution.py:18
  143.6 13.9 %copy-start.5 = (bf16[2,768,256]{2,1,0:T(8,128)(2,1)S(1)}, bf16[2,768,256]{2,1,0:T(8,128)(2,1)}, u32[]{:S(2)}) copy-start(bf16[2,768,256]{2,1,0:T(8,128)(2,1)} %param.12) | copy-start | bytes 2359300
  145.8 9.0 %collective-permute-start.15 = (bf16[32,2304]{1,0:T(8,128)(2,1)S(1)}, bf16[32,2304]{1,0:T(8,128)(2,1)S(1)}, u32[]{:S(2)}, u32[]{:S(2)}) collective-permute-start(bf16[32,2304]{1,0:T(8,128)(2,1)S(1)} %slice.89), channel_id=1, source_target_pairs={{0,128},{128,256},{256,384},{384,512},{512,640},{640,768},{768,896... | collective-permute-start | bytes 442376 | tf_op jit(solution)/shard_map/ppermute | solution.py:18
  148.4 8.7 %collective-permute-start.16 = (bf16[32,2304]{1,0:T(8,128)(2,1)S(1)}, bf16[32,2304]{1,0:T(8,128)(2,1)S(1)}, u32[]{:S(2)}, u32[]{:S(2)}) collective-permute-start(bf16[32,2304]{1,0:T(8,128)(2,1)S(1)} %slice.90), channel_id=1, source_target_pairs={{0,896},{128,0},{256,128},{384,256},{512,384},{640,512},{768,640},... | collective-permute-start | bytes 442376 | tf_op jit(solution)/shard_map/ppermute | solution.py:18
  153.5 4.4 %copy-start.3 = (bf16[2,256,768]{2,1,0:T(8,128)(2,1)S(1)}, bf16[2,256,768]{2,1,0:T(8,128)(2,1)}, u32[]{:S(2)}) copy-start(bf16[2,256,768]{2,1,0:T(8,128)(2,1)} %param.10) | copy-start | bytes 2359300
  175.8 17.5 %all-to-all-start.2 = ((bf16[32,16,256]{2,1,0:T(8,128)(2,1)}), bf16[32,16,256]{2,1,0:T(8,128)(2,1)}, u32[]{:S(2)}, u32[]{:S(2)}) async-start(bf16[32,16,256]{2,1,0:T(8,128)(2,1)} %copy_bitcast_fusion), calls=%async_computation.2 | async-start | bytes 524288 | tf_op jit(solution)/shard_map/all_to_all | solution.py:13

commit v3 on v1

v3 whole, which is shorter than its diff:
```python
import functools

import jax
import jax.numpy as jnp
from jax import lax
from jax.experimental import pallas as pl
from jax.experimental.pallas import tpu as pltpu
from jax.sharding import Mesh, PartitionSpec as P

BF = jnp.bfloat16
F32 = jnp.float32
ETP = ("z", "xl")
CAPACITY = 8
VMEM = pl.BlockSpec(memory_space=pltpu.VMEM)
SMEM = pl.BlockSpec(memory_space=pltpu.SMEM)
LIMIT = pltpu.CompilerParams(vmem_limit_bytes=40 * 1024 * 1024)
NT = (((1,), (1,)), ((), ()))


def call(kernel, outs, *args, scalars=0, scratch=()):
    return pl.pallas_call(
        kernel,
        out_shape=outs,
        in_specs=[SMEM] * scalars + [VMEM] * (len(args) - scalars),
        out_specs=jax.tree.map(lambda _: VMEM, outs),
        scratch_shapes=scratch,
        compiler_params=LIMIT,
    )(*args)


def shape(dims, kind):
    return jax.ShapeDtypeStruct(dims, kind)


def iota(dims, axis):
    return lax.broadcasted_iota(jnp.int32, dims, axis)


def place_rows(experts, core_ref, routes_ref, weights_ref, tokens_ref, cot_ref, send_ref, slot_ref):
    top_count, tok_rows = routes_ref.shape
    hots = [iota((experts, tok_rows), 0) == routes_ref[k : k + 1, :] for k in range(top_count)]
    both = sum(jnp.where(hot, 1.0, 0.0) for hot in hots)
    earlier = jnp.where(iota((tok_rows, tok_rows), 0) < iota((tok_rows, tok_rows), 1), 1.0, 0.0)
    count = jnp.dot(both.astype(BF), earlier.astype(BF), preferred_element_type=F32)
    placing = jnp.zeros((send_ref.shape[0], tok_rows), F32)
    slot_weight = jnp.zeros((send_ref.shape[0], 1), F32)
    for k, hot in enumerate(hots):
        position = jnp.sum(jnp.where(hot, count, 0.0), axis=0, keepdims=True).astype(jnp.int32)
        slot = routes_ref[k : k + 1, :] * CAPACITY + position
        slot_ref[k : k + 1, :] = slot
        hit = iota(placing.shape, 0) == slot
        placing = placing + jnp.where(hit, 1.0, 0.0)
        slot_weight = slot_weight + jnp.sum(
            jnp.where(hit, weights_ref[k : k + 1, :], 0.0), axis=1, keepdims=True
        )
    first = core_ref[0] == 0
    source = jnp.where(first, tokens_ref[...].astype(F32), cot_ref[...].astype(F32)).astype(BF)
    scale = jnp.where(first, 1.0, slot_weight)
    rows = jnp.dot(placing.astype(BF), source, preferred_element_type=F32)
    send_ref[...] = (rows * scale).astype(BF)


def first_terms(mine_ref, rows_ref, gate_ref, up_ref, down_ref, terms_ref, grad_ref, up_msg, down_msg):
    local_experts, depth, width = gate_ref.shape
    slots = rows_ref.shape[0] // 2
    groups = slots // (local_experts * CAPACITY)
    kinds = []
    for kind in range(2):
        rows = rows_ref[kind * slots : (kind + 1) * slots, :].astype(F32)
        kinds.append(rows.reshape(groups, local_experts, CAPACITY, depth))
    count = groups * CAPACITY
    for e in range(local_experts):
        rows_in = kinds[0][:, e].reshape(count, depth).astype(BF)
        rows_grad = kinds[1][:, e].reshape(count, depth).astype(BF)
        here = slice(e * count, (e + 1) * count)
        terms_ref[here, :width] = jnp.dot(rows_in, gate_ref[e], preferred_element_type=F32)
        terms_ref[here, width : 2 * width] = jnp.dot(rows_in, up_ref[e], preferred_element_type=F32)
        terms_ref[here, 2 * width :] = lax.dot_general(
            rows_grad, down_ref[e], NT, preferred_element_type=F32
        )
        grad_ref[e] = rows_grad
    half = up_msg.shape[0]
    chunk = lax.rem(mine_ref[0] + 4, 8)
    base = pl.multiple_of(chunk * 2 * half, 2 * half)
    up_msg[...] = terms_ref[pl.ds(base, half), :].astype(BF)
    down_msg[...] = terms_ref[pl.ds(base + half, half), :].astype(BF)


def add_terms(distance, mine_ref, terms_ref, up_ref, down_ref, up_msg, down_msg):
    rows = up_msg.shape[0]
    for offset, came, out in ((distance, up_ref, up_msg), (-distance, down_ref, down_msg)):
        chunk = lax.rem(mine_ref[0] + (offset + 8), 8)
        base = pl.multiple_of(chunk * rows, rows)
        if came.shape[0] == rows:
            out[...] = (terms_ref[pl.ds(base, rows), :] + came[...].astype(F32)).astype(BF)
        else:
            half = rows // 2
            for part, has in ((0, offset > 0), (half, offset < 0)):
                own = terms_ref[pl.ds(base + part, half), :]
                own = own + came[...].astype(F32) if has else own
                out[part : part + half, :] = own.astype(BF)


def end_terms(mine_ref, terms_ref, up_ref, down_ref, out_ref):
    rows = out_ref.shape[0]
    base = pl.multiple_of(mine_ref[0] * rows, rows)
    came = up_ref[...].astype(F32) + down_ref[...].astype(F32)
    out_ref[...] = (terms_ref[pl.ds(base, rows), :] + came).astype(BF)


def activate(pair_ref, out_ref):
    rows, width = out_ref.shape[0], out_ref.shape[1] // 3
    low, high = slice(0, rows), slice(rows, 2 * rows)

    def total(part):
        cols = slice(part * width, (part + 1) * width)
        return pair_ref[low, cols].astype(F32) + pair_ref[high, cols].astype(F32)

    gate, up_proj, d_hidden = total(0), total(1), total(2)
    sigmoid_gate = jax.nn.sigmoid(gate)
    silu_gate = gate * sigmoid_gate
    out_ref[:, :width] = (silu_gate * up_proj).astype(BF)
    out_ref[:, width : 2 * width] = (
        d_hidden * up_proj * sigmoid_gate * (1.0 + gate * (1.0 - sigmoid_gate))
    ).astype(BF)
    out_ref[:, 2 * width :] = (d_hidden * silu_gate).astype(BF)


def last_terms(pieces, mine_ref, *refs):
    piece_refs = refs[: len(pieces)]
    gate_ref, up_ref, down_ref, parts_ref, hidden_ref, acts = refs[len(pieces) :]
    local_experts, depth, width = gate_ref.shape
    rows = acts.shape[0] // 8
    for (offset, start), piece in zip(pieces, piece_refs):
        chunk = lax.rem(mine_ref[0] + (offset + 8), 8)
        base = pl.multiple_of(chunk * rows, rows) + start
        acts[pl.ds(pl.multiple_of(base, rows // 2), piece.shape[0]), :] = piece[...]
    count = acts.shape[0] // local_experts
    outs, grads = [], []
    for e in range(local_experts):
        here = slice(e * count, (e + 1) * count)
        hidden = acts[here, :width]
        hidden_ref[e] = hidden
        out = jnp.dot(hidden, down_ref[e], preferred_element_type=F32)
        grad = lax.dot_general(
            acts[here, width : 2 * width], gate_ref[e], NT, preferred_element_type=F32
        ) + lax.dot_general(acts[here, 2 * width :], up_ref[e], NT, preferred_element_type=F32)
        outs.append(out.reshape(count // CAPACITY, CAPACITY, depth))
        grads.append(grad.reshape(count // CAPACITY, CAPACITY, depth))
    out, grad = jnp.concatenate(outs, axis=1), jnp.concatenate(grads, axis=1)
    half = depth // 2
    for j in range(2):
        cols = slice(j * half, (j + 1) * half)
        parts_ref[j, :, :, :half] = out[:, :, cols].astype(BF)
        parts_ref[j, :, :, half:] = grad[:, :, cols].astype(BF)


def combine(slot_ref, weights_ref, back_ref, mixed_ref, grads_ref):
    top_count, tok_rows = slot_ref.shape
    slots, width = back_ref.shape[0] // 2, back_ref.shape[1]
    half = width // 2
    same = iota((tok_rows, tok_rows), 0) == iota((tok_rows, tok_rows), 1)

    def column(row):
        return jnp.sum(jnp.where(same, row, 0.0), axis=1, keepdims=True)

    mixed = jnp.zeros((tok_rows, half), F32)
    grads = jnp.zeros((tok_rows, half), F32)
    for k in range(top_count):
        slot = column(slot_ref[k : k + 1, :].astype(F32)).astype(jnp.int32)
        hot = jnp.where(iota((tok_rows, slots), 1) == slot, 1.0, 0.0).astype(BF)
        picked = jnp.dot(hot, back_ref[:slots, :], preferred_element_type=F32) + jnp.dot(
            hot, back_ref[slots:, :], preferred_element_type=F32
        )
        mixed = mixed + picked[:, :half] * column(weights_ref[k : k + 1, :])
        grads = grads + picked[:, half:]
    mixed_ref[...] = mixed.astype(BF)
    grads_ref[...] = grads.astype(BF)


def exchange(rows, axis):
    return lax.all_to_all(rows, axis, split_axis=0, concat_axis=0, tiled=True)


def step(block, axis, shift):
    size = lax.axis_size(axis)
    return lax.ppermute(block, axis, [(i, (i + shift) % size) for i in range(size)])


def both_ways(up, down):
    return step(up, "y", 1), step(down, "y", -1)


def shards(tokens, routes, route_weights, gate_weight, up_weight, down_weight, cotangent):
    local_experts, depth, width = gate_weight.shape
    groups = lax.axis_size("z") * lax.axis_size("xl")
    experts = groups * local_experts
    tok_rows, top_count = routes.shape
    slots = experts * CAPACITY
    chunk = slots // 8
    core = lax.axis_index("exp").reshape(1)
    mine = lax.axis_index("y").reshape(1)
    routes, route_weights = routes.T, route_weights.T

    send, slot_index = call(
        functools.partial(place_rows, experts),
        (shape((slots, depth), BF), shape((top_count, tok_rows), jnp.int32)),
        core, routes, route_weights, tokens, cotangent, scalars=1,
    )
    arrived = lax.all_gather(exchange(send, ETP), "exp", axis=0, tiled=True)

    block = shape((chunk, 3 * width), BF)
    half_block = shape((chunk // 2, 3 * width), BF)
    terms, expert_grad, up, down = call(
        first_terms,
        (
            shape((slots, 3 * width), F32),
            shape((local_experts, groups * CAPACITY, depth), BF),
            half_block, half_block,
        ),
        mine, arrived, gate_weight, up_weight, down_weight, scalars=1,
    )
    for distance in (3, 2, 1):
        up, down = both_ways(up, down)
        up, down = call(
            functools.partial(add_terms, distance), (block, block), mine, terms, up, down, scalars=1
        )
    up, down = both_ways(up, down)
    sums = call(end_terms, block, mine, terms, up, down, scalars=1)
    acts = call(activate, block, lax.all_gather(sums, "xh", axis=0, tiled=True))

    pieces, values = [(0, 0)], [acts]
    up = down = acts
    for distance in (1, 2, 3):
        up, down = both_ways(up, down)
        pieces += [(-distance, 0), (distance, 0)]
        values += [up, down]
    pieces += [(4, 0), (4, chunk // 2)]
    values += both_ways(up[: chunk // 2], down[chunk // 2 :])
    parts, hidden = call(
        functools.partial(last_terms, pieces),
        (
            shape((2, groups, local_experts * CAPACITY, depth), BF),
            shape((local_experts, groups * CAPACITY, width), BF),
        ),
        mine, *values, gate_weight, up_weight, down_weight, scalars=1,
        scratch=[pltpu.VMEM((slots, 3 * width), BF)],
    )
    d_down = jnp.einsum("erf,erd->efd", hidden, expert_grad, preferred_element_type=F32).astype(BF)
    back = exchange(parts.reshape(2 * slots, depth), ("exp",) + ETP)
    mixed, d_tokens = call(
        combine,
        (shape((tok_rows, depth // 2), BF), shape((tok_rows, depth // 2), BF)),
        slot_index, route_weights, back,
    )
    return mixed, d_tokens, d_down


def solution(mesh):
    fine = Mesh(mesh.devices.reshape(8, 2, 2, 8, 4), ("y", "xh", "exp", "z", "xl"))
    dp = ("y", "xh")
    in_specs = (
        P(ETP, dp),
        P(ETP, None),
        P(ETP, None),
        P(ETP, dp, "exp"),
        P(ETP, dp, "exp"),
        P(ETP, "exp", dp),
        P(ETP, dp),
    )
    out_specs = (P(ETP, dp + ("exp",)), P(ETP, dp + ("exp",)), P(ETP, "exp", dp))
    return jax.shard_map(shards, mesh=fine, in_specs=in_specs, out_specs=out_specs, check_vma=False)
```

time: 220 us -> 186 us (0.85)
  blocking collectives: 118 us -> 20.1 us
  starting transfers between devices: 11 us -> 90.9 us
  between operations: 14.3 us -> 0.87 us
  matrix products: 9.85 us -> 1.33 us
  Pallas kernels: 0 us -> 5.17 us
  other arithmetic: 3.32 us -> 0 us
  local copies, waits for them, and re-layouts: 3.55 us -> 6.47 us
    all_to_all x3 -> x0, blocking collectives: 104 us -> none  [the longest x2 96.7 us: exchange(): return lax.all_to_all(rows, axis, split_axis=0, concat_axis=0, tiled=True)]
    ppermute x0 -> x16, starting transfers between devices: none -> 53.8 us  [step(): lax.ppermute(block, axis, [(i, (i + shift) % size) for i in range(size)])]
    all_gather x1 -> x0, waiting for transfers between devices: 50.6 us -> none  [shards(): acts = lax.all_gather(acts, 'y', axis=0, tiled=True)]
    ppermute x0 -> x16, waiting for transfers between devices: none -> 32.9 us  [step(): lax.ppermute(block, axis, [(i, (i + shift) % size) for i in range(size)])]
    all_to_all x1 -> x2, starting transfers between devices: 10.9 us -> 37.1 us  [exchange(): return lax.all_to_all(rows, axis, split_axis=0, concat_axis=0, tiled=True)]
    all_to_all x1 -> x2, waiting for transfers between devices: 9.15 us -> 27.5 us  [exchange(): return lax.all_to_all(rows, axis, split_axis=0, concat_axis=0, tiled=True)]
    dot_general x10 -> x1, matrix products: 9.85 us -> 1.33 us  [shards(): jnp.einsum('erf,erd->efd', hidden, expert_grad, preferred_element_type=F32)]
    all_gather x1 -> x2, blocking collectives: 13.8 us -> 20.1 us  [the longest x1 15.9 us: shards(): acts = call(activate, block, lax.all_gather(sums, 'xh', axis=0, tiled=True))]
  transfers between devices with their start and end apart: 2 -> 18, of which waited for: 2 -> 16; matrix products, arithmetic and copies ran while one was open for 1% -> 1% of each run, Pallas kernels for 0% -> 0%
where the time goes in v3:
time: 186 us; the launch traced here: 185 us
  starting transfers between devices  90.9 us (49%)
  waiting for transfers between devices  60.4 us (32%)
  blocking collectives  20.1 us (11%)
  local copies, waits for them, and re-layouts  6.47 us (3%)
  Pallas kernels  5.17 us (3%)
    ppermute x16, starting transfers between devices, step(): lax.ppermute(block, axis, [(i, (i + shift) % size) for i in range(size)])  53.8 us
    all_to_all x2, starting transfers between devices, exchange(): return lax.all_to_all(rows, axis, split_axis=0, concat_axis=0, tiled=True)  37.1 us
    ppermute x16, waiting for transfers between devices, step(): lax.ppermute(block, axis, [(i, (i + shift) % size) for i in range(size)])  32.9 us
    all_to_all x2, waiting for transfers between devices, exchange(): return lax.all_to_all(rows, axis, split_axis=0, concat_axis=0, tiled=True)  27.5 us
    all_gather x1, blocking collectives, shards(): acts = call(activate, block, lax.all_gather(sums, 'xh', axis=0, tiled=True))  15.9 us
    unnamed x22, local copies, waits for them, and re-layouts  6.45 us
    pallas_call x9, Pallas kernels, call(): pl.pallas_call(kernel, out_shape=outs, in_specs=[SMEM] * scalars + [VMEM]...  5.17 us
    all_gather x1, blocking collectives, shards(): arrived = lax.all_gather(exchange(send, ETP), 'exp', axis=0, tiled=True)  4.22 us
  transfers between devices with their start and end apart: 18, of which 16 were waited for; matrix products, arithmetic and copies ran while one was open for 1% of the time, Pallas kernels for 0%

profile of v3, /device:TPU:1, one launch (start us, length us, event | category | flops | bytes accessed | tf_op | source)
XLA Modules:
  0.0 185.3 jit_solution(16408409248654105644)
XLA Ops:
  4.8 20.4 %all-to-all-start = ((bf16[32,16,256]{2,1,0:T(8,128)(2,1)}), bf16[32,16,256]{2,1,0:T(8,128)(2,1)S(1)}, u32[]{:S(2)}, u32[]{:S(2)}) async-start(bf16[32,16,256]{2,1,0:T(8,128)(2,1)} %bitcast.4), calls=%async_computation | async-start | bytes 524288 | tf_op jit(solution)/shard_map/all_to_all | solution.py:182
  25.2 11.2 %all-to-all-done = bf16[32,16,256]{2,1,0:T(8,128)(2,1)S(1)} async-done(((bf16[32,16,256]{2,1,0:T(8,128)(2,1)}), bf16[32,16,256]{2,1,0:T(8,128)(2,1)S(1)}, u32[]{:S(2)}, u32[]{:S(2)}) %all-to-all-start) | async-done | bytes 262176 | tf_op jit(solution)/shard_map/all_to_all | solution.py:182
  36.4 4.2 %all_gather.6.rows_ref = bf16[1024,256]{1,0:T(8,128)(2,1)S(1)} all-gather(bf16[512,256]{1,0:T(8,128)(2,1)S(1)} %bitcast.14), channel_id=1, replica_groups=mesh['y'=8,'xh'=2,'exp'=2,'z'=8,'xl'=4] {'exp'}, dimensions={0}, use_global_device_ids=true | all-gather | bytes 786432 | tf_op jit(solution)/shard_map/all_gather | solution.py:210
  44.8 3.3 %collective-permute-start = (bf16[32,2304]{1,0:T(8,128)(2,1)S(1)}, bf16[32,2304]{1,0:T(8,128)(2,1)S(1)}, u32[]{:S(2)}, u32[]{:S(2)}) collective-permute-start(bf16[32,2304]{1,0:T(8,128)(2,1)S(1)} %get-tuple-element.22), channel_id=1, source_target_pairs={{0,128},{128,256},{256,384},{384,512},{512,640},{640,768},{768,896... | collective-permute-start | bytes 442376 | tf_op jit(solution)/shard_map/ppermute | solution.py:187
  48.1 4.5 %collective-permute-start.1 = (bf16[32,2304]{1,0:T(8,128)(2,1)S(1)}, bf16[32,2304]{1,0:T(8,128)(2,1)S(1)}, u32[]{:S(2)}, u32[]{:S(2)}) collective-permute-start(bf16[32,2304]{1,0:T(8,128)(2,1)S(1)} %get-tuple-element.23), channel_id=1, source_target_pairs={{0,896},{128,0},{256,128},{384,256},{512,384},{640,512},{768,640},... | collective-permute-start | bytes 442376 | tf_op jit(solution)/shard_map/ppermute | solution.py:187
  52.6 2.0 %collective-permute-done.up_ref = bf16[32,2304]{1,0:T(8,128)(2,1)S(1)} collective-permute-done((bf16[32,2304]{1,0:T(8,128)(2,1)S(1)}, bf16[32,2304]{1,0:T(8,128)(2,1)S(1)}, u32[]{:S(2)}, u32[]{:S(2)}) %collective-permute-start) | collective-permute-done | bytes 147488 | tf_op jit(solution)/shard_map/ppermute | solution.py:187
  55.6 2.6 %collective-permute-start.2 = (bf16[64,2304]{1,0:T(8,128)(2,1)S(1)}, bf16[64,2304]{1,0:T(8,128)(2,1)S(1)}, u32[]{:S(2)}, u32[]{:S(2)}) collective-permute-start(bf16[64,2304]{1,0:T(8,128)(2,1)S(1)} %get-tuple-element.24), channel_id=1, source_target_pairs={{0,128},{128,256},{256,384},{384,512},{512,640},{640,768},{768,896... | collective-permute-start | bytes 884744 | tf_op jit(solution)/shard_map/ppermute | solution.py:187
  58.2 4.6 %collective-permute-start.3 = (bf16[64,2304]{1,0:T(8,128)(2,1)S(1)}, bf16[64,2304]{1,0:T(8,128)(2,1)S(1)}, u32[]{:S(2)}, u32[]{:S(2)}) collective-permute-start(bf16[64,2304]{1,0:T(8,128)(2,1)S(1)} %get-tuple-element.25), channel_id=1, source_target_pairs={{0,896},{128,0},{256,128},{384,256},{512,384},{640,512},{768,640},... | collective-permute-start | bytes 884744 | tf_op jit(solution)/shard_map/ppermute | solution.py:187
  62.8 4.2 %collective-permute-done.2.up_ref = bf16[64,2304]{1,0:T(8,128)(2,1)S(1)} collective-permute-done((bf16[64,2304]{1,0:T(8,128)(2,1)S(1)}, bf16[64,2304]{1,0:T(8,128)(2,1)S(1)}, u32[]{:S(2)}, u32[]{:S(2)}) %collective-permute-start.2) | collective-permute-done | bytes 294944 | tf_op jit(solution)/shard_map/ppermute | solution.py:187
  68.9 3.9 %collective-permute-start.4 = (bf16[64,2304]{1,0:T(8,128)(2,1)S(1)}, bf16[64,2304]{1,0:T(8,128)(2,1)S(1)}, u32[]{:S(2)}, u32[]{:S(2)}) collective-permute-start(bf16[64,2304]{1,0:T(8,128)(2,1)S(1)} %get-tuple-element.26), channel_id=1, source_target_pairs={{0,128},{128,256},{256,384},{384,512},{512,640},{640,768},{768,896... | collective-permute-start | bytes 884744 | tf_op jit(solution)/shard_map/ppermute | solution.py:187
  72.9 2.6 %collective-permute-start.5 = (bf16[64,2304]{1,0:T(8,128)(2,1)S(1)}, bf16[64,2304]{1,0:T(8,128)(2,1)S(1)}, u32[]{:S(2)}, u32[]{:S(2)}) collective-permute-start(bf16[64,2304]{1,0:T(8,128)(2,1)S(1)} %get-tuple-element.27), channel_id=1, source_target_pairs={{0,896},{128,0},{256,128},{384,256},{512,384},{640,512},{768,640},... | collective-permute-start | bytes 884744 | tf_op jit(solution)/shard_map/ppermute | solution.py:187
  75.4 3.0 %collective-permute-done.4.up_ref = bf16[64,2304]{1,0:T(8,128)(2,1)S(1)} collective-permute-done((bf16[64,2304]{1,0:T(8,128)(2,1)S(1)}, bf16[64,2304]{1,0:T(8,128)(2,1)S(1)}, u32[]{:S(2)}, u32[]{:S(2)}) %collective-permute-start.4) | collective-permute-done | bytes 294944 | tf_op jit(solution)/shard_map/ppermute | solution.py:187
  78.4 2.2 %collective-permute-done.5.down_ref = bf16[64,2304]{1,0:T(8,128)(2,1)S(1)} collective-permute-done((bf16[64,2304]{1,0:T(8,128)(2,1)S(1)}, bf16[64,2304]{1,0:T(8,128)(2,1)S(1)}, u32[]{:S(2)}, u32[]{:S(2)}) %collective-permute-start.5) | collective-permute-done | bytes 294944 | tf_op jit(solution)/shard_map/ppermute | solution.py:187
  80.8 3.3 %collective-permute-start.6 = (bf16[64,2304]{1,0:T(8,128)(2,1)S(1)}, bf16[64,2304]{1,0:T(8,128)(2,1)S(1)}, u32[]{:S(2)}, u32[]{:S(2)}) collective-permute-start(bf16[64,2304]{1,0:T(8,128)(2,1)S(1)} %get-tuple-element.28), channel_id=1, source_target_pairs={{0,128},{128,256},{256,384},{384,512},{512,640},{640,768},{768,896... | collective-permute-start | bytes 884744 | tf_op jit(solution)/shard_map/ppermute | solution.py:187
  84.0 3.4 %collective-permute-start.7 = (bf16[64,2304]{1,0:T(8,128)(2,1)S(1)}, bf16[64,2304]{1,0:T(8,128)(2,1)S(1)}, u32[]{:S(2)}, u32[]{:S(2)}) collective-permute-start(bf16[64,2304]{1,0:T(8,128)(2,1)S(1)} %get-tuple-element.29), channel_id=1, source_target_pairs={{0,896},{128,0},{256,128},{384,256},{512,384},{640,512},{768,640},... | collective-permute-start | bytes 884744 | tf_op jit(solution)/shard_map/ppermute | solution.py:187
  87.4 2.2 %collective-permute-done.6.up_ref = bf16[64,2304]{1,0:T(8,128)(2,1)S(1)} collective-permute-done((bf16[64,2304]{1,0:T(8,128)(2,1)S(1)}, bf16[64,2304]{1,0:T(8,128)(2,1)S(1)}, u32[]{:S(2)}, u32[]{:S(2)}) %collective-permute-start.6) | collective-permute-done | bytes 294944 | tf_op jit(solution)/shard_map/ppermute | solution.py:187
  89.6 2.2 %collective-permute-done.7.down_ref = bf16[64,2304]{1,0:T(8,128)(2,1)S(1)} collective-permute-done((bf16[64,2304]{1,0:T(8,128)(2,1)S(1)}, bf16[64,2304]{1,0:T(8,128)(2,1)S(1)}, u32[]{:S(2)}, u32[]{:S(2)}) %collective-permute-start.7) | collective-permute-done | bytes 294944 | tf_op jit(solution)/shard_map/ppermute | solution.py:187
  91.9 15.9 %all_gather.7.pair_ref = bf16[128,2304]{1,0:T(8,128)(2,1)S(1)} all-gather(bf16[64,2304]{1,0:T(8,128)(2,1)S(1)} %shard_map.99), channel_id=1, replica_groups=mesh['y'=8,'xh'=2,'exp'=2,'z'=8,'xl'=4] {'xh'}, dimensions={0}, use_global_device_ids=true | all-gather | bytes 884736 | tf_op jit(solution)/shard_map/all_gather | solution.py:230
  107.9 4.1 %collective-permute-start.9 = (bf16[64,2304]{1,0:T(8,128)(2,1)S(1)}, bf16[64,2304]{1,0:T(8,128)(2,1)S(1)}, u32[]{:S(2)}, u32[]{:S(2)}) collective-permute-start(bf16[64,2304]{1,0:T(8,128)(2,1)S(1)} %shard_map.100.refs_0_), channel_id=1, source_target_pairs={{0,896},{128,0},{256,128},{384,256},{512,384},{640,512},{768,640},... | collective-permute-start | bytes 884744 | tf_op jit(solution)/shard_map/ppermute | solution.py:187
  112.1 3.0 %collective-permute-start.8 = (bf16[64,2304]{1,0:T(8,128)(2,1)S(1)}, bf16[64,2304]{1,0:T(8,128)(2,1)S(1)}, u32[]{:S(2)}, u32[]{:S(2)}) collective-permute-start(bf16[64,2304]{1,0:T(8,128)(2,1)S(1)} %shard_map.100.refs_0_), channel_id=1, source_target_pairs={{0,128},{128,256},{256,384},{384,512},{512,640},{640,768},{768,896... | collective-permute-start | bytes 884744 | tf_op jit(solution)/shard_map/ppermute | solution.py:187
  115.1 2.2 %collective-permute-done.9.refs_2_ = bf16[64,2304]{1,0:T(8,128)(2,1)S(1)} collective-permute-done((bf16[64,2304]{1,0:T(8,128)(2,1)S(1)}, bf16[64,2304]{1,0:T(8,128)(2,1)S(1)}, u32[]{:S(2)}, u32[]{:S(2)}) %collective-permute-start.9) | collective-permute-done | bytes 294944 | tf_op jit(solution)/shard_map/ppermute | solution.py:187
  117.3 3.5 %collective-permute-start.11 = (bf16[64,2304]{1,0:T(8,128)(2,1)S(1)}, bf16[64,2304]{1,0:T(8,128)(2,1)S(1)}, u32[]{:S(2)}, u32[]{:S(2)}) collective-permute-start(bf16[64,2304]{1,0:T(8,128)(2,1)S(1)} %collective-permute-done.9.refs_2_), channel_id=1, source_target_pairs={{0,896},{128,0},{256,128},{384,256},{512,384},{640,512},{768,640},... | collective-permute-start | bytes 884744 | tf_op jit(solution)/shard_map/ppermute | solution.py:187
  120.8 2.2 %collective-permute-start.10 = (bf16[64,2304]{1,0:T(8,128)(2,1)S(1)}, bf16[64,2304]{1,0:T(8,128)(2,1)S(1)}, u32[]{:S(2)}, u32[]{:S(2)}) collective-permute-start(bf16[64,2304]{1,0:T(8,128)(2,1)S(1)} %collective-permute-done.8.refs_1_), channel_id=1, source_target_pairs={{0,128},{128,256},{256,384},{384,512},{512,640},{640,768},{768,896... | collective-permute-start | bytes 884744 | tf_op jit(solution)/shard_map/ppermute | solution.py:187
  122.9 2.5 %collective-permute-done.11.refs_4_ = bf16[64,2304]{1,0:T(8,128)(2,1)S(1)} collective-permute-done((bf16[64,2304]{1,0:T(8,128)(2,1)S(1)}, bf16[64,2304]{1,0:T(8,128)(2,1)S(1)}, u32[]{:S(2)}, u32[]{:S(2)}) %collective-permute-start.11) | collective-permute-done | bytes 294944 | tf_op jit(solution)/shard_map/ppermute | solution.py:187
  125.4 4.0 %collective-permute-start.13 = (bf16[64,2304]{1,0:T(8,128)(2,1)S(1)}, bf16[64,2304]{1,0:T(8,128)(2,1)S(1)}, u32[]{:S(2)}, u32[]{:S(2)}) collective-permute-start(bf16[64,2304]{1,0:T(8,128)(2,1)S(1)} %collective-permute-done.11.refs_4_), channel_id=1, source_target_pairs={{0,896},{128,0},{256,128},{384,256},{512,384},{640,512},{768,640},... | collective-permute-start | bytes 884744 | tf_op jit(solution)/shard_map/ppermute | solution.py:187
  129.5 1.9 %collective-permute-start.12 = (bf16[64,2304]{1,0:T(8,128)(2,1)S(1)}, bf16[64,2304]{1,0:T(8,128)(2,1)S(1)}, u32[]{:S(2)}, u32[]{:S(2)}) collective-permute-start(bf16[64,2304]{1,0:T(8,128)(2,1)S(1)} %collective-permute-done.10.refs_3_), channel_id=1, source_target_pairs={{0,128},{128,256},{256,384},{384,512},{512,640},{640,768},{768,896... | collective-permute-start | bytes 884744 | tf_op jit(solution)/shard_map/ppermute | solution.py:187
  131.4 2.5 %collective-permute-done.13.refs_6_ = bf16[64,2304]{1,0:T(8,128)(2,1)S(1)} collective-permute-done((bf16[64,2304]{1,0:T(8,128)(2,1)S(1)}, bf16[64,2304]{1,0:T(8,128)(2,1)S(1)}, u32[]{:S(2)}, u32[]{:S(2)}) %collective-permute-start.13) | collective-permute-done | bytes 294944 | tf_op jit(solution)/shard_map/ppermute | solution.py:187
  133.9 5.0 %collective-permute-start.15 = (bf16[32,2304]{1,0:T(8,128)(2,1)S(1)}, bf16[32,2304]{1,0:T(8,128)(2,1)S(1)}, u32[]{:S(2)}, u32[]{:S(2)}) collective-permute-start(bf16[32,2304]{1,0:T(8,128)(2,1)S(1)} %slice.9), channel_id=1, source_target_pairs={{0,896},{128,0},{256,128},{384,256},{512,384},{640,512},{768,640},... | collective-permute-start | bytes 442376 | tf_op jit(solution)/shard_map/ppermute | solution.py:187
  139.2 1.9 %collective-permute-start.14 = (bf16[32,2304]{1,0:T(8,128)(2,1)S(1)}, bf16[32,2304]{1,0:T(8,128)(2,1)S(1)}, u32[]{:S(2)}, u32[]{:S(2)}) collective-permute-start(bf16[32,2304]{1,0:T(8,128)(2,1)S(1)} %slice.8), channel_id=1, source_target_pairs={{0,128},{128,256},{256,384},{384,512},{512,640},{640,768},{768,896... | collective-permute-start | bytes 442376 | tf_op jit(solution)/shard_map/ppermute | solution.py:187
  142.6 5.6 %collective-permute-done.14.refs_7_ = bf16[32,2304]{1,0:T(8,128)(2,1)S(1)} collective-permute-done((bf16[32,2304]{1,0:T(8,128)(2,1)S(1)}, bf16[32,2304]{1,0:T(8,128)(2,1)S(1)}, u32[]{:S(2)}, u32[]{:S(2)}) %collective-permute-start.14) | collective-permute-done | bytes 147488 | tf_op jit(solution)/shard_map/ppermute | solution.py:187
  149.9 16.7 %all-to-all-start.1 = ((bf16[64,16,256]{2,1,0:T(8,128)(2,1)}), bf16[64,16,256]{2,1,0:T(8,128)(2,1)S(1)}, u32[]{:S(2)}, u32[]{:S(2)}) async-start(bf16[64,16,256]{2,1,0:T(8,128)(2,1)} %bitcast.6), calls=%async_computation.1 | async-start | bytes 1048576 | tf_op jit(solution)/shard_map/all_to_all | solution.py:182
  168.0 16.3 %all-to-all-done.1 = bf16[64,16,256]{2,1,0:T(8,128)(2,1)S(1)} async-done(((bf16[64,16,256]{2,1,0:T(8,128)(2,1)}), bf16[64,16,256]{2,1,0:T(8,128)(2,1)S(1)}, u32[]{:S(2)}, u32[]{:S(2)}) %all-to-all-start.1) | async-done | bytes 524320 | tf_op jit(solution)/shard_map/all_to_all | solution.py:182
  (40 shorter events, 17.4 us)
Async XLA Ops:
  0.6 0.8 copy-start.6
  1.5 0.8 copy-start.7
  2.3 0.7 copy-start.8
  3.0 0.7 copy-start.10
  4.8 31.6 %all-to-all-start = ((bf16[32,16,256]{2,1,0:T(8,128)(2,1)}), bf16[32,16,256]{2,1,0:T(8,128)(2,1)S(1)}, u32[]{:S(2)}, u32[]{:S(2)}) async-start(bf16[32,16,256]{2,1,0:T(8,128)(2,1)} %bitcast.4), calls=%async_computation | async-start | bytes 524288 | tf_op jit(solution)/shard_map/all_to_all | solution.py:182
  40.6 1.1 copy-start
  41.7 1.1 copy-start.2
  42.9 1.1 copy-start.4
  44.8 9.8 %collective-permute-start = (bf16[32,2304]{1,0:T(8,128)(2,1)S(1)}, bf16[32,2304]{1,0:T(8,128)(2,1)S(1)}, u32[]{:S(2)}, u32[]{:S(2)}) collective-permute-start(bf16[32,2304]{1,0:T(8,128)(2,1)S(1)} %get-tuple-element.22), channel_id=1, source_target_pairs={{0,128},{128,256},{256,384},{384,512},{512,640},{640,768},{768,896... | collective-permute-start | bytes 442376 | tf_op jit(solution)/shard_map/ppermute | solution.py:187
  48.1 7.3 %collective-permute-start.1 = (bf16[32,2304]{1,0:T(8,128)(2,1)S(1)}, bf16[32,2304]{1,0:T(8,128)(2,1)S(1)}, u32[]{:S(2)}, u32[]{:S(2)}) collective-permute-start(bf16[32,2304]{1,0:T(8,128)(2,1)S(1)} %get-tuple-element.23), channel_id=1, source_target_pairs={{0,896},{128,0},{256,128},{384,256},{512,384},{640,512},{768,640},... | collective-permute-start | bytes 442376 | tf_op jit(solution)/shard_map/ppermute | solution.py:187
  55.6 11.4 %collective-permute-start.2 = (bf16[64,2304]{1,0:T(8,128)(2,1)S(1)}, bf16[64,2304]{1,0:T(8,128)(2,1)S(1)}, u32[]{:S(2)}, u32[]{:S(2)}) collective-permute-start(bf16[64,2304]{1,0:T(8,128)(2,1)S(1)} %get-tuple-element.24), channel_id=1, source_target_pairs={{0,128},{128,256},{256,384},{384,512},{512,640},{640,768},{768,896... | collective-permute-start | bytes 884744 | tf_op jit(solution)/shard_map/ppermute | solution.py:187
  58.2 10.6 %collective-permute-start.3 = (bf16[64,2304]{1,0:T(8,128)(2,1)S(1)}, bf16[64,2304]{1,0:T(8,128)(2,1)S(1)}, u32[]{:S(2)}, u32[]{:S(2)}) collective-permute-start(bf16[64,2304]{1,0:T(8,128)(2,1)S(1)} %get-tuple-element.25), channel_id=1, source_target_pairs={{0,896},{128,0},{256,128},{384,256},{512,384},{640,512},{768,640},... | collective-permute-start | bytes 884744 | tf_op jit(solution)/shard_map/ppermute | solution.py:187
  68.9 9.5 %collective-permute-start.4 = (bf16[64,2304]{1,0:T(8,128)(2,1)S(1)}, bf16[64,2304]{1,0:T(8,128)(2,1)S(1)}, u32[]{:S(2)}, u32[]{:S(2)}) collective-permute-start(bf16[64,2304]{1,0:T(8,128)(2,1)S(1)} %get-tuple-element.26), channel_id=1, source_target_pairs={{0,128},{128,256},{256,384},{384,512},{512,640},{640,768},{768,896... | collective-permute-start | bytes 884744 | tf_op jit(solution)/shard_map/ppermute | solution.py:187
  72.9 7.8 %collective-permute-start.5 = (bf16[64,2304]{1,0:T(8,128)(2,1)S(1)}, bf16[64,2304]{1,0:T(8,128)(2,1)S(1)}, u32[]{:S(2)}, u32[]{:S(2)}) collective-permute-start(bf16[64,2304]{1,0:T(8,128)(2,1)S(1)} %get-tuple-element.27), channel_id=1, source_target_pairs={{0,896},{128,0},{256,128},{384,256},{512,384},{640,512},{768,640},... | collective-permute-start | bytes 884744 | tf_op jit(solution)/shard_map/ppermute | solution.py:187
  80.7 67.5 %copy-start.1 = (bf16[2,256,768]{2,1,0:T(8,128)(2,1)S(1)}, bf16[2,256,768]{2,1,0:T(8,128)(2,1)}, u32[]{:S(2)}) copy-start(bf16[2,256,768]{2,1,0:T(8,128)(2,1)} %refs_9_.1) | copy-start | bytes 2359300
  80.8 67.4 %copy-start.3 = (bf16[2,256,768]{2,1,0:T(8,128)(2,1)S(1)}, bf16[2,256,768]{2,1,0:T(8,128)(2,1)}, u32[]{:S(2)}) copy-start(bf16[2,256,768]{2,1,0:T(8,128)(2,1)} %refs_10_.1) | copy-start | bytes 2359300
  80.8 67.4 %copy-start.5 = (bf16[2,768,256]{2,1,0:T(8,128)(2,1)S(1)}, bf16[2,768,256]{2,1,0:T(8,128)(2,1)}, u32[]{:S(2)}) copy-start(bf16[2,768,256]{2,1,0:T(8,128)(2,1)} %refs_11_.1) | copy-start | bytes 2359300
  80.8 8.8 %collective-permute-start.6 = (bf16[64,2304]{1,0:T(8,128)(2,1)S(1)}, bf16[64,2304]{1,0:T(8,128)(2,1)S(1)}, u32[]{:S(2)}, u32[]{:S(2)}) collective-permute-start(bf16[64,2304]{1,0:T(8,128)(2,1)S(1)} %get-tuple-element.28), channel_id=1, source_target_pairs={{0,128},{128,256},{256,384},{384,512},{512,640},{640,768},{768,896... | collective-permute-start | bytes 884744 | tf_op jit(solution)/shard_map/ppermute | solution.py:187
  84.0 7.8 %collective-permute-start.7 = (bf16[64,2304]{1,0:T(8,128)(2,1)S(1)}, bf16[64,2304]{1,0:T(8,128)(2,1)S(1)}, u32[]{:S(2)}, u32[]{:S(2)}) collective-permute-start(bf16[64,2304]{1,0:T(8,128)(2,1)S(1)} %get-tuple-element.29), channel_id=1, source_target_pairs={{0,896},{128,0},{256,128},{384,256},{512,384},{640,512},{768,640},... | collective-permute-start | bytes 884744 | tf_op jit(solution)/shard_map/ppermute | solution.py:187
  107.8 76.5 %copy-start.9 = (f32[128,2]{0,1:T(2,128)S(1)}, f32[128,2]{0,1:T(2,128)}, u32[]{:S(2)}) copy-start(f32[128,2]{0,1:T(2,128)} %param.9) | copy-start | bytes 3076
  107.9 9.3 %collective-permute-start.9 = (bf16[64,2304]{1,0:T(8,128)(2,1)S(1)}, bf16[64,2304]{1,0:T(8,128)(2,1)S(1)}, u32[]{:S(2)}, u32[]{:S(2)}) collective-permute-start(bf16[64,2304]{1,0:T(8,128)(2,1)S(1)} %shard_map.100.refs_0_), channel_id=1, source_target_pairs={{0,896},{128,0},{256,128},{384,256},{512,384},{640,512},{768,640},... | collective-permute-start | bytes 884744 | tf_op jit(solution)/shard_map/ppermute | solution.py:187
  112.1 8.7 %collective-permute-start.8 = (bf16[64,2304]{1,0:T(8,128)(2,1)S(1)}, bf16[64,2304]{1,0:T(8,128)(2,1)S(1)}, u32[]{:S(2)}, u32[]{:S(2)}) collective-permute-start(bf16[64,2304]{1,0:T(8,128)(2,1)S(1)} %shard_map.100.refs_0_), channel_id=1, source_target_pairs={{0,128},{128,256},{256,384},{384,512},{512,640},{640,768},{768,896... | collective-permute-start | bytes 884744 | tf_op jit(solution)/shard_map/ppermute | solution.py:187
  117.3 8.1 %collective-permute-start.11 = (bf16[64,2304]{1,0:T(8,128)(2,1)S(1)}, bf16[64,2304]{1,0:T(8,128)(2,1)S(1)}, u32[]{:S(2)}, u32[]{:S(2)}) collective-permute-start(bf16[64,2304]{1,0:T(8,128)(2,1)S(1)} %collective-permute-done.9.refs_2_), channel_id=1, source_target_pairs={{0,896},{128,0},{256,128},{384,256},{512,384},{640,512},{768,640},... | collective-permute-start | bytes 884744 | tf_op jit(solution)/shard_map/ppermute | solution.py:187
  120.8 8.7 %collective-permute-start.10 = (bf16[64,2304]{1,0:T(8,128)(2,1)S(1)}, bf16[64,2304]{1,0:T(8,128)(2,1)S(1)}, u32[]{:S(2)}, u32[]{:S(2)}) collective-permute-start(bf16[64,2304]{1,0:T(8,128)(2,1)S(1)} %collective-permute-done.8.refs_1_), channel_id=1, source_target_pairs={{0,128},{128,256},{256,384},{384,512},{512,640},{640,768},{768,896... | collective-permute-start | bytes 884744 | tf_op jit(solution)/shard_map/ppermute | solution.py:187
  125.4 8.5 %collective-permute-start.13 = (bf16[64,2304]{1,0:T(8,128)(2,1)S(1)}, bf16[64,2304]{1,0:T(8,128)(2,1)S(1)}, u32[]{:S(2)}, u32[]{:S(2)}) collective-permute-start(bf16[64,2304]{1,0:T(8,128)(2,1)S(1)} %collective-permute-done.11.refs_4_), channel_id=1, source_target_pairs={{0,896},{128,0},{256,128},{384,256},{512,384},{640,512},{768,640},... | collective-permute-start | bytes 884744 | tf_op jit(solution)/shard_map/ppermute | solution.py:187
  129.5 9.8 %collective-permute-start.12 = (bf16[64,2304]{1,0:T(8,128)(2,1)S(1)}, bf16[64,2304]{1,0:T(8,128)(2,1)S(1)}, u32[]{:S(2)}, u32[]{:S(2)}) collective-permute-start(bf16[64,2304]{1,0:T(8,128)(2,1)S(1)} %collective-permute-done.10.refs_3_), channel_id=1, source_target_pairs={{0,128},{128,256},{256,384},{384,512},{512,640},{640,768},{768,896... | collective-permute-start | bytes 884744 | tf_op jit(solution)/shard_map/ppermute | solution.py:187
  133.9 8.7 %collective-permute-start.15 = (bf16[32,2304]{1,0:T(8,128)(2,1)S(1)}, bf16[32,2304]{1,0:T(8,128)(2,1)S(1)}, u32[]{:S(2)}, u32[]{:S(2)}) collective-permute-start(bf16[32,2304]{1,0:T(8,128)(2,1)S(1)} %slice.9), channel_id=1, source_target_pairs={{0,896},{128,0},{256,128},{384,256},{512,384},{640,512},{768,640},... | collective-permute-start | bytes 442376 | tf_op jit(solution)/shard_map/ppermute | solution.py:187
  139.2 9.0 %collective-permute-start.14 = (bf16[32,2304]{1,0:T(8,128)(2,1)S(1)}, bf16[32,2304]{1,0:T(8,128)(2,1)S(1)}, u32[]{:S(2)}, u32[]{:S(2)}) collective-permute-start(bf16[32,2304]{1,0:T(8,128)(2,1)S(1)} %slice.8), channel_id=1, source_target_pairs={{0,128},{128,256},{256,384},{384,512},{512,640},{640,768},{768,896... | collective-permute-start | bytes 442376 | tf_op jit(solution)/shard_map/ppermute | solution.py:187
  149.9 34.3 %all-to-all-start.1 = ((bf16[64,16,256]{2,1,0:T(8,128)(2,1)}), bf16[64,16,256]{2,1,0:T(8,128)(2,1)S(1)}, u32[]{:S(2)}, u32[]{:S(2)}) async-start(bf16[64,16,256]{2,1,0:T(8,128)(2,1)} %bitcast.6), calls=%async_computation.1 | async-start | bytes 1048576 | tf_op jit(solution)/shard_map/all_to_all | solution.py:182

commit v4 on v3

v4 whole, which is shorter than its diff:
```python
import functools

import jax
import jax.numpy as jnp
from jax import lax
from jax.experimental import pallas as pl
from jax.experimental.pallas import tpu as pltpu
from jax.sharding import Mesh, PartitionSpec as P

BF = jnp.bfloat16
F32 = jnp.float32
ETP = ("z", "xl")
CAPACITY = 8
VMEM = pl.BlockSpec(memory_space=pltpu.VMEM)
SMEM = pl.BlockSpec(memory_space=pltpu.SMEM)
LIMIT = pltpu.CompilerParams(vmem_limit_bytes=40 * 1024 * 1024)
NT = (((1,), (1,)), ((), ()))
TN = (((0,), (0,)), ((), ()))


def call(kernel, outs, *args, scalars=0, given=0):
    rest = len(args) - scalars - given
    return pl.pallas_call(
        kernel,
        out_shape=outs,
        in_specs=[SMEM] * scalars + [pl.BlockSpec()] * given + [VMEM] * rest,
        out_specs=jax.tree.map(lambda _: VMEM, outs),
        compiler_params=LIMIT,
    )(*args)


def shape(dims, kind):
    return jax.ShapeDtypeStruct(dims, kind)


def iota(dims, axis):
    return lax.broadcasted_iota(jnp.int32, dims, axis)


def begin(experts, core_ref, member_ref, routes_ref, weights_ref, tokens_ref, cot_ref,
          gate_ref, up_ref, down_ref, send_ref, slot_ref, kept_ref, given_ref):
    local_experts, _, width = gate_ref.shape
    half = width // 2
    for out, member in ((given_ref, 1 - member_ref[0]), (kept_ref, member_ref[0])):
        units = pl.ds(pl.multiple_of(member * half, 128), half)
        for e in range(local_experts):
            out[e, :, :half] = gate_ref[e, :, units]
            out[e, :, half : 2 * half] = up_ref[e, :, units]
            out[e, :, 2 * half :] = down_ref[e, units, :].T
    top_count, tok_rows = routes_ref.shape
    hots = [iota((experts, tok_rows), 0) == routes_ref[k : k + 1, :] for k in range(top_count)]
    both = sum(jnp.where(hot, 1.0, 0.0) for hot in hots)
    earlier = jnp.where(iota((tok_rows, tok_rows), 0) < iota((tok_rows, tok_rows), 1), 1.0, 0.0)
    count = jnp.dot(both.astype(BF), earlier.astype(BF), preferred_element_type=F32)
    placing = jnp.zeros((send_ref.shape[0], tok_rows), F32)
    slot_weight = jnp.zeros((send_ref.shape[0], 1), F32)
    for k, hot in enumerate(hots):
        position = jnp.sum(jnp.where(hot, count, 0.0), axis=0, keepdims=True).astype(jnp.int32)
        slot = routes_ref[k : k + 1, :] * CAPACITY + position
        slot_ref[k : k + 1, :] = slot
        hit = iota(placing.shape, 0) == slot
        placing = placing + jnp.where(hit, 1.0, 0.0)
        slot_weight = slot_weight + jnp.sum(
            jnp.where(hit, weights_ref[k : k + 1, :], 0.0), axis=1, keepdims=True
        )
    first = core_ref[0] == 0
    source = jnp.where(first, tokens_ref[...].astype(F32), cot_ref[...].astype(F32)).astype(BF)
    scale = jnp.where(first, 1.0, slot_weight)
    rows = jnp.dot(placing.astype(BF), source, preferred_element_type=F32)
    send_ref[...] = (rows * scale).astype(BF)


def first_terms(kept_ref, other_ref, rows_ref, other_rows_ref, terms_ref, grad_ref, other_grad_ref):
    local_experts, depth, width = kept_ref.shape
    two = width // 3 * 2
    slots = rows_ref.shape[0] // 2
    count = slots // local_experts
    for e in range(local_experts):
        here = slice(e * count, (e + 1) * count)
        totals = [0.0, 0.0]
        for weights, rows, grads in (
            (kept_ref, rows_ref, grad_ref), (other_ref, other_rows_ref, other_grad_ref)
        ):
            for kind, cols in enumerate((slice(0, two), slice(two, width))):
                picked = rows[kind * slots : (kind + 1) * slots, :].astype(F32)
                picked = picked.reshape(-1, local_experts, CAPACITY, depth)[:, e]
                picked = picked.reshape(count, depth).astype(BF)
                totals[kind] += jnp.dot(picked, weights[e, :, cols], preferred_element_type=F32)
                if kind == 1:
                    grads[e] = picked
        terms_ref[here, :two] = totals[0].astype(BF)
        terms_ref[here, two:] = totals[1].astype(BF)


def activate(terms_ref, out_ref):
    copies, rows, width = out_ref.shape
    width = width // 3

    def total(part):
        cols = slice(part * width, (part + 1) * width)
        return sum(terms_ref[i, :, cols].astype(F32) for i in range(terms_ref.shape[0]))

    gate, up_proj, d_hidden = total(0), total(1), total(2)
    sigmoid_gate = jax.nn.sigmoid(gate)
    silu_gate = gate * sigmoid_gate
    hidden = (silu_gate * up_proj).astype(BF)
    d_gate = (d_hidden * up_proj * sigmoid_gate * (1.0 + gate * (1.0 - sigmoid_gate))).astype(BF)
    d_up = (d_hidden * silu_gate).astype(BF)
    for i in range(copies):
        out_ref[i, :, :width] = hidden
        out_ref[i, :, width : 2 * width] = d_gate
        out_ref[i, :, 2 * width :] = d_up


def last_terms(member_ref, acts_ref, kept_ref, other_ref, parts_ref):
    local_experts, depth, width = kept_ref.shape
    one = width // 3
    count = acts_ref.shape[0] // local_experts
    half = depth // 2
    for weights, member in ((kept_ref, member_ref[0]), (other_ref, 1 - member_ref[0])):
        outs, grads = [], []
        for e in range(local_experts):
            here = slice(e * count, (e + 1) * count)
            out = lax.dot_general(
                acts_ref[here, :one], weights[e, :, 2 * one :], NT, preferred_element_type=F32
            )
            grad = lax.dot_general(
                acts_ref[here, one:], weights[e, :, : 2 * one], NT, preferred_element_type=F32
            )
            outs.append(out.reshape(count // CAPACITY, CAPACITY, depth))
            grads.append(grad.reshape(count // CAPACITY, CAPACITY, depth))
        out, grad = jnp.concatenate(outs, axis=1), jnp.concatenate(grads, axis=1)
        for j in range(2):
            cols = slice(j * half, (j + 1) * half)
            parts_ref[member * 2 + j, :, :, :half] = out[:, :, cols].astype(BF)
            parts_ref[member * 2 + j, :, :, half:] = grad[:, :, cols].astype(BF)


def down_terms(acts_ref, grad_ref, other_grad_ref, out_ref, other_out_ref):
    local_experts, count, _ = grad_ref.shape
    one = out_ref.shape[1]
    for e in range(local_experts):
        hidden = acts_ref[e * count : (e + 1) * count, :one]
        for grads, out in ((grad_ref, out_ref), (other_grad_ref, other_out_ref)):
            out[e] = lax.dot_general(hidden, grads[e], TN, preferred_element_type=F32).astype(BF)


def add_parts(parts_ref, out_ref):
    out_ref[...] = sum(parts_ref[i].astype(F32) for i in range(parts_ref.shape[0])).astype(BF)


def combine(slot_ref, weights_ref, back_ref, mixed_ref, grads_ref):
    top_count, tok_rows = slot_ref.shape
    slots, width = back_ref.shape
    half = width // 2
    same = iota((tok_rows, tok_rows), 0) == iota((tok_rows, tok_rows), 1)

    def column(row):
        return jnp.sum(jnp.where(same, row, 0.0), axis=1, keepdims=True)

    mixed = jnp.zeros((tok_rows, half), F32)
    grads = jnp.zeros((tok_rows, half), F32)
    for k in range(top_count):
        slot = column(slot_ref[k : k + 1, :].astype(F32)).astype(jnp.int32)
        hot = jnp.where(iota((tok_rows, slots), 1) == slot, 1.0, 0.0).astype(BF)
        picked = jnp.dot(hot, back_ref[...], preferred_element_type=F32)
        mixed = mixed + picked[:, :half] * column(weights_ref[k : k + 1, :])
        grads = grads + picked[:, half:]
    mixed_ref[...] = mixed.astype(BF)
    grads_ref[...] = grads.astype(BF)


def exchange(rows, axis):
    return lax.all_to_all(rows, axis, split_axis=0, concat_axis=0, tiled=True)


def swap(block):
    return lax.ppermute(block, "ym", [(0, 1), (1, 0)])


def shards(tokens, routes, route_weights, gate_weight, up_weight, down_weight, cotangent):
    local_experts, depth, width = gate_weight.shape
    groups = lax.axis_size("z") * lax.axis_size("xl")
    experts = groups * local_experts
    tok_rows, top_count = routes.shape
    slots = experts * CAPACITY
    count = groups * CAPACITY
    half = width // 2
    slices = lax.axis_size("yp") * lax.axis_size("xh")
    core = lax.axis_index("exp").reshape(1)
    member = lax.axis_index("ym").reshape(1)
    routes, route_weights = routes.T, route_weights.T

    weights = shape((local_experts, depth, 3 * half), BF)
    send, slot_index, kept, given = call(
        functools.partial(begin, experts),
        (shape((slots, depth), BF), shape((top_count, tok_rows), jnp.int32), weights, weights),
        core, member, routes, route_weights, tokens, cotangent, gate_weight, up_weight,
        down_weight, scalars=2, given=7,
    )
    other = swap(given)
    arrived = exchange(send, ETP)
    other_arrived = swap(arrived)
    rows = lax.all_gather(arrived, "exp", axis=0, tiled=True)
    other_rows = lax.all_gather(other_arrived, "exp", axis=0, tiled=True)

    grads = shape((local_experts, count, depth), BF)
    terms, expert_grad, other_grad = call(
        first_terms, (shape((slots, 3 * half), BF), grads, grads), kept, other, rows, other_rows
    )
    terms = exchange(terms, ("yp", "xh")).reshape(slices, slots // slices, 3 * half)
    acts = call(activate, shape(terms.shape, BF), terms)
    acts = exchange(acts.reshape(slots, 3 * half), ("yp", "xh"))

    parts = call(
        last_terms, shape((4, groups, local_experts * CAPACITY, depth), BF),
        member, acts, kept, other, scalars=1,
    )
    parts = exchange(parts.reshape(4 * slots, depth), ("ym", "exp")).reshape(4, slots, depth)
    slot_sums = call(add_parts, shape((slots, depth), BF), parts)
    back = exchange(slot_sums, ETP)
    downs = shape((local_experts, half, depth), BF)
    d_down, other_down = call(down_terms, (downs, downs), acts, expert_grad, other_grad)
    other_down = swap(other_down)
    first = member[0] == 0
    d_down = jnp.concatenate(
        [jnp.where(first, d_down, other_down), jnp.where(first, other_down, d_down)], axis=1
    )
    mixed, d_tokens = call(
        combine,
        (shape((tok_rows, depth // 2), BF), shape((tok_rows, depth // 2), BF)),
        slot_index, route_weights, back,
    )
    return mixed, d_tokens, d_down


def solution(mesh):
    fine = Mesh(mesh.devices.reshape(4, 2, 2, 2, 8, 4), ("yp", "ym", "xh", "exp", "z", "xl"))
    dp = ("yp", "ym", "xh")
    in_specs = (
        P(ETP, dp),
        P(ETP, None),
        P(ETP, None),
        P(ETP, dp, "exp"),
        P(ETP, dp, "exp"),
        P(ETP, "exp", dp),
        P(ETP, dp),
    )
    out_specs = (P(ETP, dp + ("exp",)), P(ETP, dp + ("exp",)), P(ETP, "exp", dp))
    return jax.shard_map(shards, mesh=fine, in_specs=in_specs, out_specs=out_specs, check_vma=False)
```

time: 186 us -> 184 us (0.989)
  blocking collectives: 20.1 us -> 116 us
  starting transfers between devices: 90.9 us -> 32.6 us
  waiting for transfers between devices: 60.4 us -> 20.2 us
    all_to_all x0 -> x3, blocking collectives: none -> 106 us  [exchange(): return lax.all_to_all(rows, axis, split_axis=0, concat_axis=0, tiled=True)]
    ppermute x16 -> x3, starting transfers between devices: 53.8 us -> 9.4 us  [swap(): return lax.ppermute(block, 'ym', [(0, 1), (1, 0)])]
    ppermute x16 -> x3, waiting for transfers between devices: 32.9 us -> 0.41 us  [swap(): return lax.ppermute(block, 'ym', [(0, 1), (1, 0)])]
    all_to_all x2, starting transfers between devices: 37.1 us -> 23.2 us  [exchange(): return lax.all_to_all(rows, axis, split_axis=0, concat_axis=0, tiled=True)]
    all_gather x2, blocking collectives: 20.1 us -> 10.3 us  [the longest x1 5.59 us: shards(): other_rows = lax.all_gather(other_arrived, 'exp', axis=0, tiled=True)]
    all_to_all x2, waiting for transfers between devices: 27.5 us -> 19.8 us  [exchange(): return lax.all_to_all(rows, axis, split_axis=0, concat_axis=0, tiled=True)]
    pallas_call x9 -> x7, Pallas kernels: 5.17 us -> 5.73 us  [call(): pl.pallas_call(kernel, out_shape=outs, in_specs=[SMEM] * scalars + [pl.Bl...]
    unnamed x22 -> x16, local copies, waits for them, and re-layouts: 6.45 us -> 6.43 us
  transfers between devices with their start and end apart: 18 -> 5, of which waited for: 16 -> 3; matrix products, arithmetic and copies ran while one was open for 1% -> 1% of each run, Pallas kernels for 0% -> 1%
where the time goes in v4:
time: 184 us; the launch traced here: 183 us
  blocking collectives  116 us (63%)
  starting transfers between devices  32.6 us (18%)
  waiting for transfers between devices  20.2 us (11%)
  local copies, waits for them, and re-layouts  6.43 us (3%)
  Pallas kernels  5.73 us (3%)
    all_to_all x3, blocking collectives, exchange(): return lax.all_to_all(rows, axis, split_axis=0, concat_axis=0, tiled=True)  106 us
    all_to_all x2, starting transfers between devices, exchange(): return lax.all_to_all(rows, axis, split_axis=0, concat_axis=0, tiled=True)  23.2 us
    all_to_all x2, waiting for transfers between devices, exchange(): return lax.all_to_all(rows, axis, split_axis=0, concat_axis=0, tiled=True)  19.8 us
    ppermute x3, starting transfers between devices, swap(): return lax.ppermute(block, 'ym', [(0, 1), (1, 0)])  9.4 us
    unnamed x16, local copies, waits for them, and re-layouts  6.43 us
    pallas_call x7, Pallas kernels, call(): pl.pallas_call(kernel, out_shape=outs, in_specs=[SMEM] * scalars + [pl.Bl...  5.73 us
    all_gather x1, blocking collectives, shards(): other_rows = lax.all_gather(other_arrived, 'exp', axis=0, tiled=True)  5.59 us
    all_gather x1, blocking collectives, shards(): rows = lax.all_gather(arrived, 'exp', axis=0, tiled=True)  4.74 us
  transfers between devices with their start and end apart: 5, of which 3 were waited for; matrix products, arithmetic and copies ran while one was open for 1% of the time, Pallas kernels for 1%

profile of v4, /device:TPU:1, one launch (start us, length us, event | category | flops | bytes accessed | tf_op | source)
XLA Modules:
  0.0 183.3 jit_solution(702959127451458811)
XLA Ops:
  0.6 1.1 copy-done
  1.8 1.1 copy-done.1
  2.9 1.1 copy-done.2
  4.0 0.8 copy-done.3
  4.9 0.8 copy-done.4
  5.7 0.7 copy-done.5
  6.4 0.7 copy-done.7
  7.1 0.6 shard_map.94
  7.7 4.1 %collective-permute-start = (bf16[2,256,1152]{2,1,0:T(8,128)(2,1)S(1)}, bf16[2,256,1152]{2,1,0:T(8,128)(2,1)S(1)}, u32[]{:S(2)}, u32[]{:S(2)}) collective-permute-start(bf16[2,256,1152]{2,1,0:T(8,128)(2,1)S(1)} %get-tuple-element.16), channel_id=1, source_target_pairs={{0,128},{128,0},{1,129},{129,1},{2,130},{130,2},{3,131},{131,3},{4... | collective-permute-start | bytes 3538952 | tf_op jit(solution)/shard_map/ppermute | solution.py:178
  11.8 30.3 %all_to_all.49 = bf16[32,16,256]{2,1,0:T(8,128)(2,1)S(1)} all-to-all(bf16[32,16,256]{2,1,0:T(8,128)(2,1)S(1)} %bitcast.15), channel_id=1, replica_groups=mesh['yp'=4,'ym'=2,'xh'=2,'exp'=2,'z'=8,'xl'=4] {'z','xl'}, dimensions={0} | all-to-all | bytes 524288 | tf_op jit(solution)/shard_map/all_to_all | solution.py:174
  42.2 2.0 %collective-permute-start.1 = (bf16[512,256]{1,0:T(8,128)(2,1)S(1)}, bf16[512,256]{1,0:T(8,128)(2,1)S(1)}, u32[]{:S(2)}, u32[]{:S(2)}) collective-permute-start(bf16[512,256]{1,0:T(8,128)(2,1)S(1)} %bitcast.19), channel_id=1, source_target_pairs={{0,128},{128,0},{1,129},{129,1},{2,130},{130,2},{3,131},{131,3},{4... | collective-permute-start | bytes 786440 | tf_op jit(solution)/shard_map/ppermute | solution.py:178
  44.1 4.7 %all_gather.6.rows_ref = bf16[1024,256]{1,0:T(8,128)(2,1)S(1)} all-gather(bf16[512,256]{1,0:T(8,128)(2,1)S(1)} %bitcast.20), channel_id=1, replica_groups=mesh['yp'=4,'ym'=2,'xh'=2,'exp'=2,'z'=8,'xl'=4] {'exp'}, dimensions={0}, use_global_device_ids=true | all-gather | bytes 786432 | tf_op jit(solution)/shard_map/all_gather | solution.py:204
  48.9 0.4 collective-permute-done.1
  49.3 5.6 %all_gather.7.other_rows_ref = bf16[1024,256]{1,0:T(8,128)(2,1)S(1)} all-gather(bf16[512,256]{1,0:T(8,128)(2,1)S(1)} %collective-permute-done.1), channel_id=1, replica_groups=mesh['yp'=4,'ym'=2,'xh'=2,'exp'=2,'z'=8,'xl'=4] {'exp'}, dimensions={0}, use_global_device_ids=true | all-gather | bytes 786432 | tf_op jit(solution)/shard_map/all_gather | solution.py:205
  54.9 0.0 collective-permute-done.other_ref
  54.9 0.9 shard_map.95
  55.7 36.7 %all_to_all.50.terms_ref = bf16[8,64,1152]{2,1,0:T(8,128)(2,1)S(1)} all-to-all(bf16[8,64,1152]{2,1,0:T(8,128)(2,1)S(1)} %bitcast.13), channel_id=1, replica_groups=mesh['yp'=4,'ym'=2,'xh'=2,'exp'=2,'z'=8,'xl'=4] {'yp','xh'}, dimensions={0} | all-to-all | bytes 2359296 | tf_op jit(solution)/shard_map/all_to_all | solution.py:174
  92.5 0.3 shard_map.96
  92.8 39.1 %all_to_all.51 = bf16[8,64,1152]{2,1,0:T(8,128)(2,1)S(1)} all-to-all(bf16[8,64,1152]{2,1,0:T(8,128)(2,1)S(1)} %shard_map.96), channel_id=1, replica_groups=mesh['yp'=4,'ym'=2,'xh'=2,'exp'=2,'z'=8,'xl'=4] {'yp','xh'}, dimensions={0} | all-to-all | bytes 2359296 | tf_op jit(solution)/shard_map/all_to_all | solution.py:174
  131.8 1.9 %shard_map.97 = bf16[4,32,16,256]{3,2,1,0:T(8,128)(2,1)} custom-call(s32[1]{0:T(128)} %bitcast.1.member_ref, bf16[512,1152]{1,0:T(8,128)(2,1)S(1)} %bitcast.11, bf16[2,256,1152]{2,1,0:T(8,128)(2,1)S(1)} %get-tuple-element.15.kept_ref, bf16[2,256,1152]{2,1,0:T(8,128)(2,1)S(1)} %collective-permute-done.other_ref), custom_call_target="tpu_custom_call" | custom-call | tf_op jit(solution)/shard_map/pallas_call | solution.py:23
  133.7 5.5 %all-to-all-start.3 = ((bf16[4,512,256]{2,1,0:T(8,128)(2,1)}), bf16[4,512,256]{2,1,0:T(8,128)(2,1)S(1)}, u32[]{:S(2)}, u32[]{:S(2)}) async-start(bf16[4,512,256]{2,1,0:T(8,128)(2,1)} %bitcast.8), calls=%async_computation.3 | async-start | bytes 2097152 | tf_op jit(solution)/shard_map/all_to_all | solution.py:174
  139.2 0.4 shard_map.100
  139.6 3.3 %collective-permute-start.2 = (bf16[2,384,256]{2,1,0:T(8,128)(2,1)S(1)}, bf16[2,384,256]{2,1,0:T(8,128)(2,1)S(1)}, u32[]{:S(2)}, u32[]{:S(2)}) collective-permute-start(bf16[2,384,256]{2,1,0:T(8,128)(2,1)S(1)} %get-tuple-element.24), channel_id=1, source_target_pairs={{0,128},{128,0},{1,129},{129,1},{2,130},{130,2},{3,131},{131,3},{4... | collective-permute-start | bytes 1179656 | tf_op jit(solution)/shard_map/ppermute | solution.py:178
  142.9 9.9 %all-to-all-done.3.parts_ref = bf16[4,512,256]{2,1,0:T(8,128)(2,1)S(1)} async-done(((bf16[4,512,256]{2,1,0:T(8,128)(2,1)}), bf16[4,512,256]{2,1,0:T(8,128)(2,1)S(1)}, u32[]{:S(2)}, u32[]{:S(2)}) %all-to-all-start.3) | async-done | bytes 1048608 | tf_op jit(solution)/shard_map/all_to_all | solution.py:174
  152.8 0.8 shard_map.98
  153.6 17.8 %all-to-all-start.4 = ((bf16[32,16,256]{2,1,0:T(8,128)(2,1)}), bf16[32,16,256]{2,1,0:T(8,128)(2,1)S(1)}, u32[]{:S(2)}, u32[]{:S(2)}) async-start(bf16[32,16,256]{2,1,0:T(8,128)(2,1)} %bitcast.9), calls=%async_computation.4 | async-start | bytes 524288 | tf_op jit(solution)/shard_map/all_to_all | solution.py:174
  171.4 0.0 collective-permute-done.2
  171.4 0.1 broadcast_select_fusion.1
  171.5 0.0 copy-start.6
  171.5 0.9 pad_maximum_fusion
  172.5 9.9 %all-to-all-done.4 = bf16[32,16,256]{2,1,0:T(8,128)(2,1)S(1)} async-done(((bf16[32,16,256]{2,1,0:T(8,128)(2,1)}), bf16[32,16,256]{2,1,0:T(8,128)(2,1)S(1)}, u32[]{:S(2)}, u32[]{:S(2)}) %all-to-all-start.4) | async-done | bytes 262176 | tf_op jit(solution)/shard_map/all_to_all | solution.py:174
  182.3 0.9 shard_map.99
  (8 shorter events, 0.0 us)
Async XLA Ops:
  0.6 1.1 copy-start
  1.8 1.1 copy-start.1
  2.9 1.1 copy-start.2
  4.0 0.8 copy-start.3
  4.9 0.8 copy-start.4
  5.7 0.7 copy-start.5
  6.4 0.7 copy-start.7
  7.7 47.2 %collective-permute-start = (bf16[2,256,1152]{2,1,0:T(8,128)(2,1)S(1)}, bf16[2,256,1152]{2,1,0:T(8,128)(2,1)S(1)}, u32[]{:S(2)}, u32[]{:S(2)}) collective-permute-start(bf16[2,256,1152]{2,1,0:T(8,128)(2,1)S(1)} %get-tuple-element.16), channel_id=1, source_target_pairs={{0,128},{128,0},{1,129},{129,1},{2,130},{130,2},{3,131},{131,3},{4... | collective-permute-start | bytes 3538952 | tf_op jit(solution)/shard_map/ppermute | solution.py:178
  42.2 7.1 %collective-permute-start.1 = (bf16[512,256]{1,0:T(8,128)(2,1)S(1)}, bf16[512,256]{1,0:T(8,128)(2,1)S(1)}, u32[]{:S(2)}, u32[]{:S(2)}) collective-permute-start(bf16[512,256]{1,0:T(8,128)(2,1)S(1)} %bitcast.19), channel_id=1, source_target_pairs={{0,128},{128,0},{1,129},{129,1},{2,130},{130,2},{3,131},{131,3},{4... | collective-permute-start | bytes 786440 | tf_op jit(solution)/shard_map/ppermute | solution.py:178
  133.7 19.1 %all-to-all-start.3 = ((bf16[4,512,256]{2,1,0:T(8,128)(2,1)}), bf16[4,512,256]{2,1,0:T(8,128)(2,1)S(1)}, u32[]{:S(2)}, u32[]{:S(2)}) async-start(bf16[4,512,256]{2,1,0:T(8,128)(2,1)} %bitcast.8), calls=%async_computation.3 | async-start | bytes 2097152 | tf_op jit(solution)/shard_map/all_to_all | solution.py:174
  139.6 31.8 %collective-permute-start.2 = (bf16[2,384,256]{2,1,0:T(8,128)(2,1)S(1)}, bf16[2,384,256]{2,1,0:T(8,128)(2,1)S(1)}, u32[]{:S(2)}, u32[]{:S(2)}) collective-permute-start(bf16[2,384,256]{2,1,0:T(8,128)(2,1)S(1)} %get-tuple-element.24), channel_id=1, source_target_pairs={{0,128},{128,0},{1,129},{129,1},{2,130},{130,2},{3,131},{131,3},{4... | collective-permute-start | bytes 1179656 | tf_op jit(solution)/shard_map/ppermute | solution.py:178
  153.6 28.7 %all-to-all-start.4 = ((bf16[32,16,256]{2,1,0:T(8,128)(2,1)}), bf16[32,16,256]{2,1,0:T(8,128)(2,1)S(1)}, u32[]{:S(2)}, u32[]{:S(2)}) async-start(bf16[32,16,256]{2,1,0:T(8,128)(2,1)} %bitcast.9), calls=%async_computation.4 | async-start | bytes 524288 | tf_op jit(solution)/shard_map/all_to_all | solution.py:174
  171.5 10.8 %copy-start.6 = (f32[128,2]{0,1:T(2,128)S(1)}, f32[128,2]{0,1:T(2,128)}, u32[]{:S(2)}) copy-start(f32[128,2]{0,1:T(2,128)} %param.9) | copy-start | bytes 3076

commit v5 on v4

--- a/solution.py
+++ b/solution.py
@@ -13,19 +13,21 @@
 CAPACITY = 8
 VMEM = pl.BlockSpec(memory_space=pltpu.VMEM)
 SMEM = pl.BlockSpec(memory_space=pltpu.SMEM)
+HBM = pl.BlockSpec(memory_space=pltpu.HBM)
 LIMIT = pltpu.CompilerParams(vmem_limit_bytes=40 * 1024 * 1024)
 NT = (((1,), (1,)), ((), ()))
 TN = (((0,), (0,)), ((), ()))
 
 
-def call(kernel, outs, *args, scalars=0, given=0):
+def call(kernel, outs, *args, scalars=0, given=0, scratch=()):
     rest = len(args) - scalars - given
     return pl.pallas_call(
         kernel,
         out_shape=outs,
-        in_specs=[SMEM] * scalars + [pl.BlockSpec()] * given + [VMEM] * rest,
+        in_specs=[SMEM] * scalars + [HBM] * given + [VMEM] * rest,
         out_specs=jax.tree.map(lambda _: VMEM, outs),
-        compiler_params=LIMIT,
+        scratch_shapes=scratch,
+        compiler_params=pltpu.CompilerParams(vmem_limit_bytes=(56 if given else 40) * 1024 * 1024),
     )(*args)
 
 
@@ -37,16 +39,47 @@
     return lax.broadcasted_iota(jnp.int32, dims, axis)
 
 
-def begin(experts, core_ref, member_ref, routes_ref, weights_ref, tokens_ref, cot_ref,
-          gate_ref, up_ref, down_ref, send_ref, slot_ref, kept_ref, given_ref):
-    local_experts, _, width = gate_ref.shape
-    half = width // 2
-    for out, member in ((given_ref, 1 - member_ref[0]), (kept_ref, member_ref[0])):
+def pack(member_ref, gate_hbm, up_hbm, down_hbm, kept_ref, given_ref, down, sems):
+    local_experts, _, width = kept_ref.shape
+    half = width // 3
+    copies = [pltpu.make_async_copy(down_hbm, down, sems.at[0])]
+    sides = ((given_ref, 1 - member_ref[0]), (kept_ref, member_ref[0]))
+    for i, (out, member) in enumerate(sides):
+        units = pl.ds(pl.multiple_of(member * half, 128), half)
+        for j, weights in enumerate((gate_hbm, up_hbm)):
+            copies.append(
+                pltpu.make_async_copy(
+                    weights.at[:, :, units],
+                    out.at[:, :, j * half : (j + 1) * half],
+                    sems.at[1 + 2 * i + j],
+                )
+            )
+    for copy in copies:
+        copy.start()
+    copies[0].wait()
+    for out, member in sides:
         units = pl.ds(pl.multiple_of(member * half, 128), half)
         for e in range(local_experts):
-            out[e, :, :half] = gate_ref[e, :, units]
-            out[e, :, half : 2 * half] = up_ref[e, :, units]
-            out[e, :, 2 * half :] = down_ref[e, units, :].T
+            out[e, :, 2 * half :] = down[e, units, :].T
+    for copy in copies[1:]:
+        copy.wait()
+
+
+def place_rows(experts, core_ref, routes_hbm, weights_hbm, tokens_hbm, cot_hbm, send_ref, slot_ref,
+               routes_ref, weights_ref, tokens_ref, cot_ref, sems):
+    copies = [
+        pltpu.make_async_copy(source, target, sems.at[i])
+        for i, (source, target) in enumerate(
+            (
+                (routes_hbm, routes_ref), (weights_hbm, weights_ref),
+                (tokens_hbm, tokens_ref), (cot_hbm, cot_ref),
+            )
+        )
+    ]
+    for copy in copies:
+        copy.start()
+    for copy in copies[:2]:
+        copy.wait()
     top_count, tok_rows = routes_ref.shape
     hots = [iota((experts, tok_rows), 0) == routes_ref[k : k + 1, :] for k in range(top_count)]
     both = sum(jnp.where(hot, 1.0, 0.0) for hot in hots)
@@ -63,6 +96,8 @@
         slot_weight = slot_weight + jnp.sum(
             jnp.where(hit, weights_ref[k : k + 1, :], 0.0), axis=1, keepdims=True
         )
+    for copy in copies[2:]:
+        copy.wait()
     first = core_ref[0] == 0
     source = jnp.where(first, tokens_ref[...].astype(F32), cot_ref[...].astype(F32)).astype(BF)
     scale = jnp.where(first, 1.0, slot_weight)
@@ -132,8 +167,8 @@
         out, grad = jnp.concatenate(outs, axis=1), jnp.concatenate(grads, axis=1)
         for j in range(2):
             cols = slice(j * half, (j + 1) * half)
-            parts_ref[member * 2 + j, :, :, :half] = out[:, :, cols].astype(BF)
-            parts_ref[member * 2 + j, :, :, half:] = grad[:, :, cols].astype(BF)
+            parts_ref[2 * j + member, :, :, :half] = out[:, :, cols].astype(BF)
+            parts_ref[2 * j + member, :, :, half:] = grad[:, :, cols].astype(BF)
 
 
 def down_terms(acts_ref, grad_ref, other_grad_ref, out_ref, other_out_ref):
@@ -151,7 +186,7 @@
 
 def combine(slot_ref, weights_ref, back_ref, mixed_ref, grads_ref):
     top_count, tok_rows = slot_ref.shape
-    slots, width = back_ref.shape
+    slots, width = back_ref.shape[0] // 2, back_ref.shape[1]
     half = width // 2
     same = iota((tok_rows, tok_rows), 0) == iota((tok_rows, tok_rows), 1)
 
@@ -163,7 +198,9 @@
     for k in range(top_count):
         slot = column(slot_ref[k : k + 1, :].astype(F32)).astype(jnp.int32)
         hot = jnp.where(iota((tok_rows, slots), 1) == slot, 1.0, 0.0).astype(BF)
-        picked = jnp.dot(hot, back_ref[...], preferred_element_type=F32)
+        picked = jnp.dot(hot, back_ref[:slots, :], preferred_element_type=F32) + jnp.dot(
+            hot, back_ref[slots:, :], preferred_element_type=F32
+        )
         mixed = mixed + picked[:, :half] * column(weights_ref[k : k + 1, :])
         grads = grads + picked[:, half:]
     mixed_ref[...] = mixed.astype(BF)
@@ -192,11 +229,19 @@
     routes, route_weights = routes.T, route_weights.T
 
     weights = shape((local_experts, depth, 3 * half), BF)
-    send, slot_index, kept, given = call(
-        functools.partial(begin, experts),
-        (shape((slots, depth), BF), shape((top_count, tok_rows), jnp.int32), weights, weights),
-        core, member, routes, route_weights, tokens, cotangent, gate_weight, up_weight,
-        down_weight, scalars=2, given=7,
+    kept, given = call(
+        pack, (weights, weights), member, gate_weight, up_weight, down_weight, scalars=1, given=3,
+        scratch=[pltpu.VMEM(down_weight.shape, BF), pltpu.SemaphoreType.DMA((5,))],
+    )
+    send, slot_index = call(
+        functools.partial(place_rows, experts),
+        (shape((slots, depth), BF), shape((top_count, tok_rows), jnp.int32)),
+        core, routes, route_weights, tokens, cotangent, scalars=1, given=4,
+        scratch=[
+            pltpu.VMEM(routes.shape, jnp.int32), pltpu.VMEM(routes.shape, F32),
+            pltpu.VMEM(tokens.shape, BF), pltpu.VMEM(tokens.shape, BF),
+            pltpu.SemaphoreType.DMA((4,)),
+        ],
     )
     other = swap(given)
     arrived = exchange(send, ETP)
@@ -216,9 +261,9 @@
         last_terms, shape((4, groups, local_experts * CAPACITY, depth), BF),
         member, acts, kept, other, scalars=1,
     )
-    parts = exchange(parts.reshape(4 * slots, depth), ("ym", "exp")).reshape(4, slots, depth)
-    slot_sums = call(add_parts, shape((slots, depth), BF), parts)
-    back = exchange(slot_sums, ETP)
+    parts = exchange(parts.reshape(4 * slots, depth), "exp").reshape(2, 2 * slots, depth)
+    slot_sums = call(add_parts, shape((2 * slots, depth), BF), parts)
+    back = exchange(slot_sums, ("ym",) + ETP)
     downs = shape((local_experts, half, depth), BF)
     d_down, other_down = call(down_terms, (downs, downs), acts, expert_grad, other_grad)
     other_down = swap(other_down)

time: 184 us -> 174 us (0.946)
  waiting for transfers between devices: 20.2 us -> 13 us
  blocking collectives: 116 us -> 123 us
  starting transfers between devices: 32.6 us -> 26 us
  local copies, waits for them, and re-layouts: 6.43 us -> 0.03 us
  Pallas kernels: 5.73 us -> 9.44 us
    all_to_all x2 -> x1, waiting for transfers between devices: 19.8 us -> 0.01 us  [exchange(): return lax.all_to_all(rows, axis, split_axis=0, concat_axis=0, tiled=True)]
    ppermute x3, waiting for transfers between devices: 0.41 us -> 13 us  [swap(): return lax.ppermute(block, 'ym', [(0, 1), (1, 0)])]
    all_to_all x2 -> x1, starting transfers between devices: 23.2 us -> 16.8 us  [exchange(): return lax.all_to_all(rows, axis, split_axis=0, concat_axis=0, tiled=True)]
    all_to_all x3 -> x4, blocking collectives: 106 us -> 113 us  [exchange(): return lax.all_to_all(rows, axis, split_axis=0, concat_axis=0, tiled=True)]
    unnamed x16 -> x14, local copies, waits for them, and re-layouts: 6.43 us -> 0.03 us
    pallas_call x7 -> x8, Pallas kernels: 5.73 us -> 9.44 us  [call(): pl.pallas_call(kernel, out_shape=outs, in_specs=[SMEM] * scalars + [HBM]...]
  transfers between devices with their start and end apart: 5 -> 4, of which waited for: 3 -> 2; matrix products, arithmetic and copies ran while one was open for 1% -> 1% of each run, Pallas kernels for 1% -> 1%
where the time goes in v5:
time: 174 us; the launch traced here: 173 us
  blocking collectives  123 us (71%)
  starting transfers between devices  26 us (15%)
  waiting for transfers between devices  13 us (7%)
  Pallas kernels  9.44 us (5%)
    all_to_all x4, blocking collectives, exchange(): return lax.all_to_all(rows, axis, split_axis=0, concat_axis=0, tiled=True)  113 us
    all_to_all x1, starting transfers between devices, exchange(): return lax.all_to_all(rows, axis, split_axis=0, concat_axis=0, tiled=True)  16.8 us
    ppermute x3, waiting for transfers between devices, swap(): return lax.ppermute(block, 'ym', [(0, 1), (1, 0)])  13 us
    pallas_call x8, Pallas kernels, call(): pl.pallas_call(kernel, out_shape=outs, in_specs=[SMEM] * scalars + [HBM]...  9.44 us
    ppermute x3, starting transfers between devices, swap(): return lax.ppermute(block, 'ym', [(0, 1), (1, 0)])  9.24 us
    all_gather x1, blocking collectives, shards(): other_rows = lax.all_gather(other_arrived, 'exp', axis=0, tiled=True)  5.59 us
    all_gather x1, blocking collectives, shards(): rows = lax.all_gather(arrived, 'exp', axis=0, tiled=True)  4.74 us
  transfers between devices with their start and end apart: 4, of which 2 were waited for; matrix products, arithmetic and copies ran while one was open for 1% of the time, Pallas kernels for 1%

profile of v5, /device:TPU:1, one launch (start us, length us, event | category | flops | bytes accessed | tf_op | source)
XLA Modules:
  0.0 173.2 jit_solution(11516274558450111729)
XLA Ops:
  0.6 3.1 %shard_map.95 = (bf16[2,256,1152]{2,1,0:T(8,128)(2,1)}, bf16[2,256,1152]{2,1,0:T(8,128)(2,1)}) custom-call(s32[1]{0:T(128)} %bitcast.3.member_ref, bf16[2,256,768]{2,1,0:T(8,128)(2,1)} %gate_hbm.1, bf16[2,256,768]{2,1,0:T(8,128)(2,1)} %up_hbm.1, bf16[2,768,256]{2,1,0:T(8,128)(2,1)} %down_hbm.1), custom_call_target="tpu_custom_call" | custom-call | tf_op jit(solution)/shard_map/pallas_call | solution.py:24
  3.7 0.0 copy-start
  3.7 4.3 %collective-permute-start = (bf16[2,256,1152]{2,1,0:T(8,128)(2,1)}, bf16[2,256,1152]{2,1,0:T(8,128)(2,1)S(1)}, u32[]{:S(2)}, u32[]{:S(2)}) collective-permute-start(bf16[2,256,1152]{2,1,0:T(8,128)(2,1)} %get-tuple-element.16), channel_id=1, source_target_pairs={{0,128},{128,0},{1,129},{129,1},{2,130},{130,2},{3,131},{131,3},{4... | collective-permute-start | bytes 3538952 | tf_op jit(solution)/shard_map/ppermute | solution.py:215
  8.0 2.1 %shard_map.94 = (bf16[512,256]{1,0:T(8,128)(2,1)}, s32[2,128]{1,0:T(2,128)}) custom-call(s32[1]{0:T(128)} %bitcast.core_ref, s32[2,128]{1,0:T(2,128)} %bitcast.21, f32[2,128]{1,0:T(2,128)} %bitcast.16, bf16[128,256]{1,0:T(8,128)(2,1)} %tokens_hbm.1, bf16[128,256]{1,0:T(8,128)(2,1)} %cot_hbm.1), custom_call_target="tpu_custom_call" | custom-call | tf_op jit(solution)/shard_map/pallas_call | solution.py:24
  10.1 30.6 %all_to_all.49 = bf16[32,16,256]{2,1,0:T(8,128)(2,1)S(1)} all-to-all(bf16[32,16,256]{2,1,0:T(8,128)(2,1)} %bitcast.20), channel_id=1, replica_groups=mesh['yp'=4,'ym'=2,'xh'=2,'exp'=2,'z'=8,'xl'=4] {'z','xl'}, dimensions={0} | all-to-all | bytes 524288 | tf_op jit(solution)/shard_map/all_to_all | solution.py:211
  40.6 1.9 %collective-permute-start.1 = (bf16[512,256]{1,0:T(8,128)(2,1)S(1)}, bf16[512,256]{1,0:T(8,128)(2,1)S(1)}, u32[]{:S(2)}, u32[]{:S(2)}) collective-permute-start(bf16[512,256]{1,0:T(8,128)(2,1)S(1)} %bitcast.18), channel_id=1, source_target_pairs={{0,128},{128,0},{1,129},{129,1},{2,130},{130,2},{3,131},{131,3},{4... | collective-permute-start | bytes 786440 | tf_op jit(solution)/shard_map/ppermute | solution.py:215
  42.6 4.7 %all_gather.6.rows_ref = bf16[1024,256]{1,0:T(8,128)(2,1)S(1)} all-gather(bf16[512,256]{1,0:T(8,128)(2,1)S(1)} %bitcast.19), channel_id=1, replica_groups=mesh['yp'=4,'ym'=2,'xh'=2,'exp'=2,'z'=8,'xl'=4] {'exp'}, dimensions={0}, use_global_device_ids=true | all-gather | bytes 786432 | tf_op jit(solution)/shard_map/all_gather | solution.py:249
  47.3 0.4 collective-permute-done.1
  47.7 5.6 %all_gather.7.other_rows_ref = bf16[1024,256]{1,0:T(8,128)(2,1)S(1)} all-gather(bf16[512,256]{1,0:T(8,128)(2,1)S(1)} %collective-permute-done.1), channel_id=1, replica_groups=mesh['yp'=4,'ym'=2,'xh'=2,'exp'=2,'z'=8,'xl'=4] {'exp'}, dimensions={0}, use_global_device_ids=true | all-gather | bytes 786432 | tf_op jit(solution)/shard_map/all_gather | solution.py:250
  53.3 0.0 collective-permute-done.other_ref
  53.3 0.0 copy-done
  53.3 0.8 shard_map.96
  54.2 0.0 copy-start.1
  54.2 36.7 %all_to_all.50.terms_ref = bf16[8,64,1152]{2,1,0:T(8,128)(2,1)S(1)} all-to-all(bf16[8,64,1152]{2,1,0:T(8,128)(2,1)S(1)} %bitcast.15), channel_id=1, replica_groups=mesh['yp'=4,'ym'=2,'xh'=2,'exp'=2,'z'=8,'xl'=4] {'yp','xh'}, dimensions={0} | all-to-all | bytes 2359296 | tf_op jit(solution)/shard_map/all_to_all | solution.py:211
  90.9 0.0 copy-done.1
  90.9 0.3 shard_map.97
  91.2 39.1 %all_to_all.51 = bf16[8,64,1152]{2,1,0:T(8,128)(2,1)S(1)} all-to-all(bf16[8,64,1152]{2,1,0:T(8,128)(2,1)S(1)} %shard_map.97), channel_id=1, replica_groups=mesh['yp'=4,'ym'=2,'xh'=2,'exp'=2,'z'=8,'xl'=4] {'yp','xh'}, dimensions={0} | all-to-all | bytes 2359296 | tf_op jit(solution)/shard_map/all_to_all | solution.py:211
  130.3 0.9 shard_map.98
  131.2 6.2 %all_to_all.52.parts_ref = bf16[2,1024,256]{2,1,0:T(8,128)(2,1)S(1)} all-to-all(bf16[2,1024,256]{2,1,0:T(8,128)(2,1)S(1)} %bitcast.13), channel_id=1, replica_groups=mesh['yp'=4,'ym'=2,'xh'=2,'exp'=2,'z'=8,'xl'=4] {'exp'}, dimensions={0} | all-to-all | bytes 2097152 | tf_op jit(solution)/shard_map/all_to_all | solution.py:211
  137.4 0.9 shard_map.99
  138.3 16.8 %all-to-all-start.4 = ((bf16[64,16,256]{2,1,0:T(8,128)(2,1)}), bf16[64,16,256]{2,1,0:T(8,128)(2,1)S(1)}, u32[]{:S(2)}, u32[]{:S(2)}) async-start(bf16[64,16,256]{2,1,0:T(8,128)(2,1)} %bitcast.9), calls=%async_computation.4 | async-start | bytes 1048576 | tf_op jit(solution)/shard_map/all_to_all | solution.py:211
  155.2 0.0 copy-done.2
  155.2 0.0 copy-done.4
  155.2 0.4 shard_map.101
  155.6 3.0 %collective-permute-start.2 = (bf16[2,384,256]{2,1,0:T(8,128)(2,1)S(1)}, bf16[2,384,256]{2,1,0:T(8,128)(2,1)S(1)}, u32[]{:S(2)}, u32[]{:S(2)}) collective-permute-start(bf16[2,384,256]{2,1,0:T(8,128)(2,1)S(1)} %get-tuple-element.24), channel_id=1, source_target_pairs={{0,128},{128,0},{1,129},{129,1},{2,130},{130,2},{3,131},{131,3},{4... | collective-permute-start | bytes 1179656 | tf_op jit(solution)/shard_map/ppermute | solution.py:215
  158.6 12.6 %collective-permute-done.2 = bf16[2,384,256]{2,1,0:T(8,128)(2,1)S(1)} collective-permute-done((bf16[2,384,256]{2,1,0:T(8,128)(2,1)S(1)}, bf16[2,384,256]{2,1,0:T(8,128)(2,1)S(1)}, u32[]{:S(2)}, u32[]{:S(2)}) %collective-permute-start.2) | collective-permute-done | bytes 393248 | tf_op jit(solution)/shard_map/ppermute | solution.py:215
  171.2 0.1 broadcast_select_fusion.1
  171.3 0.0 copy-start.5
  171.3 0.0 copy-start.6
  171.3 0.9 pad_maximum_fusion
  172.2 0.0 all-to-all-done.4
  172.2 1.0 shard_map.100
  (6 shorter events, 0.0 us)
Async XLA Ops:
  3.7 49.6 %copy-start = (bf16[2,256,1152]{2,1,0:T(8,128)(2,1)S(1)}, bf16[2,256,1152]{2,1,0:T(8,128)(2,1)}, u32[]{:S(2)}) copy-start(bf16[2,256,1152]{2,1,0:T(8,128)(2,1)} %get-tuple-element.15.kept_ref) | copy-start | bytes 3538948
  3.7 49.6 %collective-permute-start = (bf16[2,256,1152]{2,1,0:T(8,128)(2,1)}, bf16[2,256,1152]{2,1,0:T(8,128)(2,1)S(1)}, u32[]{:S(2)}, u32[]{:S(2)}) collective-permute-start(bf16[2,256,1152]{2,1,0:T(8,128)(2,1)} %get-tuple-element.16), channel_id=1, source_target_pairs={{0,128},{128,0},{1,129},{129,1},{2,130},{130,2},{3,131},{131,3},{4... | collective-permute-start | bytes 3538952 | tf_op jit(solution)/shard_map/ppermute | solution.py:215
  40.6 7.1 %collective-permute-start.1 = (bf16[512,256]{1,0:T(8,128)(2,1)S(1)}, bf16[512,256]{1,0:T(8,128)(2,1)S(1)}, u32[]{:S(2)}, u32[]{:S(2)}) collective-permute-start(bf16[512,256]{1,0:T(8,128)(2,1)S(1)} %bitcast.18), channel_id=1, source_target_pairs={{0,128},{128,0},{1,129},{129,1},{2,130},{130,2},{3,131},{131,3},{4... | collective-permute-start | bytes 786440 | tf_op jit(solution)/shard_map/ppermute | solution.py:215
  54.2 36.7 %copy-start.1 = (bf16[2,256,256]{2,1,0:T(8,128)(2,1)}, bf16[2,256,256]{2,1,0:T(8,128)(2,1)S(1)}, u32[]{:S(2)}) copy-start(bf16[2,256,256]{2,1,0:T(8,128)(2,1)S(1)} %get-tuple-element.21.grad_ref) | copy-start | bytes 786436
  54.2 36.7 %copy-start.3 = (bf16[2,256,256]{2,1,0:T(8,128)(2,1)}, bf16[2,256,256]{2,1,0:T(8,128)(2,1)S(1)}, u32[]{:S(2)}) copy-start(bf16[2,256,256]{2,1,0:T(8,128)(2,1)S(1)} %get-tuple-element.22.other_grad_ref) | copy-start | bytes 786436
  137.4 17.7 %copy-start.2 = (bf16[2,256,256]{2,1,0:T(8,128)(2,1)S(1)}, bf16[2,256,256]{2,1,0:T(8,128)(2,1)}, u32[]{:S(2)}) copy-start(bf16[2,256,256]{2,1,0:T(8,128)(2,1)} %copy-done.1) | copy-start | bytes 786436
  137.4 17.7 %copy-start.4 = (bf16[2,256,256]{2,1,0:T(8,128)(2,1)S(1)}, bf16[2,256,256]{2,1,0:T(8,128)(2,1)}, u32[]{:S(2)}) copy-start(bf16[2,256,256]{2,1,0:T(8,128)(2,1)} %copy-done.3) | copy-start | bytes 786436
  138.3 33.9 %all-to-all-start.4 = ((bf16[64,16,256]{2,1,0:T(8,128)(2,1)}), bf16[64,16,256]{2,1,0:T(8,128)(2,1)S(1)}, u32[]{:S(2)}, u32[]{:S(2)}) async-start(bf16[64,16,256]{2,1,0:T(8,128)(2,1)} %bitcast.9), calls=%async_computation.4 | async-start | bytes 1048576 | tf_op jit(solution)/shard_map/all_to_all | solution.py:211
  155.6 15.6 %collective-permute-start.2 = (bf16[2,384,256]{2,1,0:T(8,128)(2,1)S(1)}, bf16[2,384,256]{2,1,0:T(8,128)(2,1)S(1)}, u32[]{:S(2)}, u32[]{:S(2)}) collective-permute-start(bf16[2,384,256]{2,1,0:T(8,128)(2,1)S(1)} %get-tuple-element.24), channel_id=1, source_target_pairs={{0,128},{128,0},{1,129},{129,1},{2,130},{130,2},{3,131},{131,3},{4... | collective-permute-start | bytes 1179656 | tf_op jit(solution)/shard_map/ppermute | solution.py:215
  171.3 1.0 copy-start.5
  171.3 1.0 copy-start.6

commit v6 on v5

--- a/solution.py
+++ b/solution.py
@@ -39,13 +39,13 @@
     return lax.broadcasted_iota(jnp.int32, dims, axis)
 
 
-def pack(member_ref, gate_hbm, up_hbm, down_hbm, kept_ref, given_ref, down, sems):
+def pack(member_ref, gate_hbm, up_hbm, down_hbm, given_two, given_one, kept_ref, down, sems):
     local_experts, _, width = kept_ref.shape
     half = width // 3
     copies = [pltpu.make_async_copy(down_hbm, down, sems.at[0])]
-    sides = ((given_ref, 1 - member_ref[0]), (kept_ref, member_ref[0]))
-    for i, (out, member) in enumerate(sides):
-        units = pl.ds(pl.multiple_of(member * half, 128), half)
+    other = pl.ds(pl.multiple_of((1 - member_ref[0]) * half, 128), half)
+    mine = pl.ds(pl.multiple_of(member_ref[0] * half, 128), half)
+    for i, (out, units) in enumerate(((given_two, other), (kept_ref, mine))):
         for j, weights in enumerate((gate_hbm, up_hbm)):
             copies.append(
                 pltpu.make_async_copy(
@@ -57,16 +57,15 @@
     for copy in copies:
         copy.start()
     copies[0].wait()
-    for out, member in sides:
-        units = pl.ds(pl.multiple_of(member * half, 128), half)
-        for e in range(local_experts):
-            out[e, :, 2 * half :] = down[e, units, :].T
+    for e in range(local_experts):
+        given_one[e] = down[e, other, :].T
+        kept_ref[e, :, 2 * half :] = down[e, mine, :].T
     for copy in copies[1:]:
         copy.wait()
 
 
-def place_rows(experts, core_ref, routes_hbm, weights_hbm, tokens_hbm, cot_hbm, send_ref, slot_ref,
-               routes_ref, weights_ref, tokens_ref, cot_ref, sems):
+def place_rows(experts, core_ref, routes_hbm, weights_hbm, tokens_hbm, cot_hbm, packed, send_ref,
+               slot_ref, routes_ref, weights_ref, tokens_ref, cot_ref, sems):
     copies = [
         pltpu.make_async_copy(source, target, sems.at[i])
         for i, (source, target) in enumerate(
@@ -105,26 +104,28 @@
     send_ref[...] = (rows * scale).astype(BF)
 
 
-def first_terms(kept_ref, other_ref, rows_ref, other_rows_ref, terms_ref, grad_ref, other_grad_ref):
+def first_terms(kept_ref, two_ref, one_ref, rows_ref, other_rows_ref, terms_ref, grad_ref, other_grad_ref):
     local_experts, depth, width = kept_ref.shape
     two = width // 3 * 2
     slots = rows_ref.shape[0] // 2
     count = slots // local_experts
+
+    def picked(rows, kind, e):
+        taken = rows[kind * slots : (kind + 1) * slots, :].astype(F32)
+        taken = taken.reshape(-1, local_experts, CAPACITY, depth)[:, e]
+        return taken.reshape(count, depth).astype(BF)
+
     for e in range(local_experts):
         here = slice(e * count, (e + 1) * count)
-        totals = [0.0, 0.0]
-        for weights, rows, grads in (
-            (kept_ref, rows_ref, grad_ref), (other_ref, other_rows_ref, other_grad_ref)
-        ):
-            for kind, cols in enumerate((slice(0, two), slice(two, width))):
-                picked = rows[kind * slots : (kind + 1) * slots, :].astype(F32)
-                picked = picked.reshape(-1, local_experts, CAPACITY, depth)[:, e]
-                picked = picked.reshape(count, depth).astype(BF)
-                totals[kind] += jnp.dot(picked, weights[e, :, cols], preferred_element_type=F32)
-                if kind == 1:
-                    grads[e] = picked
-        terms_ref[here, :two] = totals[0].astype(BF)
-        terms_ref[here, two:] = totals[1].astype(BF)
+        grad_ref[e], other_grad_ref[e] = picked(rows_ref, 1, e), picked(other_rows_ref, 1, e)
+        terms_ref[here, :two] = (
+            jnp.dot(picked(rows_ref, 0, e), kept_ref[e, :, :two], preferred_element_type=F32)
+            + jnp.dot(picked(other_rows_ref, 0, e), two_ref[e], preferred_element_type=F32)
+        ).astype(BF)
+        terms_ref[here, two:] = (
+            jnp.dot(grad_ref[e], kept_ref[e, :, two:], preferred_element_type=F32)
+            + jnp.dot(other_grad_ref[e], one_ref[e], preferred_element_type=F32)
+        ).astype(BF)
 
 
 def activate(terms_ref, out_ref):
@@ -147,28 +148,33 @@
         out_ref[i, :, 2 * width :] = d_up
 
 
-def last_terms(member_ref, acts_ref, kept_ref, other_ref, parts_ref):
+def last_terms(acts_ref, kept_ref, two_ref, one_ref, parts_ref):
     local_experts, depth, width = kept_ref.shape
     one = width // 3
     count = acts_ref.shape[0] // local_experts
     half = depth // 2
-    for weights, member in ((kept_ref, member_ref[0]), (other_ref, 1 - member_ref[0])):
+
+    def by_group(pieces):
+        shaped = [p.reshape(count // CAPACITY, CAPACITY, depth) for p in pieces]
+        return jnp.concatenate(shaped, axis=1)
+
+    for side in range(2):
         outs, grads = [], []
         for e in range(local_experts):
             here = slice(e * count, (e + 1) * count)
-            out = lax.dot_general(
-                acts_ref[here, :one], weights[e, :, 2 * one :], NT, preferred_element_type=F32
+            down = one_ref[e] if side else kept_ref[e, :, 2 * one :]
+            two = two_ref[e] if side else kept_ref[e, :, : 2 * one]
+            outs.append(
+                lax.dot_general(acts_ref[here, :one], down, NT, preferred_element_type=F32)
             )
-            grad = lax.dot_general(
-                acts_ref[here, one:], weights[e, :, : 2 * one], NT, preferred_element_type=F32
+            grads.append(
+                lax.dot_general(acts_ref[here, one:], two, NT, preferred_element_type=F32)
             )
-            outs.append(out.reshape(count // CAPACITY, CAPACITY, depth))
-            grads.append(grad.reshape(count // CAPACITY, CAPACITY, depth))
-        out, grad = jnp.concatenate(outs, axis=1), jnp.concatenate(grads, axis=1)
+        out, grad = by_group(outs), by_group(grads)
         for j in range(2):
             cols = slice(j * half, (j + 1) * half)
-            parts_ref[2 * j + member, :, :, :half] = out[:, :, cols].astype(BF)
-            parts_ref[2 * j + member, :, :, half:] = grad[:, :, cols].astype(BF)
+            parts_ref[2 * j + side, :, :, :half] = out[:, :, cols].astype(BF)
+            parts_ref[2 * j + side, :, :, half:] = grad[:, :, cols].astype(BF)
 
 
 def down_terms(acts_ref, grad_ref, other_grad_ref, out_ref, other_out_ref):
@@ -180,13 +186,23 @@
             out[e] = lax.dot_general(hidden, grads[e], TN, preferred_element_type=F32).astype(BF)
 
 
-def add_parts(parts_ref, out_ref):
-    out_ref[...] = sum(parts_ref[i].astype(F32) for i in range(parts_ref.shape[0])).astype(BF)
+def add_parts(parts_ref, own_ref, out_ref, grad_ref):
+    total = parts_ref[0].astype(F32) + parts_ref[1].astype(F32)
+    slots, half = out_ref.shape
+    own_ref[...] = total[:slots, :]
+    out_ref[...] = total[slots:, :half].astype(BF)
+    grad_ref[...] = total[slots:, half:].astype(BF)
+
+
+def add_partners(own_ref, out_ref, grad_ref, sums_ref):
+    half = out_ref.shape[1]
+    sums_ref[:, :half] = (own_ref[:, :half] + out_ref[...].astype(F32)).astype(BF)
+    sums_ref[:, half:] = (own_ref[:, half:] + grad_ref[...].astype(F32)).astype(BF)
 
 
 def combine(slot_ref, weights_ref, back_ref, mixed_ref, grads_ref):
     top_count, tok_rows = slot_ref.shape
-    slots, width = back_ref.shape[0] // 2, back_ref.shape[1]
+    slots, width = back_ref.shape
     half = width // 2
     same = iota((tok_rows, tok_rows), 0) == iota((tok_rows, tok_rows), 1)
 
@@ -198,9 +214,7 @@
     for k in range(top_count):
         slot = column(slot_ref[k : k + 1, :].astype(F32)).astype(jnp.int32)
         hot = jnp.where(iota((tok_rows, slots), 1) == slot, 1.0, 0.0).astype(BF)
-        picked = jnp.dot(hot, back_ref[:slots, :], preferred_element_type=F32) + jnp.dot(
-            hot, back_ref[slots:, :], preferred_element_type=F32
-        )
+        picked = jnp.dot(hot, back_ref[...], preferred_element_type=F32)
         mixed = mixed + picked[:, :half] * column(weights_ref[k : k + 1, :])
         grads = grads + picked[:, half:]
     mixed_ref[...] = mixed.astype(BF)
@@ -211,8 +225,20 @@
     return lax.all_to_all(rows, axis, split_axis=0, concat_axis=0, tiled=True)
 
 
-def swap(block):
-    return lax.ppermute(block, "ym", [(0, 1), (1, 0)])
+def neighbour(y, side):
+    size = lax.axis_size("yp") * lax.axis_size("ym")
+    return (y + (1 if y % 2 == side else -1)) % size
+
+
+def swap(block, side):
+    size = lax.axis_size("yp") * lax.axis_size("ym")
+    return lax.ppermute(block, ("yp", "ym"), [(y, neighbour(y, side)) for y in range(size)])
+
+
+def swap_rows(rows):
+    size = lax.axis_size("yp") * lax.axis_size("ym")
+    pairs = [(2 * y + c, 2 * neighbour(y, c) + c) for y in range(size) for c in range(2)]
+    return lax.ppermute(rows, ("yp", "ym", "exp"), pairs)
 
 
 def shards(tokens, routes, route_weights, gate_weight, up_weight, down_weight, cotangent):
@@ -228,45 +254,51 @@
     member = lax.axis_index("ym").reshape(1)
     routes, route_weights = routes.T, route_weights.T
 
-    weights = shape((local_experts, depth, 3 * half), BF)
-    kept, given = call(
-        pack, (weights, weights), member, gate_weight, up_weight, down_weight, scalars=1, given=3,
+    def weights(parts):
+        return shape((local_experts, depth, parts * half), BF)
+
+    given_two, given_one, kept = call(
+        pack, (weights(2), weights(1), weights(3)), member, gate_weight, up_weight, down_weight,
+        scalars=1, given=3,
         scratch=[pltpu.VMEM(down_weight.shape, BF), pltpu.SemaphoreType.DMA((5,))],
     )
     send, slot_index = call(
         functools.partial(place_rows, experts),
         (shape((slots, depth), BF), shape((top_count, tok_rows), jnp.int32)),
-        core, routes, route_weights, tokens, cotangent, scalars=1, given=4,
+        core, routes, route_weights, tokens, cotangent, given_one, scalars=1, given=5,
         scratch=[
             pltpu.VMEM(routes.shape, jnp.int32), pltpu.VMEM(routes.shape, F32),
             pltpu.VMEM(tokens.shape, BF), pltpu.VMEM(tokens.shape, BF),
             pltpu.SemaphoreType.DMA((4,)),
         ],
     )
-    other = swap(given)
+    two, one = swap(given_two, 0), swap(given_one, 1)
     arrived = exchange(send, ETP)
-    other_arrived = swap(arrived)
+    arrived, two, one = lax.optimization_barrier((arrived, two, one))
+    other_arrived = swap_rows(arrived)
     rows = lax.all_gather(arrived, "exp", axis=0, tiled=True)
     other_rows = lax.all_gather(other_arrived, "exp", axis=0, tiled=True)
 
     grads = shape((local_experts, count, depth), BF)
     terms, expert_grad, other_grad = call(
-        first_terms, (shape((slots, 3 * half), BF), grads, grads), kept, other, rows, other_rows
+        first_terms, (shape((slots, 3 * half), BF), grads, grads), kept, two, one, rows, other_rows
     )
     terms = exchange(terms, ("yp", "xh")).reshape(slices, slots // slices, 3 * half)
     acts = call(activate, shape(terms.shape, BF), terms)
     acts = exchange(acts.reshape(slots, 3 * half), ("yp", "xh"))
 
     parts = call(
-        last_terms, shape((4, groups, local_experts * CAPACITY, depth), BF),
-        member, acts, kept, other, scalars=1,
+        last_terms, shape((4, groups, local_experts * CAPACITY, depth), BF), acts, kept, two, one
     )
     parts = exchange(parts.reshape(4 * slots, depth), "exp").reshape(2, 2 * slots, depth)
-    slot_sums = call(add_parts, shape((2 * slots, depth), BF), parts)
-    back = exchange(slot_sums, ("ym",) + ETP)
+    part = shape((slots, depth // 2), BF)
+    own, out_other, grad_other = call(add_parts, (shape((slots, depth), F32), part, part), parts)
+    out_other, grad_other = swap(out_other, 1), swap(grad_other, 0)
+    slot_sums = call(add_partners, shape((slots, depth), BF), own, out_other, grad_other)
+    back = exchange(slot_sums, ETP)
     downs = shape((local_experts, half, depth), BF)
     d_down, other_down = call(down_terms, (downs, downs), acts, expert_grad, other_grad)
-    other_down = swap(other_down)
+    other_down = swap(other_down, 1)
     first = member[0] == 0
     d_down = jnp.concatenate(
         [jnp.where(first, d_down, other_down), jnp.where(first, other_down, d_down)], axis=1

time: 174 us -> 180 us (1.034)
  blocking collectives: 123 us -> 87.5 us
  starting transfers between devices: 26 us -> 56.3 us
  waiting for transfers between devices: 13 us -> 24.5 us
    all_to_all x4 -> x3, blocking collectives: 113 us -> 81.7 us  [exchange(): return lax.all_to_all(rows, axis, split_axis=0, concat_axis=0, tiled=True)]
    all_to_all x1 -> x2, starting transfers between devices: 16.8 us -> 34.6 us  [exchange(): return lax.all_to_all(rows, axis, split_axis=0, concat_axis=0, tiled=True)]
    ppermute x3 -> x6, starting transfers between devices: 9.24 us -> 21.7 us  [the longest x5 17.4 us: swap(): lax.ppermute(block, ('yp', 'ym'), [(y, neighbour(y, side)) for y in range...]
    all_to_all x1 -> x2, waiting for transfers between devices: 0.01 us -> 9.88 us  [exchange(): return lax.all_to_all(rows, axis, split_axis=0, concat_axis=0, tiled=True)]
    all_gather x1, blocking collectives: 4.74 us -> 2.18 us  [shards(): rows = lax.all_gather(arrived, 'exp', axis=0, tiled=True)]
    all_gather x1, blocking collectives: 5.59 us -> 3.62 us  [shards(): other_rows = lax.all_gather(other_arrived, 'exp', axis=0, tiled=True)]
    ppermute x3 -> x6, waiting for transfers between devices: 13 us -> 14.6 us  [the longest x5 12.7 us: swap(): lax.ppermute(block, ('yp', 'ym'), [(y, neighbour(y, side)) for y in range...]
    pallas_call x8 -> x9, Pallas kernels: 9.44 us -> 9.3 us  [call(): pl.pallas_call(kernel, out_shape=outs, in_specs=[SMEM] * scalars + [HBM]...]
  transfers between devices with their start and end apart: 4 -> 8, of which waited for: 2 -> 5; matrix products, arithmetic and copies ran while one was open for 1% -> 1% of each run, Pallas kernels for 1% -> 2%
where the time goes in v6:
time: 180 us; the launch traced here: 179 us
  blocking collectives  87.5 us (49%)
  starting transfers between devices  56.3 us (31%)
  waiting for transfers between devices  24.5 us (14%)
  Pallas kernels  9.3 us (5%)
    all_to_all x3, blocking collectives, exchange(): return lax.all_to_all(rows, axis, split_axis=0, concat_axis=0, tiled=True)  81.7 us
    all_to_all x2, starting transfers between devices, exchange(): return lax.all_to_all(rows, axis, split_axis=0, concat_axis=0, tiled=True)  34.6 us
    ppermute x5, starting transfers between devices, swap(): lax.ppermute(block, ('yp', 'ym'), [(y, neighbour(y, side)) for y in range...  17.4 us
    ppermute x5, waiting for transfers between devices, swap(): lax.ppermute(block, ('yp', 'ym'), [(y, neighbour(y, side)) for y in range...  12.7 us
    all_to_all x2, waiting for transfers between devices, exchange(): return lax.all_to_all(rows, axis, split_axis=0, concat_axis=0, tiled=True)  9.88 us
    pallas_call x9, Pallas kernels, call(): pl.pallas_call(kernel, out_shape=outs, in_specs=[SMEM] * scalars + [HBM]...  9.3 us
    ppermute x1, starting transfers between devices, swap_rows(): return lax.ppermute(rows, ('yp', 'ym', 'exp'), pairs)  4.28 us
    all_gather x1, blocking collectives, shards(): other_rows = lax.all_gather(other_arrived, 'exp', axis=0, tiled=True)  3.62 us
  transfers between devices with their start and end apart: 8, of which 5 were waited for; matrix products, arithmetic and copies ran while one was open for 1% of the time, Pallas kernels for 2%

profile of v6, /device:TPU:1, one launch (start us, length us, event | category | flops | bytes accessed | tf_op | source)
XLA Modules:
  0.0 179.4 jit_solution(596699201930853656)
XLA Ops:
  0.6 3.1 %shard_map.94 = (bf16[2,256,768]{2,1,0:T(8,128)(2,1)}, bf16[2,256,384]{2,1,0:T(8,128)(2,1)}, bf16[2,256,1152]{2,1,0:T(8,128)(2,1)}) custom-call(s32[1]{0:T(128)} %bitcast.3.member_ref, bf16[2,256,768]{2,1,0:T(8,128)(2,1)} %gate_hbm.1, bf16[2,256,768]{2,1,0:T(8,128)(2,1)} %up_hbm.1, bf16[2,768,256]{2,1,0:T(8,128)(2,1)} %down_hbm.1), custom_call_target="tpu_custom_call" | custom-call | tf_op jit(solution)/shard_map/pallas_call | solution.py:24
  3.7 4.1 %collective-permute-start = (bf16[2,256,768]{2,1,0:T(8,128)(2,1)}, bf16[2,256,768]{2,1,0:T(8,128)(2,1)S(1)}, u32[]{:S(2)}, u32[]{:S(2)}) collective-permute-start(bf16[2,256,768]{2,1,0:T(8,128)(2,1)} %get-tuple-element.25), channel_id=1, source_target_pairs={{0,128},{128,0},{256,384},{384,256},{512,640},{640,512},{768,896},... | collective-permute-start | bytes 2359304 | tf_op jit(solution)/shard_map/ppermute | solution.py:235
  7.9 2.1 %shard_map.95 = (bf16[512,256]{1,0:T(8,128)(2,1)}, s32[2,128]{1,0:T(2,128)}) custom-call(s32[1]{0:T(128)} %bitcast.core_ref, s32[2,128]{1,0:T(2,128)} %bitcast.21, f32[2,128]{1,0:T(2,128)} %bitcast.16, bf16[128,256]{1,0:T(8,128)(2,1)} %tokens_hbm.1, bf16[128,256]{1,0:T(8,128)(2,1)} %cot_hbm.1, bf16[2,256,384]{2,1,0:T(8,128)(2,1)} %get-tuple-element.21.packed), custom_call_target="tpu_custom_call" | custom-call | tf_op jit(solution)/shard_map/pallas_call | solution.py:24
  10.0 19.7 %all-to-all-start = ((bf16[32,16,256]{2,1,0:T(8,128)(2,1)}), bf16[32,16,256]{2,1,0:T(8,128)(2,1)S(1)}, u32[]{:S(2)}, u32[]{:S(2)}) async-start(bf16[32,16,256]{2,1,0:T(8,128)(2,1)} %bitcast.20), calls=%async_computation | async-start | bytes 524288 | tf_op jit(solution)/shard_map/all_to_all | solution.py:225
  29.7 5.4 %collective-permute-start.1 = (bf16[2,256,384]{2,1,0:T(8,128)(2,1)}, bf16[2,256,384]{2,1,0:T(8,128)(2,1)S(1)}, u32[]{:S(2)}, u32[]{:S(2)}) collective-permute-start(bf16[2,256,384]{2,1,0:T(8,128)(2,1)} %get-tuple-element.21.packed), channel_id=1, source_target_pairs={{0,896},{128,256},{256,128},{384,512},{512,384},{640,768},{768,640... | collective-permute-start | bytes 1179656 | tf_op jit(solution)/shard_map/ppermute | solution.py:235
  35.1 8.4 %collective-permute-done.1.one_ref = bf16[2,256,384]{2,1,0:T(8,128)(2,1)S(1)} collective-permute-done((bf16[2,256,384]{2,1,0:T(8,128)(2,1)}, bf16[2,256,384]{2,1,0:T(8,128)(2,1)S(1)}, u32[]{:S(2)}, u32[]{:S(2)}) %collective-permute-start.1) | collective-permute-done | bytes 393248 | tf_op jit(solution)/shard_map/ppermute | solution.py:235
  43.5 0.0 all-to-all-done
  43.5 4.3 %collective-permute-start.2 = (bf16[512,256]{1,0:T(8,128)(2,1)S(1)}, bf16[512,256]{1,0:T(8,128)(2,1)S(1)}, u32[]{:S(2)}, u32[]{:S(2)}) collective-permute-start(bf16[512,256]{1,0:T(8,128)(2,1)S(1)} %bitcast.18), channel_id=1, source_target_pairs={{0,128},{32,928},{128,0},{160,288},{256,384},{288,160},{384,256},{... | collective-permute-start | bytes 786440 | tf_op jit(solution)/shard_map/ppermute | solution.py:241
  47.8 2.2 %all_gather.6.rows_ref = bf16[1024,256]{1,0:T(8,128)(2,1)S(1)} all-gather(bf16[512,256]{1,0:T(8,128)(2,1)S(1)} %bitcast.19), channel_id=1, replica_groups=mesh['yp'=4,'ym'=2,'xh'=2,'exp'=2,'z'=8,'xl'=4] {'exp'}, dimensions={0}, use_global_device_ids=true | all-gather | bytes 786432 | tf_op jit(solution)/shard_map/all_gather | solution.py:279
  50.0 1.8 %collective-permute-done.2 = bf16[512,256]{1,0:T(8,128)(2,1)S(1)} collective-permute-done((bf16[512,256]{1,0:T(8,128)(2,1)S(1)}, bf16[512,256]{1,0:T(8,128)(2,1)S(1)}, u32[]{:S(2)}, u32[]{:S(2)}) %collective-permute-start.2) | collective-permute-done | bytes 262176 | tf_op jit(solution)/shard_map/ppermute | solution.py:241
  51.8 3.6 %all_gather.7.other_rows_ref = bf16[1024,256]{1,0:T(8,128)(2,1)S(1)} all-gather(bf16[512,256]{1,0:T(8,128)(2,1)S(1)} %collective-permute-done.2), channel_id=1, replica_groups=mesh['yp'=4,'ym'=2,'xh'=2,'exp'=2,'z'=8,'xl'=4] {'exp'}, dimensions={0}, use_global_device_ids=true | all-gather | bytes 786432 | tf_op jit(solution)/shard_map/all_gather | solution.py:280
  55.4 0.8 shard_map.96
  56.3 36.4 %all_to_all.49.terms_ref = bf16[8,64,1152]{2,1,0:T(8,128)(2,1)S(1)} all-to-all(bf16[8,64,1152]{2,1,0:T(8,128)(2,1)S(1)} %bitcast.14), channel_id=1, replica_groups=mesh['yp'=4,'ym'=2,'xh'=2,'exp'=2,'z'=8,'xl'=4] {'yp','xh'}, dimensions={0} | all-to-all | bytes 2359296 | tf_op jit(solution)/shard_map/all_to_all | solution.py:225
  92.7 0.3 shard_map.97
  93.0 37.3 %all_to_all.50 = bf16[8,64,1152]{2,1,0:T(8,128)(2,1)S(1)} all-to-all(bf16[8,64,1152]{2,1,0:T(8,128)(2,1)S(1)} %shard_map.97), channel_id=1, replica_groups=mesh['yp'=4,'ym'=2,'xh'=2,'exp'=2,'z'=8,'xl'=4] {'yp','xh'}, dimensions={0} | all-to-all | bytes 2359296 | tf_op jit(solution)/shard_map/all_to_all | solution.py:225
  130.3 0.4 shard_map.102
  130.7 1.9 %collective-permute-start.5 = (bf16[2,384,256]{2,1,0:T(8,128)(2,1)S(1)}, bf16[2,384,256]{2,1,0:T(8,128)(2,1)S(1)}, u32[]{:S(2)}, u32[]{:S(2)}) collective-permute-start(bf16[2,384,256]{2,1,0:T(8,128)(2,1)S(1)} %get-tuple-element.38), channel_id=1, source_target_pairs={{0,896},{128,256},{256,128},{384,512},{512,384},{640,768},{768,640... | collective-permute-start | bytes 1179656 | tf_op jit(solution)/shard_map/ppermute | solution.py:235
  132.6 0.9 shard_map.98
  133.5 8.0 %all_to_all.51.parts_ref = bf16[2,1024,256]{2,1,0:T(8,128)(2,1)S(1)} all-to-all(bf16[2,1024,256]{2,1,0:T(8,128)(2,1)S(1)} %bitcast.13), channel_id=1, replica_groups=mesh['yp'=4,'ym'=2,'xh'=2,'exp'=2,'z'=8,'xl'=4] {'exp'}, dimensions={0} | all-to-all | bytes 2097152 | tf_op jit(solution)/shard_map/all_to_all | solution.py:225
  141.5 0.1 shard_map.99
  141.6 4.0 %collective-permute-start.3 = (bf16[512,128]{1,0:T(8,128)(2,1)S(1)}, bf16[512,128]{1,0:T(8,128)(2,1)S(1)}, u32[]{:S(2)}, u32[]{:S(2)}) collective-permute-start(bf16[512,128]{1,0:T(8,128)(2,1)S(1)} %get-tuple-element.31), channel_id=1, source_target_pairs={{0,896},{128,256},{256,128},{384,512},{512,384},{640,768},{768,640... | collective-permute-start | bytes 393224 | tf_op jit(solution)/shard_map/ppermute | solution.py:235
  145.6 1.9 %collective-permute-start.4 = (bf16[512,128]{1,0:T(8,128)(2,1)S(1)}, bf16[512,128]{1,0:T(8,128)(2,1)S(1)}, u32[]{:S(2)}, u32[]{:S(2)}) collective-permute-start(bf16[512,128]{1,0:T(8,128)(2,1)S(1)} %get-tuple-element.32), channel_id=1, source_target_pairs={{0,128},{128,0},{256,384},{384,256},{512,640},{640,512},{768,896},... | collective-permute-start | bytes 393224 | tf_op jit(solution)/shard_map/ppermute | solution.py:235
  147.5 1.9 %collective-permute-done.3.out_ref = bf16[512,128]{1,0:T(8,128)(2,1)S(1)} collective-permute-done((bf16[512,128]{1,0:T(8,128)(2,1)S(1)}, bf16[512,128]{1,0:T(8,128)(2,1)S(1)}, u32[]{:S(2)}, u32[]{:S(2)}) %collective-permute-start.3) | collective-permute-done | bytes 131104 | tf_op jit(solution)/shard_map/ppermute | solution.py:235
  149.4 2.5 %collective-permute-done.4.grad_ref = bf16[512,128]{1,0:T(8,128)(2,1)S(1)} collective-permute-done((bf16[512,128]{1,0:T(8,128)(2,1)S(1)}, bf16[512,128]{1,0:T(8,128)(2,1)S(1)}, u32[]{:S(2)}, u32[]{:S(2)}) %collective-permute-start.4) | collective-permute-done | bytes 131104 | tf_op jit(solution)/shard_map/ppermute | solution.py:235
  151.8 0.7 shard_map.100
  152.6 14.9 %all-to-all-start.4 = ((bf16[32,16,256]{2,1,0:T(8,128)(2,1)}), bf16[32,16,256]{2,1,0:T(8,128)(2,1)S(1)}, u32[]{:S(2)}, u32[]{:S(2)}) async-start(bf16[32,16,256]{2,1,0:T(8,128)(2,1)} %bitcast.9), calls=%async_computation.4 | async-start | bytes 524288 | tf_op jit(solution)/shard_map/all_to_all | solution.py:225
  167.5 0.1 broadcast_select_fusion.1
  167.6 0.0 copy-start.1
  167.6 0.0 copy-start.2
  167.6 0.9 pad_maximum_fusion
  168.6 9.9 %all-to-all-done.4 = bf16[32,16,256]{2,1,0:T(8,128)(2,1)S(1)} async-done(((bf16[32,16,256]{2,1,0:T(8,128)(2,1)}), bf16[32,16,256]{2,1,0:T(8,128)(2,1)S(1)}, u32[]{:S(2)}, u32[]{:S(2)}) %all-to-all-start.4) | async-done | bytes 262176 | tf_op jit(solution)/shard_map/all_to_all | solution.py:225
  178.4 0.9 shard_map.101
  (6 shorter events, 0.0 us)
Async XLA Ops:
  3.7 39.8 %collective-permute-start = (bf16[2,256,768]{2,1,0:T(8,128)(2,1)}, bf16[2,256,768]{2,1,0:T(8,128)(2,1)S(1)}, u32[]{:S(2)}, u32[]{:S(2)}) collective-permute-start(bf16[2,256,768]{2,1,0:T(8,128)(2,1)} %get-tuple-element.25), channel_id=1, source_target_pairs={{0,128},{128,0},{256,384},{384,256},{512,640},{640,512},{768,896},... | collective-permute-start | bytes 2359304 | tf_op jit(solution)/shard_map/ppermute | solution.py:235
  9.9 45.5 %copy-start = (bf16[2,256,1152]{2,1,0:T(8,128)(2,1)S(1)}, bf16[2,256,1152]{2,1,0:T(8,128)(2,1)}, u32[]{:S(2)}) copy-start(bf16[2,256,1152]{2,1,0:T(8,128)(2,1)} %get-tuple-element.23.kept_ref) | copy-start | bytes 3538948
  10.0 33.5 %all-to-all-start = ((bf16[32,16,256]{2,1,0:T(8,128)(2,1)}), bf16[32,16,256]{2,1,0:T(8,128)(2,1)S(1)}, u32[]{:S(2)}, u32[]{:S(2)}) async-start(bf16[32,16,256]{2,1,0:T(8,128)(2,1)} %bitcast.20), calls=%async_computation | async-start | bytes 524288 | tf_op jit(solution)/shard_map/all_to_all | solution.py:225
  29.7 13.8 %collective-permute-start.1 = (bf16[2,256,384]{2,1,0:T(8,128)(2,1)}, bf16[2,256,384]{2,1,0:T(8,128)(2,1)S(1)}, u32[]{:S(2)}, u32[]{:S(2)}) collective-permute-start(bf16[2,256,384]{2,1,0:T(8,128)(2,1)} %get-tuple-element.21.packed), channel_id=1, source_target_pairs={{0,896},{128,256},{256,128},{384,512},{512,384},{640,768},{768,640... | collective-permute-start | bytes 1179656 | tf_op jit(solution)/shard_map/ppermute | solution.py:235
  43.5 8.3 %collective-permute-start.2 = (bf16[512,256]{1,0:T(8,128)(2,1)S(1)}, bf16[512,256]{1,0:T(8,128)(2,1)S(1)}, u32[]{:S(2)}, u32[]{:S(2)}) collective-permute-start(bf16[512,256]{1,0:T(8,128)(2,1)S(1)} %bitcast.18), channel_id=1, source_target_pairs={{0,128},{32,928},{128,0},{160,288},{256,384},{288,160},{384,256},{... | collective-permute-start | bytes 786440 | tf_op jit(solution)/shard_map/ppermute | solution.py:241
  130.7 36.9 %collective-permute-start.5 = (bf16[2,384,256]{2,1,0:T(8,128)(2,1)S(1)}, bf16[2,384,256]{2,1,0:T(8,128)(2,1)S(1)}, u32[]{:S(2)}, u32[]{:S(2)}) collective-permute-start(bf16[2,384,256]{2,1,0:T(8,128)(2,1)S(1)} %get-tuple-element.38), channel_id=1, source_target_pairs={{0,896},{128,256},{256,128},{384,512},{512,384},{640,768},{768,640... | collective-permute-start | bytes 1179656 | tf_op jit(solution)/shard_map/ppermute | solution.py:235
  141.6 7.8 %collective-permute-start.3 = (bf16[512,128]{1,0:T(8,128)(2,1)S(1)}, bf16[512,128]{1,0:T(8,128)(2,1)S(1)}, u32[]{:S(2)}, u32[]{:S(2)}) collective-permute-start(bf16[512,128]{1,0:T(8,128)(2,1)S(1)} %get-tuple-element.31), channel_id=1, source_target_pairs={{0,896},{128,256},{256,128},{384,512},{512,384},{640,768},{768,640... | collective-permute-start | bytes 393224 | tf_op jit(solution)/shard_map/ppermute | solution.py:235
  145.6 6.3 %collective-permute-start.4 = (bf16[512,128]{1,0:T(8,128)(2,1)S(1)}, bf16[512,128]{1,0:T(8,128)(2,1)S(1)}, u32[]{:S(2)}, u32[]{:S(2)}) collective-permute-start(bf16[512,128]{1,0:T(8,128)(2,1)S(1)} %get-tuple-element.32), channel_id=1, source_target_pairs={{0,128},{128,0},{256,384},{384,256},{512,640},{640,512},{768,896},... | collective-permute-start | bytes 393224 | tf_op jit(solution)/shard_map/ppermute | solution.py:235
  152.6 25.9 %all-to-all-start.4 = ((bf16[32,16,256]{2,1,0:T(8,128)(2,1)}), bf16[32,16,256]{2,1,0:T(8,128)(2,1)S(1)}, u32[]{:S(2)}, u32[]{:S(2)}) async-start(bf16[32,16,256]{2,1,0:T(8,128)(2,1)} %bitcast.9), calls=%async_computation.4 | async-start | bytes 524288 | tf_op jit(solution)/shard_map/all_to_all | solution.py:225
  167.6 10.8 %copy-start.1 = (f32[128,2]{0,1:T(2,128)S(1)}, f32[128,2]{0,1:T(2,128)}, u32[]{:S(2)}) copy-start(f32[128,2]{0,1:T(2,128)} %param.9) | copy-start | bytes 3076
  167.6 10.8 %copy-start.2 = (s32[2,128]{1,0:T(2,128)S(1)}, s32[2,128]{1,0:T(2,128)}, u32[]{:S(2)}) copy-start(s32[2,128]{1,0:T(2,128)} %get-tuple-element.22.slot_ref) | copy-start | bytes 3076

commit v7 on v5

--- a/solution.py
+++ b/solution.py
@@ -105,7 +105,8 @@
     send_ref[...] = (rows * scale).astype(BF)
 
 
-def first_terms(kept_ref, other_ref, rows_ref, other_rows_ref, terms_ref, grad_ref, other_grad_ref):
+def first_terms(turn_ref, kept_ref, other_ref, rows_ref, other_rows_ref, *refs):
+    own_ref, *messages, grad_ref, other_grad_ref, terms = refs
     local_experts, depth, width = kept_ref.shape
     two = width // 3 * 2
     slots = rows_ref.shape[0] // 2
@@ -123,31 +124,43 @@
                 totals[kind] += jnp.dot(picked, weights[e, :, cols], preferred_element_type=F32)
                 if kind == 1:
                     grads[e] = picked
-        terms_ref[here, :two] = totals[0].astype(BF)
-        terms_ref[here, two:] = totals[1].astype(BF)
-
-
-def activate(terms_ref, out_ref):
-    copies, rows, width = out_ref.shape
-    width = width // 3
+        terms[here, :two] = totals[0]
+        terms[here, two:] = totals[1]
+    turns = 1 + len(messages)
+    rows = own_ref.shape[0]
+    for k, out in enumerate((own_ref, *messages)):
+        base = pl.multiple_of(lax.rem(turn_ref[0] + k, turns) * rows, rows)
+        out[...] = terms[pl.ds(base, rows), :].astype(out.dtype)
+
+
+def add_terms(own_ref, *refs):
+    *came, out_ref = refs
+    out_ref[...] = (own_ref[...] + sum(piece[...].astype(F32) for piece in came)).astype(BF)
+
+
+def activate(pair_ref, out_ref):
+    rows, width = out_ref.shape[0], out_ref.shape[1] // 3
 
     def total(part):
         cols = slice(part * width, (part + 1) * width)
-        return sum(terms_ref[i, :, cols].astype(F32) for i in range(terms_ref.shape[0]))
+        return pair_ref[:rows, cols].astype(F32) + pair_ref[rows:, cols].astype(F32)
 
     gate, up_proj, d_hidden = total(0), total(1), total(2)
     sigmoid_gate = jax.nn.sigmoid(gate)
     silu_gate = gate * sigmoid_gate
-    hidden = (silu_gate * up_proj).astype(BF)
-    d_gate = (d_hidden * up_proj * sigmoid_gate * (1.0 + gate * (1.0 - sigmoid_gate))).astype(BF)
-    d_up = (d_hidden * silu_gate).astype(BF)
-    for i in range(copies):
-        out_ref[i, :, :width] = hidden
-        out_ref[i, :, width : 2 * width] = d_gate
-        out_ref[i, :, 2 * width :] = d_up
-
-
-def last_terms(member_ref, acts_ref, kept_ref, other_ref, parts_ref):
+    out_ref[:, :width] = (silu_gate * up_proj).astype(BF)
+    out_ref[:, width : 2 * width] = (
+        d_hidden * up_proj * sigmoid_gate * (1.0 + gate * (1.0 - sigmoid_gate))
+    ).astype(BF)
+    out_ref[:, 2 * width :] = (d_hidden * silu_gate).astype(BF)
+
+
+def last_terms(member_ref, turn_ref, kept_ref, other_ref, *refs):
+    *pieces, parts_ref, acts_ref = refs
+    rows = pieces[0].shape[0]
+    for k, piece in enumerate(pieces):
+        turn = lax.rem(turn_ref[0] + (len(pieces) - k), len(pieces))
+        acts_ref[pl.ds(pl.multiple_of(turn * rows, rows), rows), :] = piece[...]
     local_experts, depth, width = kept_ref.shape
     one = width // 3
     count = acts_ref.shape[0] // local_experts
@@ -211,6 +224,11 @@
     return lax.all_to_all(rows, axis, split_axis=0, concat_axis=0, tiled=True)
 
 
+def onward(block, turns):
+    size = lax.axis_size("yp")
+    return lax.ppermute(block, "yp", [(i, (i + turns) % size) for i in range(size)])
+
+
 def swap(block):
     return lax.ppermute(block, "ym", [(0, 1), (1, 0)])
 
@@ -223,9 +241,11 @@
     slots = experts * CAPACITY
     count = groups * CAPACITY
     half = width // 2
-    slices = lax.axis_size("yp") * lax.axis_size("xh")
+    turns = lax.axis_size("yp")
+    rows_each = slots // turns
     core = lax.axis_index("exp").reshape(1)
     member = lax.axis_index("ym").reshape(1)
+    turn = lax.axis_index("yp").reshape(1)
     routes, route_weights = routes.T, route_weights.T
 
     weights = shape((local_experts, depth, 3 * half), BF)
@@ -250,16 +270,25 @@
     other_rows = lax.all_gather(other_arrived, "exp", axis=0, tiled=True)
 
     grads = shape((local_experts, count, depth), BF)
-    terms, expert_grad, other_grad = call(
-        first_terms, (shape((slots, 3 * half), BF), grads, grads), kept, other, rows, other_rows
-    )
-    terms = exchange(terms, ("yp", "xh")).reshape(slices, slots // slices, 3 * half)
-    acts = call(activate, shape(terms.shape, BF), terms)
-    acts = exchange(acts.reshape(slots, 3 * half), ("yp", "xh"))
-
-    parts = call(
-        last_terms, shape((4, groups, local_experts * CAPACITY, depth), BF),
-        member, acts, kept, other, scalars=1,
+    block = shape((rows_each, 3 * half), BF)
+    own, *messages, expert_grad, other_grad = call(
+        first_terms,
+        (shape(block.shape, F32),) + (block,) * (turns - 1) + (grads, grads),
+        turn, kept, other, rows, other_rows, scalars=1,
+        scratch=[pltpu.VMEM((slots, 3 * half), F32)],
+    )
+    came = [onward(message, k) for k, message in enumerate(messages, 1)]
+    sums = call(add_terms, block, own, *came)
+    acts = call(activate, block, lax.all_gather(sums, "xh", axis=0, tiled=True))
+    pieces = [acts] + [onward(acts, k) for k in range(1, turns)]
+
+    parts, acts = call(
+        last_terms,
+        (
+            shape((4, groups, local_experts * CAPACITY, depth), BF),
+            shape((slots, 3 * half), BF),
+        ),
+        member, turn, kept, other, *pieces, scalars=2,
     )
     parts = exchange(parts.reshape(4 * slots, depth), "exp").reshape(2, 2 * slots, depth)
     slot_sums = call(add_parts, shape((2 * slots, depth), BF), parts)

time: 174 us -> 176 us (1.011)
  blocking collectives: 123 us -> 61.7 us
  waiting for transfers between devices: 13 us -> 51.8 us
  starting transfers between devices: 26 us -> 49.3 us
    all_to_all x4 -> x2, blocking collectives: 113 us -> 35.3 us  [exchange(): return lax.all_to_all(rows, axis, split_axis=0, concat_axis=0, tiled=True)]
    ppermute x0 -> x6, waiting for transfers between devices: none -> 38.8 us  [onward(): lax.ppermute(block, 'yp', [(i, (i + turns) % size) for i in range(size)])]
    ppermute x0 -> x6, starting transfers between devices: none -> 28.6 us  [onward(): lax.ppermute(block, 'yp', [(i, (i + turns) % size) for i in range(size)])]
    all_gather x0 -> x1, blocking collectives: none -> 16.1 us  [shards(): acts = call(activate, block, lax.all_gather(sums, 'xh', axis=0, tiled=True))]
    all_to_all x1, starting transfers between devices: 16.8 us -> 11.3 us  [exchange(): return lax.all_to_all(rows, axis, split_axis=0, concat_axis=0, tiled=True)]
    pallas_call x8 -> x9, Pallas kernels: 9.44 us -> 9.88 us  [call(): pl.pallas_call(kernel, out_shape=outs, in_specs=[SMEM] * scalars + [HBM]...]
  transfers between devices with their start and end apart: 4 -> 10, of which waited for: 2 -> 6; matrix products, arithmetic and copies ran while one was open for 1% -> 1% of each run, Pallas kernels for 1% -> 1%
where the time goes in v7:
time: 176 us; the launch traced here: 175 us
  blocking collectives  61.7 us (35%)
  waiting for transfers between devices  51.8 us (29%)
  starting transfers between devices  49.3 us (28%)
  Pallas kernels  9.88 us (6%)
    ppermute x6, waiting for transfers between devices, onward(): lax.ppermute(block, 'yp', [(i, (i + turns) % size) for i in range(size)])  38.8 us
    all_to_all x2, blocking collectives, exchange(): return lax.all_to_all(rows, axis, split_axis=0, concat_axis=0, tiled=True)  35.3 us
    ppermute x6, starting transfers between devices, onward(): lax.ppermute(block, 'yp', [(i, (i + turns) % size) for i in range(size)])  28.6 us
    all_gather x1, blocking collectives, shards(): acts = call(activate, block, lax.all_gather(sums, 'xh', axis=0, tiled=True))  16.1 us
    ppermute x3, waiting for transfers between devices, swap(): return lax.ppermute(block, 'ym', [(0, 1), (1, 0)])  13 us
    all_to_all x1, starting transfers between devices, exchange(): return lax.all_to_all(rows, axis, split_axis=0, concat_axis=0, tiled=True)  11.3 us
    pallas_call x9, Pallas kernels, call(): pl.pallas_call(kernel, out_shape=outs, in_specs=[SMEM] * scalars + [HBM]...  9.88 us
    ppermute x3, starting transfers between devices, swap(): return lax.ppermute(block, 'ym', [(0, 1), (1, 0)])  9.27 us
  transfers between devices with their start and end apart: 10, of which 6 were waited for; matrix products, arithmetic and copies ran while one was open for 1% of the time, Pallas kernels for 1%

profile of v7, /device:TPU:1, one launch (start us, length us, event | category | flops | bytes accessed | tf_op | source)
XLA Modules:
  0.0 174.5 jit_solution(15617648052609262665)
XLA Ops:
  0.6 3.1 %shard_map.95 = (bf16[2,256,1152]{2,1,0:T(8,128)(2,1)}, bf16[2,256,1152]{2,1,0:T(8,128)(2,1)}) custom-call(s32[1]{0:T(128)} %bitcast.3.member_ref, bf16[2,256,768]{2,1,0:T(8,128)(2,1)} %gate_hbm.1, bf16[2,256,768]{2,1,0:T(8,128)(2,1)} %up_hbm.1, bf16[2,768,256]{2,1,0:T(8,128)(2,1)} %down_hbm.1), custom_call_target="tpu_custom_call" | custom-call | tf_op jit(solution)/shard_map/pallas_call | solution.py:24
  3.7 4.3 %collective-permute-start = (bf16[2,256,1152]{2,1,0:T(8,128)(2,1)}, bf16[2,256,1152]{2,1,0:T(8,128)(2,1)S(1)}, u32[]{:S(2)}, u32[]{:S(2)}) collective-permute-start(bf16[2,256,1152]{2,1,0:T(8,128)(2,1)} %get-tuple-element.21), channel_id=1, source_target_pairs={{0,128},{128,0},{1,129},{129,1},{2,130},{130,2},{3,131},{131,3},{4... | collective-permute-start | bytes 3538952 | tf_op jit(solution)/shard_map/ppermute | solution.py:233
  8.0 2.1 %shard_map.94 = (bf16[512,256]{1,0:T(8,128)(2,1)}, s32[2,128]{1,0:T(2,128)}) custom-call(s32[1]{0:T(128)} %bitcast.core_ref, s32[2,128]{1,0:T(2,128)} %bitcast.17, f32[2,128]{1,0:T(2,128)} %bitcast.12, bf16[128,256]{1,0:T(8,128)(2,1)} %tokens_hbm.1, bf16[128,256]{1,0:T(8,128)(2,1)} %cot_hbm.1), custom_call_target="tpu_custom_call" | custom-call | tf_op jit(solution)/shard_map/pallas_call | solution.py:24
  10.1 30.6 %all_to_all.32 = bf16[32,16,256]{2,1,0:T(8,128)(2,1)S(1)} all-to-all(bf16[32,16,256]{2,1,0:T(8,128)(2,1)} %bitcast.16), channel_id=1, replica_groups=mesh['yp'=4,'ym'=2,'xh'=2,'exp'=2,'z'=8,'xl'=4] {'z','xl'}, dimensions={0} | all-to-all | bytes 524288 | tf_op jit(solution)/shard_map/all_to_all | solution.py:224
  40.6 2.0 %collective-permute-start.1 = (bf16[512,256]{1,0:T(8,128)(2,1)S(1)}, bf16[512,256]{1,0:T(8,128)(2,1)S(1)}, u32[]{:S(2)}, u32[]{:S(2)}) collective-permute-start(bf16[512,256]{1,0:T(8,128)(2,1)S(1)} %bitcast.14), channel_id=1, source_target_pairs={{0,128},{128,0},{1,129},{129,1},{2,130},{130,2},{3,131},{131,3},{4... | collective-permute-start | bytes 786440 | tf_op jit(solution)/shard_map/ppermute | solution.py:233
  42.6 4.7 %all_gather.9.rows_ref = bf16[1024,256]{1,0:T(8,128)(2,1)S(1)} all-gather(bf16[512,256]{1,0:T(8,128)(2,1)S(1)} %bitcast.15), channel_id=1, replica_groups=mesh['yp'=4,'ym'=2,'xh'=2,'exp'=2,'z'=8,'xl'=4] {'exp'}, dimensions={0}, use_global_device_ids=true | all-gather | bytes 786432 | tf_op jit(solution)/shard_map/all_gather | solution.py:269
  47.3 0.4 collective-permute-done.1
  47.7 5.6 %all_gather.10.other_rows_ref = bf16[1024,256]{1,0:T(8,128)(2,1)S(1)} all-gather(bf16[512,256]{1,0:T(8,128)(2,1)S(1)} %collective-permute-done.1), channel_id=1, replica_groups=mesh['yp'=4,'ym'=2,'xh'=2,'exp'=2,'z'=8,'xl'=4] {'exp'}, dimensions={0}, use_global_device_ids=true | all-gather | bytes 786432 | tf_op jit(solution)/shard_map/all_gather | solution.py:270
  53.3 1.2 shard_map.96
  54.5 4.5 %collective-permute-start.2 = (bf16[128,1152]{1,0:T(8,128)(2,1)S(1)}, bf16[128,1152]{1,0:T(8,128)(2,1)S(1)}, u32[]{:S(2)}, u32[]{:S(2)}) collective-permute-start(bf16[128,1152]{1,0:T(8,128)(2,1)S(1)} %get-tuple-element.24), channel_id=1, source_target_pairs={{0,256},{256,512},{512,768},{768,0},{1,257},{257,513},{513,769},{7... | collective-permute-start | bytes 884744 | tf_op jit(solution)/shard_map/ppermute | solution.py:229
  59.0 5.2 %collective-permute-start.3 = (bf16[128,1152]{1,0:T(8,128)(2,1)S(1)}, bf16[128,1152]{1,0:T(8,128)(2,1)S(1)}, u32[]{:S(2)}, u32[]{:S(2)}) collective-permute-start(bf16[128,1152]{1,0:T(8,128)(2,1)S(1)} %get-tuple-element.25), channel_id=1, source_target_pairs={{0,512},{256,768},{512,0},{768,256},{1,513},{257,769},{513,1},{769... | collective-permute-start | bytes 884744 | tf_op jit(solution)/shard_map/ppermute | solution.py:229
  64.2 4.7 %collective-permute-start.4 = (bf16[128,1152]{1,0:T(8,128)(2,1)S(1)}, bf16[128,1152]{1,0:T(8,128)(2,1)S(1)}, u32[]{:S(2)}, u32[]{:S(2)}) collective-permute-start(bf16[128,1152]{1,0:T(8,128)(2,1)S(1)} %get-tuple-element.26), channel_id=1, source_target_pairs={{0,768},{256,0},{512,256},{768,512},{1,769},{257,1},{513,257},{769... | collective-permute-start | bytes 884744 | tf_op jit(solution)/shard_map/ppermute | solution.py:229
  69.0 9.6 %collective-permute-done.3.refs_1_ = bf16[128,1152]{1,0:T(8,128)(2,1)S(1)} collective-permute-done((bf16[128,1152]{1,0:T(8,128)(2,1)S(1)}, bf16[128,1152]{1,0:T(8,128)(2,1)S(1)}, u32[]{:S(2)}, u32[]{:S(2)}) %collective-permute-start.3) | collective-permute-done | bytes 294944 | tf_op jit(solution)/shard_map/ppermute | solution.py:229
  78.6 12.7 %collective-permute-done.4.refs_2_ = bf16[128,1152]{1,0:T(8,128)(2,1)S(1)} collective-permute-done((bf16[128,1152]{1,0:T(8,128)(2,1)S(1)}, bf16[128,1152]{1,0:T(8,128)(2,1)S(1)}, u32[]{:S(2)}, u32[]{:S(2)}) %collective-permute-start.4) | collective-permute-done | bytes 294944 | tf_op jit(solution)/shard_map/ppermute | solution.py:229
  91.3 0.1 shard_map.97
  91.4 16.1 %all_gather.11.pair_ref = bf16[256,1152]{1,0:T(8,128)(2,1)S(1)} all-gather(bf16[128,1152]{1,0:T(8,128)(2,1)S(1)} %shard_map.97), channel_id=1, replica_groups=mesh['yp'=4,'ym'=2,'xh'=2,'exp'=2,'z'=8,'xl'=4] {'xh'}, dimensions={0}, use_global_device_ids=true | all-gather | bytes 884736 | tf_op jit(solution)/shard_map/all_gather | solution.py:282
  107.6 0.2 shard_map.98.refs_0_
  107.7 3.4 %collective-permute-start.5 = (bf16[128,1152]{1,0:T(8,128)(2,1)S(1)}, bf16[128,1152]{1,0:T(8,128)(2,1)S(1)}, u32[]{:S(2)}, u32[]{:S(2)}) collective-permute-start(bf16[128,1152]{1,0:T(8,128)(2,1)S(1)} %shard_map.98.refs_0_), channel_id=1, source_target_pairs={{0,256},{256,512},{512,768},{768,0},{1,257},{257,513},{513,769},{7... | collective-permute-start | bytes 884744 | tf_op jit(solution)/shard_map/ppermute | solution.py:229
  111.1 5.9 %collective-permute-start.6 = (bf16[128,1152]{1,0:T(8,128)(2,1)S(1)}, bf16[128,1152]{1,0:T(8,128)(2,1)S(1)}, u32[]{:S(2)}, u32[]{:S(2)}) collective-permute-start(bf16[128,1152]{1,0:T(8,128)(2,1)S(1)} %shard_map.98.refs_0_), channel_id=1, source_target_pairs={{0,512},{256,768},{512,0},{768,256},{1,513},{257,769},{513,1},{769... | collective-permute-start | bytes 884744 | tf_op jit(solution)/shard_map/ppermute | solution.py:229
  117.0 5.0 %collective-permute-start.7 = (bf16[128,1152]{1,0:T(8,128)(2,1)S(1)}, bf16[128,1152]{1,0:T(8,128)(2,1)S(1)}, u32[]{:S(2)}, u32[]{:S(2)}) collective-permute-start(bf16[128,1152]{1,0:T(8,128)(2,1)S(1)} %shard_map.98.refs_0_), channel_id=1, source_target_pairs={{0,768},{256,0},{512,256},{768,512},{1,769},{257,1},{513,257},{769... | collective-permute-start | bytes 884744 | tf_op jit(solution)/shard_map/ppermute | solution.py:229
  122.0 12.5 %collective-permute-done.6.refs_2_ = bf16[128,1152]{1,0:T(8,128)(2,1)S(1)} collective-permute-done((bf16[128,1152]{1,0:T(8,128)(2,1)S(1)}, bf16[128,1152]{1,0:T(8,128)(2,1)S(1)}, u32[]{:S(2)}, u32[]{:S(2)}) %collective-permute-start.6) | collective-permute-done | bytes 294944 | tf_op jit(solution)/shard_map/ppermute | solution.py:229
  134.5 4.0 %collective-permute-done.7.refs_3_ = bf16[128,1152]{1,0:T(8,128)(2,1)S(1)} collective-permute-done((bf16[128,1152]{1,0:T(8,128)(2,1)S(1)}, bf16[128,1152]{1,0:T(8,128)(2,1)S(1)}, u32[]{:S(2)}, u32[]{:S(2)}) %collective-permute-start.7) | collective-permute-done | bytes 294944 | tf_op jit(solution)/shard_map/ppermute | solution.py:229
  138.4 1.0 shard_map.99
  139.4 4.7 %all_to_all.33.parts_ref = bf16[2,1024,256]{2,1,0:T(8,128)(2,1)S(1)} all-to-all(bf16[2,1024,256]{2,1,0:T(8,128)(2,1)S(1)} %bitcast.11), channel_id=1, replica_groups=mesh['yp'=4,'ym'=2,'xh'=2,'exp'=2,'z'=8,'xl'=4] {'exp'}, dimensions={0} | all-to-all | bytes 2097152 | tf_op jit(solution)/shard_map/all_to_all | solution.py:224
  144.2 0.9 shard_map.100
  145.1 11.3 %all-to-all-start.2 = ((bf16[64,16,256]{2,1,0:T(8,128)(2,1)}), bf16[64,16,256]{2,1,0:T(8,128)(2,1)S(1)}, u32[]{:S(2)}, u32[]{:S(2)}) async-start(bf16[64,16,256]{2,1,0:T(8,128)(2,1)} %bitcast.8), calls=%async_computation.2 | async-start | bytes 1048576 | tf_op jit(solution)/shard_map/all_to_all | solution.py:224
  156.5 0.4 shard_map.102
  156.9 3.0 %collective-permute-start.8 = (bf16[2,384,256]{2,1,0:T(8,128)(2,1)S(1)}, bf16[2,384,256]{2,1,0:T(8,128)(2,1)S(1)}, u32[]{:S(2)}, u32[]{:S(2)}) collective-permute-start(bf16[2,384,256]{2,1,0:T(8,128)(2,1)S(1)} %get-tuple-element.34), channel_id=1, source_target_pairs={{0,128},{128,0},{1,129},{129,1},{2,130},{130,2},{3,131},{131,3},{4... | collective-permute-start | bytes 1179656 | tf_op jit(solution)/shard_map/ppermute | solution.py:233
  159.9 12.6 %collective-permute-done.8 = bf16[2,384,256]{2,1,0:T(8,128)(2,1)S(1)} collective-permute-done((bf16[2,384,256]{2,1,0:T(8,128)(2,1)S(1)}, bf16[2,384,256]{2,1,0:T(8,128)(2,1)S(1)}, u32[]{:S(2)}, u32[]{:S(2)}) %collective-permute-start.8) | collective-permute-done | bytes 393248 | tf_op jit(solution)/shard_map/ppermute | solution.py:233
  172.5 0.1 broadcast_select_fusion.1
  172.6 0.9 pad_maximum_fusion
  173.5 1.0 shard_map.101
  (18 shorter events, 0.0 us)
Async XLA Ops:
  3.7 49.6 %copy-start = (bf16[2,256,1152]{2,1,0:T(8,128)(2,1)S(1)}, bf16[2,256,1152]{2,1,0:T(8,128)(2,1)}, u32[]{:S(2)}) copy-start(bf16[2,256,1152]{2,1,0:T(8,128)(2,1)} %get-tuple-element.20.kept_ref) | copy-start | bytes 3538948
  3.7 49.6 %collective-permute-start = (bf16[2,256,1152]{2,1,0:T(8,128)(2,1)}, bf16[2,256,1152]{2,1,0:T(8,128)(2,1)S(1)}, u32[]{:S(2)}, u32[]{:S(2)}) collective-permute-start(bf16[2,256,1152]{2,1,0:T(8,128)(2,1)} %get-tuple-element.21), channel_id=1, source_target_pairs={{0,128},{128,0},{1,129},{129,1},{2,130},{130,2},{3,131},{131,3},{4... | collective-permute-start | bytes 3538952 | tf_op jit(solution)/shard_map/ppermute | solution.py:233
  40.6 7.1 %collective-permute-start.1 = (bf16[512,256]{1,0:T(8,128)(2,1)S(1)}, bf16[512,256]{1,0:T(8,128)(2,1)S(1)}, u32[]{:S(2)}, u32[]{:S(2)}) collective-permute-start(bf16[512,256]{1,0:T(8,128)(2,1)S(1)} %bitcast.14), channel_id=1, source_target_pairs={{0,128},{128,0},{1,129},{129,1},{2,130},{130,2},{3,131},{131,3},{4... | collective-permute-start | bytes 786440 | tf_op jit(solution)/shard_map/ppermute | solution.py:233
  54.5 53.1 %copy-start.1 = (bf16[2,256,256]{2,1,0:T(8,128)(2,1)}, bf16[2,256,256]{2,1,0:T(8,128)(2,1)S(1)}, u32[]{:S(2)}) copy-start(bf16[2,256,256]{2,1,0:T(8,128)(2,1)S(1)} %get-tuple-element.31.grad_ref) | copy-start | bytes 786436
  54.5 53.0 %copy-start.3 = (bf16[2,256,256]{2,1,0:T(8,128)(2,1)}, bf16[2,256,256]{2,1,0:T(8,128)(2,1)S(1)}, u32[]{:S(2)}) copy-start(bf16[2,256,256]{2,1,0:T(8,128)(2,1)S(1)} %get-tuple-element.32.other_grad_ref) | copy-start | bytes 786436
  54.5 14.4 %collective-permute-start.2 = (bf16[128,1152]{1,0:T(8,128)(2,1)S(1)}, bf16[128,1152]{1,0:T(8,128)(2,1)S(1)}, u32[]{:S(2)}, u32[]{:S(2)}) collective-permute-start(bf16[128,1152]{1,0:T(8,128)(2,1)S(1)} %get-tuple-element.24), channel_id=1, source_target_pairs={{0,256},{256,512},{512,768},{768,0},{1,257},{257,513},{513,769},{7... | collective-permute-start | bytes 884744 | tf_op jit(solution)/shard_map/ppermute | solution.py:229
  59.0 19.6 %collective-permute-start.3 = (bf16[128,1152]{1,0:T(8,128)(2,1)S(1)}, bf16[128,1152]{1,0:T(8,128)(2,1)S(1)}, u32[]{:S(2)}, u32[]{:S(2)}) collective-permute-start(bf16[128,1152]{1,0:T(8,128)(2,1)S(1)} %get-tuple-element.25), channel_id=1, source_target_pairs={{0,512},{256,768},{512,0},{768,256},{1,513},{257,769},{513,1},{769... | collective-permute-start | bytes 884744 | tf_op jit(solution)/shard_map/ppermute | solution.py:229
  64.2 27.1 %collective-permute-start.4 = (bf16[128,1152]{1,0:T(8,128)(2,1)S(1)}, bf16[128,1152]{1,0:T(8,128)(2,1)S(1)}, u32[]{:S(2)}, u32[]{:S(2)}) collective-permute-start(bf16[128,1152]{1,0:T(8,128)(2,1)S(1)} %get-tuple-element.26), channel_id=1, source_target_pairs={{0,768},{256,0},{512,256},{768,512},{1,769},{257,1},{513,257},{769... | collective-permute-start | bytes 884744 | tf_op jit(solution)/shard_map/ppermute | solution.py:229
  107.7 14.3 %collective-permute-start.5 = (bf16[128,1152]{1,0:T(8,128)(2,1)S(1)}, bf16[128,1152]{1,0:T(8,128)(2,1)S(1)}, u32[]{:S(2)}, u32[]{:S(2)}) collective-permute-start(bf16[128,1152]{1,0:T(8,128)(2,1)S(1)} %shard_map.98.refs_0_), channel_id=1, source_target_pairs={{0,256},{256,512},{512,768},{768,0},{1,257},{257,513},{513,769},{7... | collective-permute-start | bytes 884744 | tf_op jit(solution)/shard_map/ppermute | solution.py:229
  111.1 23.4 %collective-permute-start.6 = (bf16[128,1152]{1,0:T(8,128)(2,1)S(1)}, bf16[128,1152]{1,0:T(8,128)(2,1)S(1)}, u32[]{:S(2)}, u32[]{:S(2)}) collective-permute-start(bf16[128,1152]{1,0:T(8,128)(2,1)S(1)} %shard_map.98.refs_0_), channel_id=1, source_target_pairs={{0,512},{256,768},{512,0},{768,256},{1,513},{257,769},{513,1},{769... | collective-permute-start | bytes 884744 | tf_op jit(solution)/shard_map/ppermute | solution.py:229
  117.0 21.5 %collective-permute-start.7 = (bf16[128,1152]{1,0:T(8,128)(2,1)S(1)}, bf16[128,1152]{1,0:T(8,128)(2,1)S(1)}, u32[]{:S(2)}, u32[]{:S(2)}) collective-permute-start(bf16[128,1152]{1,0:T(8,128)(2,1)S(1)} %shard_map.98.refs_0_), channel_id=1, source_target_pairs={{0,768},{256,0},{512,256},{768,512},{1,769},{257,1},{513,257},{769... | collective-permute-start | bytes 884744 | tf_op jit(solution)/shard_map/ppermute | solution.py:229
  144.2 12.3 %copy-start.2 = (bf16[2,256,256]{2,1,0:T(8,128)(2,1)S(1)}, bf16[2,256,256]{2,1,0:T(8,128)(2,1)}, u32[]{:S(2)}) copy-start(bf16[2,256,256]{2,1,0:T(8,128)(2,1)} %copy-done.1) | copy-start | bytes 786436
  144.2 12.3 %copy-start.4 = (bf16[2,256,256]{2,1,0:T(8,128)(2,1)S(1)}, bf16[2,256,256]{2,1,0:T(8,128)(2,1)}, u32[]{:S(2)}) copy-start(bf16[2,256,256]{2,1,0:T(8,128)(2,1)} %copy-done.3) | copy-start | bytes 786436
  145.1 28.4 %all-to-all-start.2 = ((bf16[64,16,256]{2,1,0:T(8,128)(2,1)}), bf16[64,16,256]{2,1,0:T(8,128)(2,1)S(1)}, u32[]{:S(2)}, u32[]{:S(2)}) async-start(bf16[64,16,256]{2,1,0:T(8,128)(2,1)} %bitcast.8), calls=%async_computation.2 | async-start | bytes 1048576 | tf_op jit(solution)/shard_map/all_to_all | solution.py:224
  156.9 15.6 %collective-permute-start.8 = (bf16[2,384,256]{2,1,0:T(8,128)(2,1)S(1)}, bf16[2,384,256]{2,1,0:T(8,128)(2,1)S(1)}, u32[]{:S(2)}, u32[]{:S(2)}) collective-permute-start(bf16[2,384,256]{2,1,0:T(8,128)(2,1)S(1)} %get-tuple-element.34), channel_id=1, source_target_pairs={{0,128},{128,0},{1,129},{129,1},{2,130},{130,2},{3,131},{131,3},{4... | collective-permute-start | bytes 1179656 | tf_op jit(solution)/shard_map/ppermute | solution.py:233
  172.6 1.0 copy-start.5
  172.6 1.0 copy-start.6

commit v8 on v4

--- a/solution.py
+++ b/solution.py
@@ -13,19 +13,21 @@
 CAPACITY = 8
 VMEM = pl.BlockSpec(memory_space=pltpu.VMEM)
 SMEM = pl.BlockSpec(memory_space=pltpu.SMEM)
+HBM = pl.BlockSpec(memory_space=pltpu.HBM)
 LIMIT = pltpu.CompilerParams(vmem_limit_bytes=40 * 1024 * 1024)
 NT = (((1,), (1,)), ((), ()))
 TN = (((0,), (0,)), ((), ()))
 
 
-def call(kernel, outs, *args, scalars=0, given=0):
+def call(kernel, outs, *args, scalars=0, given=0, scratch=()):
     rest = len(args) - scalars - given
     return pl.pallas_call(
         kernel,
         out_shape=outs,
-        in_specs=[SMEM] * scalars + [pl.BlockSpec()] * given + [VMEM] * rest,
+        in_specs=[SMEM] * scalars + [HBM] * given + [VMEM] * rest,
         out_specs=jax.tree.map(lambda _: VMEM, outs),
-        compiler_params=LIMIT,
+        scratch_shapes=scratch,
+        compiler_params=pltpu.CompilerParams(vmem_limit_bytes=(56 if given else 40) * 1024 * 1024),
     )(*args)
 
 
@@ -37,16 +39,31 @@
     return lax.broadcasted_iota(jnp.int32, dims, axis)
 
 
-def begin(experts, core_ref, member_ref, routes_ref, weights_ref, tokens_ref, cot_ref,
-          gate_ref, up_ref, down_ref, send_ref, slot_ref, kept_ref, given_ref):
-    local_experts, _, width = gate_ref.shape
-    half = width // 2
-    for out, member in ((given_ref, 1 - member_ref[0]), (kept_ref, member_ref[0])):
-        units = pl.ds(pl.multiple_of(member * half, 128), half)
+def begin(experts, core_ref, member_ref, routes_hbm, weights_hbm, tokens_hbm, cot_hbm, gate_hbm,
+          up_hbm, down_hbm, send_ref, slot_ref, kept_ref, given_ref,
+          routes_ref, weights_ref, tokens_ref, cot_ref, down, sems):
+    local_experts, _, width = kept_ref.shape
+    part = width // 3
+    sides = [
+        (out, pl.ds(pl.multiple_of(owner * part, 128), part))
+        for out, owner in ((given_ref, 1 - member_ref[0]), (kept_ref, member_ref[0]))
+    ]
+    moves = [
+        (routes_hbm, routes_ref), (weights_hbm, weights_ref), (down_hbm, down),
+        (tokens_hbm, tokens_ref), (cot_hbm, cot_ref),
+    ]
+    for out, units in sides:
+        for j, source in enumerate((gate_hbm, up_hbm)):
+            target = out.at[:, :, j * part : (j + 1) * part]
+            moves.append((source.at[:, :, units], target))
+    copies = [pltpu.make_async_copy(a, b, sems.at[i]) for i, (a, b) in enumerate(moves)]
+    for copy in copies:
+        copy.start()
+    for copy in copies[:3]:
+        copy.wait()
+    for out, units in sides:
         for e in range(local_experts):
-            out[e, :, :half] = gate_ref[e, :, units]
-            out[e, :, half : 2 * half] = up_ref[e, :, units]
-            out[e, :, 2 * half :] = down_ref[e, units, :].T
+            out[e, :, 2 * part :] = down[e, units, :].T
     top_count, tok_rows = routes_ref.shape
     hots = [iota((experts, tok_rows), 0) == routes_ref[k : k + 1, :] for k in range(top_count)]
     both = sum(jnp.where(hot, 1.0, 0.0) for hot in hots)
@@ -63,6 +80,8 @@
         slot_weight = slot_weight + jnp.sum(
             jnp.where(hit, weights_ref[k : k + 1, :], 0.0), axis=1, keepdims=True
         )
+    for copy in copies[3:]:
+        copy.wait()
     first = core_ref[0] == 0
     source = jnp.where(first, tokens_ref[...].astype(F32), cot_ref[...].astype(F32)).astype(BF)
     scale = jnp.where(first, 1.0, slot_weight)
@@ -132,8 +151,8 @@
         out, grad = jnp.concatenate(outs, axis=1), jnp.concatenate(grads, axis=1)
         for j in range(2):
             cols = slice(j * half, (j + 1) * half)
-            parts_ref[member * 2 + j, :, :, :half] = out[:, :, cols].astype(BF)
-            parts_ref[member * 2 + j, :, :, half:] = grad[:, :, cols].astype(BF)
+            parts_ref[2 * j + member, :, :, :half] = out[:, :, cols].astype(BF)
+            parts_ref[2 * j + member, :, :, half:] = grad[:, :, cols].astype(BF)
 
 
 def down_terms(acts_ref, grad_ref, other_grad_ref, out_ref, other_out_ref):
@@ -151,7 +170,7 @@
 
 def combine(slot_ref, weights_ref, back_ref, mixed_ref, grads_ref):
     top_count, tok_rows = slot_ref.shape
-    slots, width = back_ref.shape
+    slots, width = back_ref.shape[0] // 2, back_ref.shape[1]
     half = width // 2
     same = iota((tok_rows, tok_rows), 0) == iota((tok_rows, tok_rows), 1)
 
@@ -163,7 +182,9 @@
     for k in range(top_count):
         slot = column(slot_ref[k : k + 1, :].astype(F32)).astype(jnp.int32)
         hot = jnp.where(iota((tok_rows, slots), 1) == slot, 1.0, 0.0).astype(BF)
-        picked = jnp.dot(hot, back_ref[...], preferred_element_type=F32)
+        picked = jnp.dot(hot, back_ref[:slots, :], preferred_element_type=F32) + jnp.dot(
+            hot, back_ref[slots:, :], preferred_element_type=F32
+        )
         mixed = mixed + picked[:, :half] * column(weights_ref[k : k + 1, :])
         grads = grads + picked[:, half:]
     mixed_ref[...] = mixed.astype(BF)
@@ -197,6 +218,11 @@
         (shape((slots, depth), BF), shape((top_count, tok_rows), jnp.int32), weights, weights),
         core, member, routes, route_weights, tokens, cotangent, gate_weight, up_weight,
         down_weight, scalars=2, given=7,
+        scratch=[
+            pltpu.VMEM(routes.shape, jnp.int32), pltpu.VMEM(routes.shape, F32),
+            pltpu.VMEM(tokens.shape, BF), pltpu.VMEM(tokens.shape, BF),
+            pltpu.VMEM(down_weight.shape, BF), pltpu.SemaphoreType.DMA((9,)),
+        ],
     )
     other = swap(given)
     arrived = exchange(send, ETP)
@@ -216,9 +242,9 @@
         last_terms, shape((4, groups, local_experts * CAPACITY, depth), BF),
         member, acts, kept, other, scalars=1,
     )
-    parts = exchange(parts.reshape(4 * slots, depth), ("ym", "exp")).reshape(4, slots, depth)
-    slot_sums = call(add_parts, shape((slots, depth), BF), parts)
-    back = exchange(slot_sums, ETP)
+    parts = exchange(parts.reshape(4 * slots, depth), "exp").reshape(2, 2 * slots, depth)
+    slot_sums = call(add_parts, shape((2 * slots, depth), BF), parts)
+    back = exchange(slot_sums, ("ym",) + ETP)
     downs = shape((local_experts, half, depth), BF)
     d_down, other_down = call(down_terms, (downs, downs), acts, expert_grad, other_grad)
     other_down = swap(other_down)

time: 184 us -> 174 us (0.946)
  waiting for transfers between devices: 20.2 us -> 13 us
  blocking collectives: 116 us -> 123 us
  local copies, waits for them, and re-layouts: 6.43 us -> 0.02 us
  starting transfers between devices: 32.6 us -> 28 us
    all_to_all x2 -> x1, waiting for transfers between devices: 19.8 us -> 0.01 us  [exchange(): return lax.all_to_all(rows, axis, split_axis=0, concat_axis=0, tiled=True)]
    ppermute x3, waiting for transfers between devices: 0.41 us -> 13 us  [swap(): return lax.ppermute(block, 'ym', [(0, 1), (1, 0)])]
    unnamed x16 -> x6, local copies, waits for them, and re-layouts: 6.43 us -> 0.02 us
    all_to_all x3 -> x4, blocking collectives: 106 us -> 113 us  [exchange(): return lax.all_to_all(rows, axis, split_axis=0, concat_axis=0, tiled=True)]
    all_to_all x2 -> x1, starting transfers between devices: 23.2 us -> 18.8 us  [exchange(): return lax.all_to_all(rows, axis, split_axis=0, concat_axis=0, tiled=True)]
  transfers between devices with their start and end apart: 5 -> 4, of which waited for: 3 -> 2; matrix products, arithmetic and copies ran while one was open for 1% -> 1% of each run, Pallas kernels for 1% -> 0%
where the time goes in v8:
time: 174 us; the launch traced here: 173 us
  blocking collectives  123 us (71%)
  starting transfers between devices  28 us (16%)
  waiting for transfers between devices  13 us (7%)
  Pallas kernels  7.56 us (4%)
    all_to_all x4, blocking collectives, exchange(): return lax.all_to_all(rows, axis, split_axis=0, concat_axis=0, tiled=True)  113 us
    all_to_all x1, starting transfers between devices, exchange(): return lax.all_to_all(rows, axis, split_axis=0, concat_axis=0, tiled=True)  18.8 us
    ppermute x3, waiting for transfers between devices, swap(): return lax.ppermute(block, 'ym', [(0, 1), (1, 0)])  13 us
    ppermute x3, starting transfers between devices, swap(): return lax.ppermute(block, 'ym', [(0, 1), (1, 0)])  9.24 us
    pallas_call x7, Pallas kernels, call(): pl.pallas_call(kernel, out_shape=outs, in_specs=[SMEM] * scalars + [HBM]...  7.56 us
    all_gather x1, blocking collectives, shards(): other_rows = lax.all_gather(other_arrived, 'exp', axis=0, tiled=True)  5.59 us
    all_gather x1, blocking collectives, shards(): rows = lax.all_gather(arrived, 'exp', axis=0, tiled=True)  4.74 us
  transfers between devices with their start and end apart: 4, of which 2 were waited for; matrix products, arithmetic and copies ran while one was open for 1% of the time, Pallas kernels for 0%

profile of v8, /device:TPU:1, one launch (start us, length us, event | category | flops | bytes accessed | tf_op | source)
XLA Modules:
  0.0 173.3 jit_solution(10713882077924457815)
XLA Ops:
  0.6 3.2 %shard_map.94 = (bf16[512,256]{1,0:T(8,128)(2,1)}, s32[2,128]{1,0:T(2,128)}, bf16[2,256,1152]{2,1,0:T(8,128)(2,1)}, bf16[2,256,1152]{2,1,0:T(8,128)(2,1)}) custom-call(s32[1]{0:T(128)} %bitcast.core_ref, s32[1]{0:T(128)} %bitcast.1.member_ref, s32[2,128]{1,0:T(2,128)} %bitcast.21, f32[2,128]{1,0:T(2,128)} %bitcast.16, bf16[128,256]{1,0:T(8,128)(2,1)} %tokens_hbm.1, ...), custom_call_target="tpu_custom_call" | custom-call | tf_op jit(solution)/shard_map/pallas_call | solution.py:24
  3.9 0.0 copy-start
  3.9 4.3 %collective-permute-start = (bf16[2,256,1152]{2,1,0:T(8,128)(2,1)}, bf16[2,256,1152]{2,1,0:T(8,128)(2,1)S(1)}, u32[]{:S(2)}, u32[]{:S(2)}) collective-permute-start(bf16[2,256,1152]{2,1,0:T(8,128)(2,1)} %get-tuple-element.16), channel_id=1, source_target_pairs={{0,128},{128,0},{1,129},{129,1},{2,130},{130,2},{3,131},{131,3},{4... | collective-permute-start | bytes 3538952 | tf_op jit(solution)/shard_map/ppermute | solution.py:199
  8.2 30.6 %all_to_all.49 = bf16[32,16,256]{2,1,0:T(8,128)(2,1)S(1)} all-to-all(bf16[32,16,256]{2,1,0:T(8,128)(2,1)} %bitcast.20), channel_id=1, replica_groups=mesh['yp'=4,'ym'=2,'xh'=2,'exp'=2,'z'=8,'xl'=4] {'z','xl'}, dimensions={0} | all-to-all | bytes 524288 | tf_op jit(solution)/shard_map/all_to_all | solution.py:195
  38.7 1.9 %collective-permute-start.1 = (bf16[512,256]{1,0:T(8,128)(2,1)S(1)}, bf16[512,256]{1,0:T(8,128)(2,1)S(1)}, u32[]{:S(2)}, u32[]{:S(2)}) collective-permute-start(bf16[512,256]{1,0:T(8,128)(2,1)S(1)} %bitcast.18), channel_id=1, source_target_pairs={{0,128},{128,0},{1,129},{129,1},{2,130},{130,2},{3,131},{131,3},{4... | collective-permute-start | bytes 786440 | tf_op jit(solution)/shard_map/ppermute | solution.py:199
  40.7 4.7 %all_gather.6.rows_ref = bf16[1024,256]{1,0:T(8,128)(2,1)S(1)} all-gather(bf16[512,256]{1,0:T(8,128)(2,1)S(1)} %bitcast.19), channel_id=1, replica_groups=mesh['yp'=4,'ym'=2,'xh'=2,'exp'=2,'z'=8,'xl'=4] {'exp'}, dimensions={0}, use_global_device_ids=true | all-gather | bytes 786432 | tf_op jit(solution)/shard_map/all_gather | solution.py:230
  45.4 0.4 collective-permute-done.1
  45.8 5.6 %all_gather.7.other_rows_ref = bf16[1024,256]{1,0:T(8,128)(2,1)S(1)} all-gather(bf16[512,256]{1,0:T(8,128)(2,1)S(1)} %collective-permute-done.1), channel_id=1, replica_groups=mesh['yp'=4,'ym'=2,'xh'=2,'exp'=2,'z'=8,'xl'=4] {'exp'}, dimensions={0}, use_global_device_ids=true | all-gather | bytes 786432 | tf_op jit(solution)/shard_map/all_gather | solution.py:231
  51.4 0.0 collective-permute-done.other_ref
  51.4 0.0 copy-done
  51.4 0.8 shard_map.95
  52.3 36.7 %all_to_all.50.terms_ref = bf16[8,64,1152]{2,1,0:T(8,128)(2,1)S(1)} all-to-all(bf16[8,64,1152]{2,1,0:T(8,128)(2,1)S(1)} %bitcast.15), channel_id=1, replica_groups=mesh['yp'=4,'ym'=2,'xh'=2,'exp'=2,'z'=8,'xl'=4] {'yp','xh'}, dimensions={0} | all-to-all | bytes 2359296 | tf_op jit(solution)/shard_map/all_to_all | solution.py:195
  89.0 0.3 shard_map.96
  89.3 39.1 %all_to_all.51 = bf16[8,64,1152]{2,1,0:T(8,128)(2,1)S(1)} all-to-all(bf16[8,64,1152]{2,1,0:T(8,128)(2,1)S(1)} %shard_map.96), channel_id=1, replica_groups=mesh['yp'=4,'ym'=2,'xh'=2,'exp'=2,'z'=8,'xl'=4] {'yp','xh'}, dimensions={0} | all-to-all | bytes 2359296 | tf_op jit(solution)/shard_map/all_to_all | solution.py:195
  128.4 0.9 shard_map.97
  129.3 6.2 %all_to_all.52.parts_ref = bf16[2,1024,256]{2,1,0:T(8,128)(2,1)S(1)} all-to-all(bf16[2,1024,256]{2,1,0:T(8,128)(2,1)S(1)} %bitcast.13), channel_id=1, replica_groups=mesh['yp'=4,'ym'=2,'xh'=2,'exp'=2,'z'=8,'xl'=4] {'exp'}, dimensions={0} | all-to-all | bytes 2097152 | tf_op jit(solution)/shard_map/all_to_all | solution.py:195
  135.5 0.9 shard_map.98
  136.4 18.8 %all-to-all-start.4 = ((bf16[64,16,256]{2,1,0:T(8,128)(2,1)}), bf16[64,16,256]{2,1,0:T(8,128)(2,1)S(1)}, u32[]{:S(2)}, u32[]{:S(2)}) async-start(bf16[64,16,256]{2,1,0:T(8,128)(2,1)} %bitcast.9), calls=%async_computation.4 | async-start | bytes 1048576 | tf_op jit(solution)/shard_map/all_to_all | solution.py:195
  155.2 0.4 shard_map.100
  155.6 3.0 %collective-permute-start.2 = (bf16[2,384,256]{2,1,0:T(8,128)(2,1)S(1)}, bf16[2,384,256]{2,1,0:T(8,128)(2,1)S(1)}, u32[]{:S(2)}, u32[]{:S(2)}) collective-permute-start(bf16[2,384,256]{2,1,0:T(8,128)(2,1)S(1)} %get-tuple-element.24), channel_id=1, source_target_pairs={{0,128},{128,0},{1,129},{129,1},{2,130},{130,2},{3,131},{131,3},{4... | collective-permute-start | bytes 1179656 | tf_op jit(solution)/shard_map/ppermute | solution.py:199
  158.6 12.6 %collective-permute-done.2 = bf16[2,384,256]{2,1,0:T(8,128)(2,1)S(1)} collective-permute-done((bf16[2,384,256]{2,1,0:T(8,128)(2,1)S(1)}, bf16[2,384,256]{2,1,0:T(8,128)(2,1)S(1)}, u32[]{:S(2)}, u32[]{:S(2)}) %collective-permute-start.2) | collective-permute-done | bytes 393248 | tf_op jit(solution)/shard_map/ppermute | solution.py:199
  171.3 0.1 broadcast_select_fusion.1
  171.3 0.0 copy-start.1
  171.3 0.0 copy-start.2
  171.3 0.9 pad_maximum_fusion
  172.3 0.0 all-to-all-done.4
  172.3 0.0 copy-done.1
  172.3 0.0 copy-done.2
  172.3 1.0 shard_map.99
Async XLA Ops:
  3.9 47.6 %copy-start = (bf16[2,256,1152]{2,1,0:T(8,128)(2,1)S(1)}, bf16[2,256,1152]{2,1,0:T(8,128)(2,1)}, u32[]{:S(2)}) copy-start(bf16[2,256,1152]{2,1,0:T(8,128)(2,1)} %get-tuple-element.15.kept_ref) | copy-start | bytes 3538948
  3.9 47.5 %collective-permute-start = (bf16[2,256,1152]{2,1,0:T(8,128)(2,1)}, bf16[2,256,1152]{2,1,0:T(8,128)(2,1)S(1)}, u32[]{:S(2)}, u32[]{:S(2)}) collective-permute-start(bf16[2,256,1152]{2,1,0:T(8,128)(2,1)} %get-tuple-element.16), channel_id=1, source_target_pairs={{0,128},{128,0},{1,129},{129,1},{2,130},{130,2},{3,131},{131,3},{4... | collective-permute-start | bytes 3538952 | tf_op jit(solution)/shard_map/ppermute | solution.py:199
  38.7 7.1 %collective-permute-start.1 = (bf16[512,256]{1,0:T(8,128)(2,1)S(1)}, bf16[512,256]{1,0:T(8,128)(2,1)S(1)}, u32[]{:S(2)}, u32[]{:S(2)}) collective-permute-start(bf16[512,256]{1,0:T(8,128)(2,1)S(1)} %bitcast.18), channel_id=1, source_target_pairs={{0,128},{128,0},{1,129},{129,1},{2,130},{130,2},{3,131},{131,3},{4... | collective-permute-start | bytes 786440 | tf_op jit(solution)/shard_map/ppermute | solution.py:199
  136.4 35.9 %all-to-all-start.4 = ((bf16[64,16,256]{2,1,0:T(8,128)(2,1)}), bf16[64,16,256]{2,1,0:T(8,128)(2,1)S(1)}, u32[]{:S(2)}, u32[]{:S(2)}) async-start(bf16[64,16,256]{2,1,0:T(8,128)(2,1)} %bitcast.9), calls=%async_computation.4 | async-start | bytes 1048576 | tf_op jit(solution)/shard_map/all_to_all | solution.py:195
  155.6 15.6 %collective-permute-start.2 = (bf16[2,384,256]{2,1,0:T(8,128)(2,1)S(1)}, bf16[2,384,256]{2,1,0:T(8,128)(2,1)S(1)}, u32[]{:S(2)}, u32[]{:S(2)}) collective-permute-start(bf16[2,384,256]{2,1,0:T(8,128)(2,1)S(1)} %get-tuple-element.24), channel_id=1, source_target_pairs={{0,128},{128,0},{1,129},{129,1},{2,130},{130,2},{3,131},{131,3},{4... | collective-permute-start | bytes 1179656 | tf_op jit(solution)/shard_map/ppermute | solution.py:199
  171.3 1.0 copy-start.1
  171.3 1.0 copy-start.2

commit v9 on v8

--- a/solution.py
+++ b/solution.py
@@ -19,7 +19,7 @@
 TN = (((0,), (0,)), ((), ()))
 
 
-def call(kernel, outs, *args, scalars=0, given=0, scratch=()):
+def call(kernel, outs, *args, scalars=0, given=0, scratch=(), cost=None):
     rest = len(args) - scalars - given
     return pl.pallas_call(
         kernel,
@@ -27,6 +27,7 @@
         in_specs=[SMEM] * scalars + [HBM] * given + [VMEM] * rest,
         out_specs=jax.tree.map(lambda _: VMEM, outs),
         scratch_shapes=scratch,
+        cost_estimate=cost,
         compiler_params=pltpu.CompilerParams(vmem_limit_bytes=(56 if given else 40) * 1024 * 1024),
     )(*args)
 
@@ -164,6 +165,13 @@
             out[e] = lax.dot_general(hidden, grads[e], TN, preferred_element_type=F32).astype(BF)
 
 
+def join(member_ref, mine_ref, other_ref, out_ref):
+    half = mine_ref.shape[1]
+    for source, member in ((mine_ref, member_ref[0]), (other_ref, 1 - member_ref[0])):
+        units = pl.ds(pl.multiple_of(member * half, half), half)
+        out_ref[:, units, :] = source[...]
+
+
 def add_parts(parts_ref, out_ref):
     out_ref[...] = sum(parts_ref[i].astype(F32) for i in range(parts_ref.shape[0])).astype(BF)
 
@@ -248,9 +256,9 @@
     downs = shape((local_experts, half, depth), BF)
     d_down, other_down = call(down_terms, (downs, downs), acts, expert_grad, other_grad)
     other_down = swap(other_down)
-    first = member[0] == 0
-    d_down = jnp.concatenate(
-        [jnp.where(first, d_down, other_down), jnp.where(first, other_down, d_down)], axis=1
+    d_down = call(
+        join, shape(down_weight.shape, BF), member, d_down, other_down, scalars=1,
+        cost=pl.CostEstimate(flops=30_000_000_000, bytes_accessed=1 << 20, transcendentals=0),
     )
     mixed, d_tokens = call(
         combine,

time: 174 us -> 177 us (1.017)
  waiting for transfers between devices: 13 us -> 16.3 us
  blocking collectives: 123 us -> 125 us
    all_to_all x1, waiting for transfers between devices: 0.01 us -> 15.9 us  [exchange(): return lax.all_to_all(rows, axis, split_axis=0, concat_axis=0, tiled=True)]
    ppermute x3, waiting for transfers between devices: 13 us -> 0.42 us  [swap(): return lax.ppermute(block, 'ym', [(0, 1), (1, 0)])]
    pallas_call x7 -> x8, Pallas kernels: 7.56 us -> 8.51 us  [call(): pl.pallas_call(kernel, out_shape=outs, in_specs=[SMEM] * scalars + [HBM]...]
  transfers between devices with their start and end apart: 4 -> 4, of which waited for: 2 -> 2; matrix products, arithmetic and copies ran while one was open for 1% -> 0% of each run, Pallas kernels for 0% -> 2%
where the time goes in v9:
time: 177 us
  blocking collectives  125 us (71%)
  starting transfers between devices  26.4 us (15%)
  waiting for transfers between devices  16.3 us (9%)
  Pallas kernels  8.51 us (5%)
    all_to_all x4, blocking collectives, exchange(): return lax.all_to_all(rows, axis, split_axis=0, concat_axis=0, tiled=True)  114 us
    all_to_all x1, starting transfers between devices, exchange(): return lax.all_to_all(rows, axis, split_axis=0, concat_axis=0, tiled=True)  18.2 us
    all_to_all x1, waiting for transfers between devices, exchange(): return lax.all_to_all(rows, axis, split_axis=0, concat_axis=0, tiled=True)  15.9 us
    pallas_call x8, Pallas kernels, call(): pl.pallas_call(kernel, out_shape=outs, in_specs=[SMEM] * scalars + [HBM]...  8.51 us
    ppermute x3, starting transfers between devices, swap(): return lax.ppermute(block, 'ym', [(0, 1), (1, 0)])  8.14 us
    all_gather x1, blocking collectives, shards(): other_rows = lax.all_gather(other_arrived, 'exp', axis=0, tiled=True)  5.59 us
    all_gather x1, blocking collectives, shards(): rows = lax.all_gather(arrived, 'exp', axis=0, tiled=True)  4.74 us
  transfers between devices with their start and end apart: 4, of which 2 were waited for; matrix products, arithmetic and copies ran while one was open for 0% of the time, Pallas kernels for 2%

profile of v9, /device:TPU:1, one launch (start us, length us, event | category | flops | bytes accessed | tf_op | source)
XLA Modules:
  0.0 176.5 jit_solution(11398682154493749694)
XLA Ops:
  0.6 3.2 %shard_map.94 = (bf16[512,256]{1,0:T(8,128)(2,1)}, s32[2,128]{1,0:T(2,128)}, bf16[2,256,1152]{2,1,0:T(8,128)(2,1)}, bf16[2,256,1152]{2,1,0:T(8,128)(2,1)}) custom-call(s32[1]{0:T(128)} %bitcast.core_ref, s32[1]{0:T(128)} %bitcast.1.member_ref, s32[2,128]{1,0:T(2,128)} %bitcast.21, f32[2,128]{1,0:T(2,128)} %bitcast.16, bf16[128,256]{1,0:T(8,128)(2,1)} %tokens_hbm.1, ...), custom_call_target="tpu_custom_call" | custom-call | tf_op jit(solution)/shard_map/pallas_call | solution.py:24
  3.9 0.0 copy-start
  3.9 4.3 %collective-permute-start = (bf16[2,256,1152]{2,1,0:T(8,128)(2,1)}, bf16[2,256,1152]{2,1,0:T(8,128)(2,1)S(1)}, u32[]{:S(2)}, u32[]{:S(2)}) collective-permute-start(bf16[2,256,1152]{2,1,0:T(8,128)(2,1)} %get-tuple-element.16), channel_id=1, source_target_pairs={{0,128},{128,0},{1,129},{129,1},{2,130},{130,2},{3,131},{131,3},{4... | collective-permute-start | bytes 3538952 | tf_op jit(solution)/shard_map/ppermute | solution.py:207
  8.2 30.6 %all_to_all.49 = bf16[32,16,256]{2,1,0:T(8,128)(2,1)S(1)} all-to-all(bf16[32,16,256]{2,1,0:T(8,128)(2,1)} %bitcast.20), channel_id=1, replica_groups=mesh['yp'=4,'ym'=2,'xh'=2,'exp'=2,'z'=8,'xl'=4] {'z','xl'}, dimensions={0} | all-to-all | bytes 524288 | tf_op jit(solution)/shard_map/all_to_all | solution.py:203
  38.7 1.9 %collective-permute-start.1 = (bf16[512,256]{1,0:T(8,128)(2,1)S(1)}, bf16[512,256]{1,0:T(8,128)(2,1)S(1)}, u32[]{:S(2)}, u32[]{:S(2)}) collective-permute-start(bf16[512,256]{1,0:T(8,128)(2,1)S(1)} %bitcast.18), channel_id=1, source_target_pairs={{0,128},{128,0},{1,129},{129,1},{2,130},{130,2},{3,131},{131,3},{4... | collective-permute-start | bytes 786440 | tf_op jit(solution)/shard_map/ppermute | solution.py:207
  40.7 4.7 %all_gather.6.rows_ref = bf16[1024,256]{1,0:T(8,128)(2,1)S(1)} all-gather(bf16[512,256]{1,0:T(8,128)(2,1)S(1)} %bitcast.19), channel_id=1, replica_groups=mesh['yp'=4,'ym'=2,'xh'=2,'exp'=2,'z'=8,'xl'=4] {'exp'}, dimensions={0}, use_global_device_ids=true | all-gather | bytes 786432 | tf_op jit(solution)/shard_map/all_gather | solution.py:238
  45.4 0.4 collective-permute-done.1
  45.8 5.6 %all_gather.7.other_rows_ref = bf16[1024,256]{1,0:T(8,128)(2,1)S(1)} all-gather(bf16[512,256]{1,0:T(8,128)(2,1)S(1)} %collective-permute-done.1), channel_id=1, replica_groups=mesh['yp'=4,'ym'=2,'xh'=2,'exp'=2,'z'=8,'xl'=4] {'exp'}, dimensions={0}, use_global_device_ids=true | all-gather | bytes 786432 | tf_op jit(solution)/shard_map/all_gather | solution.py:239
  51.4 0.0 collective-permute-done.other_ref
  51.4 0.0 copy-done
  51.4 0.9 shard_map.95
  52.3 36.7 %all_to_all.50.terms_ref = bf16[8,64,1152]{2,1,0:T(8,128)(2,1)S(1)} all-to-all(bf16[8,64,1152]{2,1,0:T(8,128)(2,1)S(1)} %bitcast.15), channel_id=1, replica_groups=mesh['yp'=4,'ym'=2,'xh'=2,'exp'=2,'z'=8,'xl'=4] {'yp','xh'}, dimensions={0} | all-to-all | bytes 2359296 | tf_op jit(solution)/shard_map/all_to_all | solution.py:203
  89.0 0.3 shard_map.96
  89.3 39.1 %all_to_all.51 = bf16[8,64,1152]{2,1,0:T(8,128)(2,1)S(1)} all-to-all(bf16[8,64,1152]{2,1,0:T(8,128)(2,1)S(1)} %shard_map.96), channel_id=1, replica_groups=mesh['yp'=4,'ym'=2,'xh'=2,'exp'=2,'z'=8,'xl'=4] {'yp','xh'}, dimensions={0} | all-to-all | bytes 2359296 | tf_op jit(solution)/shard_map/all_to_all | solution.py:203
  128.4 0.4 shard_map.100
  128.8 1.9 %collective-permute-start.2 = (bf16[2,384,256]{2,1,0:T(8,128)(2,1)S(1)}, bf16[2,384,256]{2,1,0:T(8,128)(2,1)S(1)}, u32[]{:S(2)}, u32[]{:S(2)}) collective-permute-start(bf16[2,384,256]{2,1,0:T(8,128)(2,1)S(1)} %get-tuple-element.24), channel_id=1, source_target_pairs={{0,128},{128,0},{1,129},{129,1},{2,130},{130,2},{3,131},{131,3},{4... | collective-permute-start | bytes 1179656 | tf_op jit(solution)/shard_map/ppermute | solution.py:207
  130.7 0.9 shard_map.97
  131.7 7.8 %all_to_all.52.parts_ref = bf16[2,1024,256]{2,1,0:T(8,128)(2,1)S(1)} all-to-all(bf16[2,1024,256]{2,1,0:T(8,128)(2,1)S(1)} %bitcast.13), channel_id=1, replica_groups=mesh['yp'=4,'ym'=2,'xh'=2,'exp'=2,'z'=8,'xl'=4] {'exp'}, dimensions={0} | all-to-all | bytes 2097152 | tf_op jit(solution)/shard_map/all_to_all | solution.py:203
  139.4 0.9 shard_map.98
  140.4 18.2 %all-to-all-start.4 = ((bf16[64,16,256]{2,1,0:T(8,128)(2,1)}), bf16[64,16,256]{2,1,0:T(8,128)(2,1)S(1)}, u32[]{:S(2)}, u32[]{:S(2)}) async-start(bf16[64,16,256]{2,1,0:T(8,128)(2,1)} %bitcast.9), calls=%async_computation.4 | async-start | bytes 1048576 | tf_op jit(solution)/shard_map/all_to_all | solution.py:203
  158.6 0.0 collective-permute-done.2.other_ref
  158.6 0.0 copy-start.1
  158.6 0.0 copy-start.2
  158.6 0.9 shard_map.101
  159.6 15.9 %all-to-all-done.4 = bf16[64,16,256]{2,1,0:T(8,128)(2,1)S(1)} async-done(((bf16[64,16,256]{2,1,0:T(8,128)(2,1)}), bf16[64,16,256]{2,1,0:T(8,128)(2,1)S(1)}, u32[]{:S(2)}, u32[]{:S(2)}) %all-to-all-start.4) | async-done | bytes 524320 | tf_op jit(solution)/shard_map/all_to_all | solution.py:203
  175.5 0.0 copy-done.1
  175.5 0.0 copy-done.2
  175.5 1.0 shard_map.99
Async XLA Ops:
  3.9 47.6 %copy-start = (bf16[2,256,1152]{2,1,0:T(8,128)(2,1)S(1)}, bf16[2,256,1152]{2,1,0:T(8,128)(2,1)}, u32[]{:S(2)}) copy-start(bf16[2,256,1152]{2,1,0:T(8,128)(2,1)} %get-tuple-element.15.kept_ref) | copy-start | bytes 3538948
  3.9 47.5 %collective-permute-start = (bf16[2,256,1152]{2,1,0:T(8,128)(2,1)}, bf16[2,256,1152]{2,1,0:T(8,128)(2,1)S(1)}, u32[]{:S(2)}, u32[]{:S(2)}) collective-permute-start(bf16[2,256,1152]{2,1,0:T(8,128)(2,1)} %get-tuple-element.16), channel_id=1, source_target_pairs={{0,128},{128,0},{1,129},{129,1},{2,130},{130,2},{3,131},{131,3},{4... | collective-permute-start | bytes 3538952 | tf_op jit(solution)/shard_map/ppermute | solution.py:207
  38.7 7.1 %collective-permute-start.1 = (bf16[512,256]{1,0:T(8,128)(2,1)S(1)}, bf16[512,256]{1,0:T(8,128)(2,1)S(1)}, u32[]{:S(2)}, u32[]{:S(2)}) collective-permute-start(bf16[512,256]{1,0:T(8,128)(2,1)S(1)} %bitcast.18), channel_id=1, source_target_pairs={{0,128},{128,0},{1,129},{129,1},{2,130},{130,2},{3,131},{131,3},{4... | collective-permute-start | bytes 786440 | tf_op jit(solution)/shard_map/ppermute | solution.py:207
  128.8 29.8 %collective-permute-start.2 = (bf16[2,384,256]{2,1,0:T(8,128)(2,1)S(1)}, bf16[2,384,256]{2,1,0:T(8,128)(2,1)S(1)}, u32[]{:S(2)}, u32[]{:S(2)}) collective-permute-start(bf16[2,384,256]{2,1,0:T(8,128)(2,1)S(1)} %get-tuple-element.24), channel_id=1, source_target_pairs={{0,128},{128,0},{1,129},{129,1},{2,130},{130,2},{3,131},{131,3},{4... | collective-permute-start | bytes 1179656 | tf_op jit(solution)/shard_map/ppermute | solution.py:207
  140.4 35.1 %all-to-all-start.4 = ((bf16[64,16,256]{2,1,0:T(8,128)(2,1)}), bf16[64,16,256]{2,1,0:T(8,128)(2,1)S(1)}, u32[]{:S(2)}, u32[]{:S(2)}) async-start(bf16[64,16,256]{2,1,0:T(8,128)(2,1)} %bitcast.9), calls=%async_computation.4 | async-start | bytes 1048576 | tf_op jit(solution)/shard_map/all_to_all | solution.py:203
  158.6 16.9 %copy-start.1 = (f32[128,2]{0,1:T(2,128)S(1)}, f32[128,2]{0,1:T(2,128)}, u32[]{:S(2)}) copy-start(f32[128,2]{0,1:T(2,128)} %param.9) | copy-start | bytes 3076
  158.6 16.9 %copy-start.2 = (s32[2,128]{1,0:T(2,128)S(1)}, s32[2,128]{1,0:T(2,128)}, u32[]{:S(2)}) copy-start(s32[2,128]{1,0:T(2,128)} %get-tuple-element.14.slot_ref) | copy-start | bytes 3076

commit v10 on v8

--- a/solution.py
+++ b/solution.py
@@ -234,9 +234,9 @@
     terms, expert_grad, other_grad = call(
         first_terms, (shape((slots, 3 * half), BF), grads, grads), kept, other, rows, other_rows
     )
-    terms = exchange(terms, ("yp", "xh")).reshape(slices, slots // slices, 3 * half)
+    terms = exchange(terms, ("xh", "yp")).reshape(slices, slots // slices, 3 * half)
     acts = call(activate, shape(terms.shape, BF), terms)
-    acts = exchange(acts.reshape(slots, 3 * half), ("yp", "xh"))
+    acts = exchange(acts.reshape(slots, 3 * half), ("xh", "yp"))
 
     parts = call(
         last_terms, shape((4, groups, local_experts * CAPACITY, depth), BF),

time: 174 us -> 174 us (level)
  no operation moved by 1% of the time
where the time goes in v10:
time: 174 us
  blocking collectives  123 us (71%)
  starting transfers between devices  28.2 us (16%)
  waiting for transfers between devices  13 us (7%)
  Pallas kernels  7.55 us (4%)
    all_to_all x4, blocking collectives, exchange(): return lax.all_to_all(rows, axis, split_axis=0, concat_axis=0, tiled=True)  113 us
    all_to_all x1, starting transfers between devices, exchange(): return lax.all_to_all(rows, axis, split_axis=0, concat_axis=0, tiled=True)  19 us
    ppermute x3, waiting for transfers between devices, swap(): return lax.ppermute(block, 'ym', [(0, 1), (1, 0)])  13 us
    ppermute x3, starting transfers between devices, swap(): return lax.ppermute(block, 'ym', [(0, 1), (1, 0)])  9.24 us
    pallas_call x7, Pallas kernels, call(): pl.pallas_call(kernel, out_shape=outs, in_specs=[SMEM] * scalars + [HBM]...  7.55 us
    all_gather x1, blocking collectives, shards(): other_rows = lax.all_gather(other_arrived, 'exp', axis=0, tiled=True)  5.59 us
    all_gather x1, blocking collectives, shards(): rows = lax.all_gather(arrived, 'exp', axis=0, tiled=True)  4.74 us
  transfers between devices with their start and end apart: 4, of which 2 were waited for; matrix products, arithmetic and copies ran while one was open for 1% of the time, Pallas kernels for 0%

profile of v10, /device:TPU:1, one launch (start us, length us, event | category | flops | bytes accessed | tf_op | source)
XLA Modules:
  0.0 173.7 jit_solution(8810585844241728191)
XLA Ops:
  0.6 3.2 %shard_map.94 = (bf16[512,256]{1,0:T(8,128)(2,1)}, s32[2,128]{1,0:T(2,128)}, bf16[2,256,1152]{2,1,0:T(8,128)(2,1)}, bf16[2,256,1152]{2,1,0:T(8,128)(2,1)}) custom-call(s32[1]{0:T(128)} %bitcast.core_ref, s32[1]{0:T(128)} %bitcast.1.member_ref, s32[2,128]{1,0:T(2,128)} %bitcast.21, f32[2,128]{1,0:T(2,128)} %bitcast.16, bf16[128,256]{1,0:T(8,128)(2,1)} %tokens_hbm.1, ...), custom_call_target="tpu_custom_call" | custom-call | tf_op jit(solution)/shard_map/pallas_call | solution.py:24
  3.9 0.0 copy-start
  3.9 4.3 %collective-permute-start = (bf16[2,256,1152]{2,1,0:T(8,128)(2,1)}, bf16[2,256,1152]{2,1,0:T(8,128)(2,1)S(1)}, u32[]{:S(2)}, u32[]{:S(2)}) collective-permute-start(bf16[2,256,1152]{2,1,0:T(8,128)(2,1)} %get-tuple-element.16), channel_id=1, source_target_pairs={{0,128},{128,0},{1,129},{129,1},{2,130},{130,2},{3,131},{131,3},{4... | collective-permute-start | bytes 3538952 | tf_op jit(solution)/shard_map/ppermute | solution.py:199
  8.2 30.6 %all_to_all.49 = bf16[32,16,256]{2,1,0:T(8,128)(2,1)S(1)} all-to-all(bf16[32,16,256]{2,1,0:T(8,128)(2,1)} %bitcast.20), channel_id=1, replica_groups=mesh['yp'=4,'ym'=2,'xh'=2,'exp'=2,'z'=8,'xl'=4] {'z','xl'}, dimensions={0} | all-to-all | bytes 524288 | tf_op jit(solution)/shard_map/all_to_all | solution.py:195
  38.7 1.9 %collective-permute-start.1 = (bf16[512,256]{1,0:T(8,128)(2,1)S(1)}, bf16[512,256]{1,0:T(8,128)(2,1)S(1)}, u32[]{:S(2)}, u32[]{:S(2)}) collective-permute-start(bf16[512,256]{1,0:T(8,128)(2,1)S(1)} %bitcast.18), channel_id=1, source_target_pairs={{0,128},{128,0},{1,129},{129,1},{2,130},{130,2},{3,131},{131,3},{4... | collective-permute-start | bytes 786440 | tf_op jit(solution)/shard_map/ppermute | solution.py:199
  40.7 4.7 %all_gather.6.rows_ref = bf16[1024,256]{1,0:T(8,128)(2,1)S(1)} all-gather(bf16[512,256]{1,0:T(8,128)(2,1)S(1)} %bitcast.19), channel_id=1, replica_groups=mesh['yp'=4,'ym'=2,'xh'=2,'exp'=2,'z'=8,'xl'=4] {'exp'}, dimensions={0}, use_global_device_ids=true | all-gather | bytes 786432 | tf_op jit(solution)/shard_map/all_gather | solution.py:230
  45.4 0.4 collective-permute-done.1
  45.8 5.6 %all_gather.7.other_rows_ref = bf16[1024,256]{1,0:T(8,128)(2,1)S(1)} all-gather(bf16[512,256]{1,0:T(8,128)(2,1)S(1)} %collective-permute-done.1), channel_id=1, replica_groups=mesh['yp'=4,'ym'=2,'xh'=2,'exp'=2,'z'=8,'xl'=4] {'exp'}, dimensions={0}, use_global_device_ids=true | all-gather | bytes 786432 | tf_op jit(solution)/shard_map/all_gather | solution.py:231
  51.4 0.0 collective-permute-done.other_ref
  51.4 0.0 copy-done
  51.4 0.8 shard_map.95
  52.3 37.5 %all_to_all.50.terms_ref = bf16[8,64,1152]{2,1,0:T(8,128)(2,1)S(1)} all-to-all(bf16[8,64,1152]{2,1,0:T(8,128)(2,1)S(1)} %bitcast.15), channel_id=1, replica_groups=mesh['yp'=4,'ym'=2,'xh'=2,'exp'=2,'z'=8,'xl'=4] {'xh','yp'}, dimensions={0} | all-to-all | bytes 2359296 | tf_op jit(solution)/shard_map/all_to_all | solution.py:195
  89.8 0.3 shard_map.96
  90.0 38.0 %all_to_all.51 = bf16[8,64,1152]{2,1,0:T(8,128)(2,1)S(1)} all-to-all(bf16[8,64,1152]{2,1,0:T(8,128)(2,1)S(1)} %shard_map.96), channel_id=1, replica_groups=mesh['yp'=4,'ym'=2,'xh'=2,'exp'=2,'z'=8,'xl'=4] {'xh','yp'}, dimensions={0} | all-to-all | bytes 2359296 | tf_op jit(solution)/shard_map/all_to_all | solution.py:195
  128.1 0.9 shard_map.97
  129.0 6.7 %all_to_all.52.parts_ref = bf16[2,1024,256]{2,1,0:T(8,128)(2,1)S(1)} all-to-all(bf16[2,1024,256]{2,1,0:T(8,128)(2,1)S(1)} %bitcast.13), channel_id=1, replica_groups=mesh['yp'=4,'ym'=2,'xh'=2,'exp'=2,'z'=8,'xl'=4] {'exp'}, dimensions={0} | all-to-all | bytes 2097152 | tf_op jit(solution)/shard_map/all_to_all | solution.py:195
  135.7 0.9 shard_map.98
  136.6 19.0 %all-to-all-start.4 = ((bf16[64,16,256]{2,1,0:T(8,128)(2,1)}), bf16[64,16,256]{2,1,0:T(8,128)(2,1)S(1)}, u32[]{:S(2)}, u32[]{:S(2)}) async-start(bf16[64,16,256]{2,1,0:T(8,128)(2,1)} %bitcast.9), calls=%async_computation.4 | async-start | bytes 1048576 | tf_op jit(solution)/shard_map/all_to_all | solution.py:195
  155.6 0.4 shard_map.100
  156.0 3.0 %collective-permute-start.2 = (bf16[2,384,256]{2,1,0:T(8,128)(2,1)S(1)}, bf16[2,384,256]{2,1,0:T(8,128)(2,1)S(1)}, u32[]{:S(2)}, u32[]{:S(2)}) collective-permute-start(bf16[2,384,256]{2,1,0:T(8,128)(2,1)S(1)} %get-tuple-element.24), channel_id=1, source_target_pairs={{0,128},{128,0},{1,129},{129,1},{2,130},{130,2},{3,131},{131,3},{4... | collective-permute-start | bytes 1179656 | tf_op jit(solution)/shard_map/ppermute | solution.py:199
  159.1 12.6 %collective-permute-done.2 = bf16[2,384,256]{2,1,0:T(8,128)(2,1)S(1)} collective-permute-done((bf16[2,384,256]{2,1,0:T(8,128)(2,1)S(1)}, bf16[2,384,256]{2,1,0:T(8,128)(2,1)S(1)}, u32[]{:S(2)}, u32[]{:S(2)}) %collective-permute-start.2) | collective-permute-done | bytes 393248 | tf_op jit(solution)/shard_map/ppermute | solution.py:199
  171.7 0.1 broadcast_select_fusion.1
  171.7 0.0 copy-start.1
  171.7 0.0 copy-start.2
  171.7 0.9 pad_maximum_fusion
  172.7 0.0 all-to-all-done.4
  172.7 0.0 copy-done.1
  172.7 0.0 copy-done.2
  172.7 1.0 shard_map.99
Async XLA Ops:
  3.9 47.6 %copy-start = (bf16[2,256,1152]{2,1,0:T(8,128)(2,1)S(1)}, bf16[2,256,1152]{2,1,0:T(8,128)(2,1)}, u32[]{:S(2)}) copy-start(bf16[2,256,1152]{2,1,0:T(8,128)(2,1)} %get-tuple-element.15.kept_ref) | copy-start | bytes 3538948
  3.9 47.5 %collective-permute-start = (bf16[2,256,1152]{2,1,0:T(8,128)(2,1)}, bf16[2,256,1152]{2,1,0:T(8,128)(2,1)S(1)}, u32[]{:S(2)}, u32[]{:S(2)}) collective-permute-start(bf16[2,256,1152]{2,1,0:T(8,128)(2,1)} %get-tuple-element.16), channel_id=1, source_target_pairs={{0,128},{128,0},{1,129},{129,1},{2,130},{130,2},{3,131},{131,3},{4... | collective-permute-start | bytes 3538952 | tf_op jit(solution)/shard_map/ppermute | solution.py:199
  38.7 7.1 %collective-permute-start.1 = (bf16[512,256]{1,0:T(8,128)(2,1)S(1)}, bf16[512,256]{1,0:T(8,128)(2,1)S(1)}, u32[]{:S(2)}, u32[]{:S(2)}) collective-permute-start(bf16[512,256]{1,0:T(8,128)(2,1)S(1)} %bitcast.18), channel_id=1, source_target_pairs={{0,128},{128,0},{1,129},{129,1},{2,130},{130,2},{3,131},{131,3},{4... | collective-permute-start | bytes 786440 | tf_op jit(solution)/shard_map/ppermute | solution.py:199
  136.6 36.1 %all-to-all-start.4 = ((bf16[64,16,256]{2,1,0:T(8,128)(2,1)}), bf16[64,16,256]{2,1,0:T(8,128)(2,1)S(1)}, u32[]{:S(2)}, u32[]{:S(2)}) async-start(bf16[64,16,256]{2,1,0:T(8,128)(2,1)} %bitcast.9), calls=%async_computation.4 | async-start | bytes 1048576 | tf_op jit(solution)/shard_map/all_to_all | solution.py:195
  156.0 15.6 %collective-permute-start.2 = (bf16[2,384,256]{2,1,0:T(8,128)(2,1)S(1)}, bf16[2,384,256]{2,1,0:T(8,128)(2,1)S(1)}, u32[]{:S(2)}, u32[]{:S(2)}) collective-permute-start(bf16[2,384,256]{2,1,0:T(8,128)(2,1)S(1)} %get-tuple-element.24), channel_id=1, source_target_pairs={{0,128},{128,0},{1,129},{129,1},{2,130},{130,2},{3,131},{131,3},{4... | collective-permute-start | bytes 1179656 | tf_op jit(solution)/shard_map/ppermute | solution.py:199
  171.7 1.0 copy-start.1
  171.7 1.0 copy-start.2
